TPU v7x, 256 devices: a whole 4x4x8 slice. The times are simulated.
256 devices in a mesh: dp: 128 (over x, y, z), shard: 2 (over core).
Axes of the slice: x: 4, y: 4, z: 8, core: 2. Of those that a mesh axis runs over, the one named last changes fastest.
Arguments:
- params: float32 [160272], replicated, may hold values from -5 to 5
- first_moment: float32 [160272], replicated, may hold values from -10 to 10
- second_moment: float32 [160272], replicated, may hold values from 0.05 to 0.5
- positions: float32 [2048, 3, 128], P(('dp', 'shard')), may hold values from 0 to 4
- species: int32 [2048, 128], P(('dp', 'shard')), may hold values from 0 to 9
- neighbours: int32 [2048, 16, 128], P(('dp', 'shard')), may hold values from -1 to 127, as said below
- window_of: int32 [2048], P(('dp', 'shard')), may hold values from 0 to 31
- frame_count: int32 [256], P(('dp', 'shard')), may hold values from 1 to 8, 768 in all
Outputs:
- new_params: float32 [160272], replicated
- new_first: float32 [160272], replicated
- new_second: float32 [160272], replicated
- window_means: float32 [32], replicated
Inputs may be any that keep to these rules, and one draw needn't show every extreme that they name: `neighbours`: -1 marks an empty slot; no atom lists itself; the last slot of every atom is empty. Slots 0 to frame_count - 1 of a device hold its frames.
All inputs are finite; a program needn't handle non-finite values.
Results may differ from a plain program's by a relative error of at most 0.0003.
Values sent between devices are 32-bit elements; how exact they have to be, the bound alone decides.
No kernel may reach another device: no remote copies, remote signals or barrier semaphores. Data moves between devices by JAX's collectives and lax.ppermute only.
A program may use at most 128 MiB of HBM per device.

v0:
```python
import math

import jax
import jax.numpy as jnp
from jax import lax
from jax.sharding import PartitionSpec as P

C = 128
HID = 64
NB = 8
SPECIES = 10
RO = 16
LAYERS = 2
WINDOWS = 32
SOLUTE = 16
NPAR = 160272


RADIUS_CUT = 8.0
SOFTENING = 0.01
GRAD_SCALE = 4.0


def mult(left, right):
    return jnp.dot(left, right, precision=lax.Precision.HIGHEST, preferred_element_type=jnp.float32)


def take_block(theta, offset, rows, cols, fan_in):
    block = theta[offset : offset + rows * cols].reshape(rows, cols) * fan_in ** (-0.5)
    return (block, offset + rows * cols)


def frame_energy(theta, coords, species_row, neighbour_rows, coupling):
    atoms_n = coords.shape[1]
    slots_n = neighbour_rows.shape[0]
    offset = 0
    embed, offset = take_block(theta, offset, C, SPECIES, 1.0)
    onehot = (species_row[None, :] == jnp.arange(SPECIES, dtype=jnp.int32)[:, None]).astype(
        jnp.float32
    )
    features = mult(embed, onehot)
    partner = jnp.maximum(neighbour_rows, 0).reshape(-1)
    present = (neighbour_rows >= 0).reshape(-1)
    others = jnp.take(coords, partner, axis=1)
    own_pos = jnp.tile(coords, (1, slots_n))
    delta = others - own_pos
    radius = jnp.sqrt(jnp.sum(delta * delta, axis=0) + SOFTENING)
    atom_ids = jnp.tile(jnp.arange(atoms_n, dtype=jnp.int32), slots_n)
    crossing = (atom_ids < SOLUTE) != (partner < SOLUTE)
    envelope = (1.0 - (radius / RADIUS_CUT) ** 2) ** 2
    factor = jnp.where(present, envelope, 0.0) * jnp.where(crossing, coupling, 1.0)
    orders = jnp.arange(1, NB + 1).astype(jnp.float32)
    basis = (
        jnp.sqrt(2.0 / RADIUS_CUT)
        * jnp.sin(orders[:, None] * jnp.pi * radius[None, :] / RADIUS_CUT)
        / radius[None, :]
    )
    energy = jnp.zeros((), jnp.float32)
    for layer_id in range(LAYERS):
        w_one, offset = take_block(theta, offset, HID, NB, NB)
        w_two, offset = take_block(theta, offset, HID, HID, HID)
        w_three, offset = take_block(theta, offset, C, HID, HID)
        w_up, offset = take_block(theta, offset, C, C, C)
        w_lin, offset = take_block(theta, offset, C, C, C)
        w_sq, offset = take_block(theta, offset, C, C, C)
        w_skip, offset = take_block(theta, offset, C, C, C)
        w_read, offset = take_block(theta, offset, C, 1, C)
        radial = mult(w_three, jax.nn.silu(mult(w_two, jax.nn.silu(mult(w_one, basis)))))
        lifted = mult(w_up, features)
        carried = jnp.take(lifted, partner, axis=1)
        message = radial * carried * factor[None, :]
        pooled = message.reshape(C, slots_n, atoms_n).sum(axis=1) / slots_n
        features = mult(w_lin, pooled) + mult(w_sq, pooled * pooled) + mult(w_skip, features)
        energy = energy + jnp.sum(w_read * features)
    w_head, offset = take_block(theta, offset, RO, C, C)
    w_out, offset = take_block(theta, offset, RO, 1, RO)
    energy = energy + jnp.sum(w_out * jax.nn.silu(mult(w_head, features)))
    return energy


def frame_pair(theta, coords, species_row, neighbour_rows, coupling):

    def energy_of(value):
        return frame_energy(theta, coords, species_row, neighbour_rows, value)

    return jax.jvp(energy_of, (coupling,), (jnp.ones_like(coupling),))


def trapezoid():
    index = jnp.arange(WINDOWS, dtype=jnp.int32)
    edges = (index == 0) | (index == WINDOWS - 1)
    return jnp.where(edges, 0.5, 1.0).astype(jnp.float32) / (WINDOWS - 1)


def adam_step(params, first_moment, second_moment, unit):
    new_first = 0.9 * first_moment + 0.1 * unit
    new_second = 0.999 * second_moment + 0.001 * unit * unit
    unbiased_first = new_first / (1.0 - 0.9**10)
    unbiased_second = new_second / (1.0 - 0.999**10)
    new_params = params - 0.01 * unbiased_first / (jnp.sqrt(unbiased_second) + 1e-08)
    return (new_params, new_first, new_second)


def tally(window_ids, count):
    slot_ids = jnp.arange(window_ids.shape[0], dtype=jnp.int32)
    live = (slot_ids < count).astype(jnp.float32)
    onehot = (window_ids[:, None] == jnp.arange(WINDOWS, dtype=jnp.int32)[None, :]).astype(
        jnp.float32
    )
    return onehot * live[:, None]


def on_device(
    params, first_moment, second_moment, positions, species, neighbours, window_of, frame_count
):
    count = frame_count[0]
    onehot = tally(window_of, count)
    couplings = window_of.astype(jnp.float32) / (WINDOWS - 1)

    def forward(slot_id, deriv):
        value = frame_pair(
            params, positions[slot_id], species[slot_id], neighbours[slot_id], couplings[slot_id]
        )[1]
        return deriv.at[slot_id].set(value)

    deriv = lax.fori_loop(0, count, forward, jnp.zeros((positions.shape[0],), jnp.float32))
    local_sums = jnp.sum(onehot * deriv[:, None], axis=0)
    sizes, sums = lax.psum((jnp.sum(onehot, axis=0), local_sums), ("dp", "shard"))
    means = sums / jnp.maximum(sizes, 1.0)
    share = jnp.sum(onehot * (trapezoid() / jnp.maximum(sizes, 1.0))[None, :], axis=1)
    centre = jnp.sum(onehot * means[None, :], axis=1)
    cot_energy = -share * (deriv - centre)

    def backward(slot_id, total):

        def pair_of(th):
            return frame_pair(
                th, positions[slot_id], species[slot_id], neighbours[slot_id], couplings[slot_id]
            )

        _, pull = jax.vjp(pair_of, params)
        return total + pull((cot_energy[slot_id], share[slot_id]))[0]

    grad = lax.fori_loop(0, count, backward, jnp.zeros((NPAR,), jnp.float32))
    summed = lax.psum(grad, ("dp", "shard"))
    norm = jnp.sqrt(jnp.sum(summed * summed))
    unit = summed * (GRAD_SCALE * math.sqrt(NPAR) / (norm + 1e-06))
    new_params, new_first, new_second = adam_step(params, first_moment, second_moment, unit)
    return (new_params, new_first, new_second, means)


def solution(mesh):
    in_specs = (
        P(),
        P(),
        P(),
        P(("dp", "shard"), None, None),
        P(("dp", "shard"), None),
        P(("dp", "shard"), None, None),
        P(("dp", "shard")),
        P(("dp", "shard")),
    )
    out_specs = (P(), P(), P(), P())
    return jax.shard_map(
        on_device, mesh=mesh, in_specs=in_specs, out_specs=out_specs, check_vma=False
    )
```

profile of v0, /device:TPU:1, one launch (start us, length us, event | category | flops | bytes accessed | tf_op | source)
XLA Modules:
  0.0 2048.2 jit_solution(13583995908080014207)
XLA Ops:
  9.6 210.1 %while.21 = (s32[]{:T(128)}, f32[8]{0:T(128)S(1)}, s32[]{:T(128)}, f32[160272]{0:T(1024)}, f32[8,3,128]{1,2,0:T(8,128)}, /*index=5*/s32[8,16,128]{2,1,0:T(8,128)...) while((s32[]{:T(128)}, f32[8]{0:T(128)S(1)}, s32[]{:T(128)}, ...), condition=%wide.region_12.14_spmd, body=%wide.region_3.13_spmd.sunk | while | flops 996904704 | bytes 43914556 | solution.py:126
  40.5 7.6 gather_fusion.3
  92.9 7.6 gather_fusion.3
  145.2 7.6 gather_fusion.3
  197.6 7.6 gather_fusion.3
  219.9 288.8 %all-reduce.19 = (f32[32]{0:T(128)S(1)}, f32[32]{0:T(128)S(1)}) all-reduce(f32[32]{0:T(128)S(1)} %get-tuple-element.173, f32[32]{0:T(128)S(1)} %get-tuple-element.174), channel_id=1, replica_groups=mesh['dp'=128,'shard'=2] {'dp','shard'}, use_global_device_ids=true, to_apply=%region_14.16 | all-reduce | flops 64 | bytes 512 | tf_op jit(solution)/shard_map/psum | solution.py:128
  510.3 639.8 %while.22 = (s32[]{:T(128)}, f32[160272]{0:T(1024)}, s32[]{:T(128)}, f32[8]{0:T(128)S(1)}, f32[160272]{0:T(1024)S(1)}, /*index=5*/f32[8,3,128]{1,2,0:T(8,128)}, ...) while((s32[]{:T(128)}, f32[160272]{0:T(1024)}, ...), condition=%wide.region_31.33_spmd, body=%wide.region_16.32_spmd.sunk | while | flops 2971525120 | bytes 168802928 | solution.py:144
  550.9 7.9 gather_fusion.6
  589.9 12.2 scatter_custom_fusion.16
  605.5 12.4 scatter_custom_fusion.15
  653.5 12.1 scatter_custom_fusion.17
  710.5 7.7 gather_fusion.6
  749.2 12.1 scatter_custom_fusion.16
  764.8 12.4 scatter_custom_fusion.15
  812.7 12.0 scatter_custom_fusion.17
  869.4 7.7 gather_fusion.6
  908.2 12.1 scatter_custom_fusion.16
  923.8 12.5 scatter_custom_fusion.15
  971.9 12.0 scatter_custom_fusion.17
  1028.6 7.9 gather_fusion.6
  1067.6 12.1 scatter_custom_fusion.16
  1083.1 12.3 scatter_custom_fusion.15
  1131.0 12.0 scatter_custom_fusion.17
  1150.2 885.3 %all-reduce.22.cloned.1.call-done = f32[160272]{0:T(1024)} async-done(((f32[160272]{0:T(1024)}), f32[160272]{0:T(1024)}) %all-reduce.22.cloned.1.call-update) | async-done | bytes 641104 | tf_op jit(solution)/shard_map/psum | solution.py:145
  (1303 shorter events, 616.1 us)
Async XLA Ops:
  7.2 2028.3 %all-reduce.22.cloned.1.call-start = ((), (), s32[]{:S(2)}) async-start(), calls=%async_computation | async-start | bytes 1286144 | tf_op jit(solution)/shard_map/psum | solution.py:145
  219.8 290.5 %copy-start.1 = (f32[160272]{0:T(1024)S(1)}, f32[160272]{0:T(1024)}, u32[]{:S(2)}) copy-start(f32[160272]{0:T(1024)} %get-tuple-element.623) | copy-start | bytes 1923268
  511.2 28.6 %copy-start.59 = (f32[8]{0:T(128)}, f32[8]{0:T(128)S(1)}, u32[]{:S(2)}) copy-start(f32[8]{0:T(128)S(1)} %get-tuple-element.609) | copy-start | bytes 100 | tf_op jit(solution)/shard_map/while
  511.2 37.4 %copy-start.61 = (f32[8]{0:T(128)}, f32[8]{0:T(128)S(1)}, u32[]{:S(2)}) copy-start(f32[8]{0:T(128)S(1)} %get-tuple-element.615) | copy-start | bytes 100 | tf_op jit(solution)/shard_map/while
  511.9 55.1 %copy-start.41 = (pred[2048]{0:T(1024)(128)(4,1)}, pred[2048]{0:T(1024)(128)(4,1)S(1)}, u32[]{:S(2)}) copy-start(pred[2048]{0:T(1024)(128)(4,1)S(1)} %get-tuple-element.508) | copy-start | bytes 6148 | tf_op jit(solution)/shard_map/while
  522.1 38.4 %copy-start.31 = (f32[2048]{0:T(1024)}, f32[2048]{0:T(1024)S(1)}, u32[]{:S(2)}) copy-start(f32[2048]{0:T(1024)S(1)} %get-tuple-element.502) | copy-start | bytes 24580 | tf_op jit(solution)/shard_map/while
  522.3 38.3 %copy-start.48 = (f32[8]{0:T(128)}, f32[8]{0:T(128)S(1)}, u32[]{:S(2)}) copy-start(f32[8]{0:T(128)S(1)} %convert_multiply_fusion.6) | copy-start | bytes 100 | tf_op jit(solution)/shard_map/while
  653.4 14.5 copy-start.11
  670.7 28.6 %copy-start.59 = (f32[8]{0:T(128)}, f32[8]{0:T(128)S(1)}, u32[]{:S(2)}) copy-start(f32[8]{0:T(128)S(1)} %get-tuple-element.609) | copy-start | bytes 100 | tf_op jit(solution)/shard_map/while
  670.7 37.4 %copy-start.61 = (f32[8]{0:T(128)}, f32[8]{0:T(128)S(1)}, u32[]{:S(2)}) copy-start(f32[8]{0:T(128)S(1)} %get-tuple-element.615) | copy-start | bytes 100 | tf_op jit(solution)/shard_map/while
  671.4 54.9 %copy-start.41 = (pred[2048]{0:T(1024)(128)(4,1)}, pred[2048]{0:T(1024)(128)(4,1)S(1)}, u32[]{:S(2)}) copy-start(pred[2048]{0:T(1024)(128)(4,1)S(1)} %get-tuple-element.508) | copy-start | bytes 6148 | tf_op jit(solution)/shard_map/while
  681.6 38.2 %copy-start.31 = (f32[2048]{0:T(1024)}, f32[2048]{0:T(1024)S(1)}, u32[]{:S(2)}) copy-start(f32[2048]{0:T(1024)S(1)} %get-tuple-element.502) | copy-start | bytes 24580 | tf_op jit(solution)/shard_map/while
  681.8 38.1 %copy-start.48 = (f32[8]{0:T(128)}, f32[8]{0:T(128)S(1)}, u32[]{:S(2)}) copy-start(f32[8]{0:T(128)S(1)} %convert_multiply_fusion.6) | copy-start | bytes 100 | tf_op jit(solution)/shard_map/while
  829.6 28.6 %copy-start.59 = (f32[8]{0:T(128)}, f32[8]{0:T(128)S(1)}, u32[]{:S(2)}) copy-start(f32[8]{0:T(128)S(1)} %get-tuple-element.609) | copy-start | bytes 100 | tf_op jit(solution)/shard_map/while
  829.7 37.4 %copy-start.61 = (f32[8]{0:T(128)}, f32[8]{0:T(128)S(1)}, u32[]{:S(2)}) copy-start(f32[8]{0:T(128)S(1)} %get-tuple-element.615) | copy-start | bytes 100 | tf_op jit(solution)/shard_map/while
  830.4 54.9 %copy-start.41 = (pred[2048]{0:T(1024)(128)(4,1)}, pred[2048]{0:T(1024)(128)(4,1)S(1)}, u32[]{:S(2)}) copy-start(pred[2048]{0:T(1024)(128)(4,1)S(1)} %get-tuple-element.508) | copy-start | bytes 6148 | tf_op jit(solution)/shard_map/while
  840.6 38.2 %copy-start.31 = (f32[2048]{0:T(1024)}, f32[2048]{0:T(1024)S(1)}, u32[]{:S(2)}) copy-start(f32[2048]{0:T(1024)S(1)} %get-tuple-element.502) | copy-start | bytes 24580 | tf_op jit(solution)/shard_map/while
  840.7 38.1 %copy-start.48 = (f32[8]{0:T(128)}, f32[8]{0:T(128)S(1)}, u32[]{:S(2)}) copy-start(f32[8]{0:T(128)S(1)} %convert_multiply_fusion.6) | copy-start | bytes 100 | tf_op jit(solution)/shard_map/while
  988.8 28.6 %copy-start.59 = (f32[8]{0:T(128)}, f32[8]{0:T(128)S(1)}, u32[]{:S(2)}) copy-start(f32[8]{0:T(128)S(1)} %get-tuple-element.609) | copy-start | bytes 100 | tf_op jit(solution)/shard_map/while
  988.8 37.4 %copy-start.61 = (f32[8]{0:T(128)}, f32[8]{0:T(128)S(1)}, u32[]{:S(2)}) copy-start(f32[8]{0:T(128)S(1)} %get-tuple-element.615) | copy-start | bytes 100 | tf_op jit(solution)/shard_map/while
  989.6 55.1 %copy-start.41 = (pred[2048]{0:T(1024)(128)(4,1)}, pred[2048]{0:T(1024)(128)(4,1)S(1)}, u32[]{:S(2)}) copy-start(pred[2048]{0:T(1024)(128)(4,1)S(1)} %get-tuple-element.508) | copy-start | bytes 6148 | tf_op jit(solution)/shard_map/while
  999.8 38.4 %copy-start.31 = (f32[2048]{0:T(1024)}, f32[2048]{0:T(1024)S(1)}, u32[]{:S(2)}) copy-start(f32[2048]{0:T(1024)S(1)} %get-tuple-element.502) | copy-start | bytes 24580 | tf_op jit(solution)/shard_map/while
  999.9 38.3 %copy-start.48 = (f32[8]{0:T(128)}, f32[8]{0:T(128)S(1)}, u32[]{:S(2)}) copy-start(f32[8]{0:T(128)S(1)} %convert_multiply_fusion.6) | copy-start | bytes 100 | tf_op jit(solution)/shard_map/while
  1150.1 888.0 %copy-start.40 = (f32[160272]{0:T(1024)S(1)}, f32[160272]{0:T(1024)}, u32[]{:S(2)}) copy-start(f32[160272]{0:T(1024)} %param.17) | copy-start | bytes 1923268
  (230 other events, 490.1 us)
Sparse Core Ops, SparseCore 0:
  1150.3 885.1 all-reduce.21
where the time goes:
time: 2070 us; the launch traced here: 2050 us
  waiting for transfers between devices  885 us (43%)
  local copies, waits for them, and re-layouts  344 us (17%)
  blocking collectives  289 us (14%)
  matrix products  249 us (12%)
  other arithmetic  231 us (11%)
  loops' own time  34.2 us (2%)
    psum x1, waiting for transfers between devices, on_device(): summed = lax.psum(grad, ('dp', 'shard'))  885 us
    psum x1, blocking collectives, on_device(): lax.psum((jnp.sum(onehot, axis=0), local_sums), ('dp', 'shard'))  289 us
    dot_general x356, matrix products, mult(): jnp.dot(left, right, precision=lax.Precision.HIGHEST, preferred_element_t...  249 us
    gather x48, local copies, waits for them, and re-layouts, frame_energy(): carried = jnp.take(lifted, partner, axis=1)  180 us
    scatter-add x12, other arithmetic, frame_energy(): carried = jnp.take(lifted, partner, axis=1)  146 us
    while x540, local copies, waits for them, and re-layouts  48.3 us
    gather x8, local copies, waits for them, and re-layouts, frame_energy(): others = jnp.take(coords, partner, axis=1)  43.7 us
  transfers between devices with their start and end apart: 1, of which 1 were waited for; matrix products, arithmetic and copies ran while one was open for 0% of the time, Pallas kernels for 0%

commit v1 on v0

v1 whole, which is shorter than its diff:
```python
import math

import jax
import jax.numpy as jnp
from jax import lax
from jax.experimental import pallas as pl
from jax.experimental.pallas import tpu as pltpu
from jax.sharding import Mesh
from jax.sharding import PartitionSpec as P

C = 128
HID = 64
NB = 8
SPECIES = 10
RO = 16
LAYERS = 2
WINDOWS = 32
ATOMS = 128
SOLUTE = 16
K = 16
SLOTS = K - 1
EDGES = SLOTS * ATOMS
NPAR = 160272
ROWS = 1280

RADIUS_CUT = 8.0
SOFTENING = 0.01
GRAD_SCALE = 4.0

ROW_EMBED = 0
ROW_LAYER = 10
LAYER_ROWS = 613
OFF_W1, OFF_W2, OFF_W3, OFF_UP, OFF_LIN, OFF_SQ, OFF_SKIP, OFF_READ = 0, 4, 36, 100, 228, 356, 484, 612
ROW_HEAD = ROW_LAYER + LAYERS * LAYER_ROWS
ROW_OUT = ROW_HEAD + RO
USED_ROWS = ROW_OUT + 1

CHUNKS = ((0, 4), (4, 8), (8, 12), (12, 15))
F32, BF16 = jnp.float32, jnp.bfloat16

N_H0, N_P0, N_CH1, N_CL0, N_CP0, N_H1, N_P1, N_CH2, N_CL1, N_CP1, N_H2, N_CH0 = range(12)
N_NODES = 12


def halves(x):
    hi = x.astype(BF16)
    return hi, (x - hi.astype(F32)).astype(BF16)


def stack_left(w):
    hi, lo = halves(w)
    return jnp.concatenate([hi, hi, lo], axis=1)


def dot(a, b):
    return jnp.dot(a, b, preferred_element_type=F32)


def dot_nt(a, b):
    return lax.dot_general(a, b, (((1,), (1,)), ((), ())), preferred_element_type=F32)


def mm(left, x):
    hi, lo = halves(x)
    return dot(left, jnp.concatenate([hi, lo, hi], axis=0))


def nt_stacked(xs, ys):
    m, n = xs.shape[0] // 2, ys.shape[0] // 2
    o = dot_nt(xs, ys)
    return o[:m, :n] + (o[:m, n:] + o[m:, :n])


def tall(x):
    return jnp.concatenate(halves(x), axis=0)


def nt(x, y):
    return nt_stacked(tall(x), tall(y))


def tile_rows(x, reps):
    return jnp.concatenate([x] * reps, axis=1)


def unflatten(rows, height, width):
    total = None
    for r, row in enumerate(rows):
        place = lax.broadcasted_iota(jnp.int32, (height, 128), 1) + 128 * r
        own = lax.broadcasted_iota(jnp.int32, (height, 128), 0)
        first = own * width
        kept = jnp.where((place >= first) & (place < first + width), jnp.broadcast_to(row, (height, 128)), 0.0)
        col = lax.broadcasted_iota(jnp.int32, (128, 16), 1)
        pos = (lax.broadcasted_iota(jnp.int32, (128, 16), 0) + 128 * r) % width
        pick = (col == pos).astype(BF16)
        a = kept.astype(BF16)
        rest = kept - a.astype(F32)
        b = rest.astype(BF16)
        c = (rest - b.astype(F32)).astype(BF16)
        piece = dot(a, pick) + (dot(b, pick) + dot(c, pick))
        total = piece if total is None else total + piece
    return total


def flatten(mat, height, width, n_rows):
    a = mat.astype(BF16)
    rest = mat - a.astype(F32)
    b = rest.astype(BF16)
    c = (rest - b.astype(F32)).astype(BF16)
    out = []
    for r in range(n_rows):
        col = lax.broadcasted_iota(jnp.int32, (16, 128), 0)
        pos = (lax.broadcasted_iota(jnp.int32, (16, 128), 1) + 128 * r) % width
        pick = (col == pos).astype(BF16)
        spread = dot(a, pick) + (dot(b, pick) + dot(c, pick))
        place = lax.broadcasted_iota(jnp.int32, (height, 128), 1) + 128 * r
        first = lax.broadcasted_iota(jnp.int32, (height, 128), 0) * width
        kept = jnp.where((place >= first) & (place < first + width), spread, 0.0)
        out.append(jnp.sum(kept, axis=0, keepdims=True))
    return out


def silu_parts(z):
    s = 0.5 * jnp.tanh(0.5 * z) + 0.5
    value = z * s
    return value, s + value * (1.0 - s)


def forward_kernel(
    count_ref, lam_ref, th_ref, pos_ref, spc_ref, nb_ref,
    deriv_ref, basis_ref, fac_ref, act_ref, slope_ref, gath_ref, node_ref, head_ref, w3t_ref, w2t_ref,
    w1_s, w2_s, w3_s, up_s, upt_s, mix_s, mixt_s, hd_s, hdt_s, emb_s, read_s, out_s, tmp_s, tmpw_s, oh_s, rad_s, dist_s,
):
    step = pl.program_id(0)

    def column(row):
        return jnp.transpose(jnp.broadcast_to(row, (128, 128)))[:, :1]

    @pl.when(step == 0)
    def _():
        emb = unflatten([th_ref[ROW_EMBED + r : ROW_EMBED + r + 1, :] for r in range(10)], C, SPECIES)
        emb_s[...] = stack_left(emb)
        for l in range(LAYERS):
            o = ROW_LAYER + l * LAYER_ROWS
            w1 = unflatten([th_ref[o + OFF_W1 + r : o + OFF_W1 + r + 1, :] for r in range(4)], HID, NB) * NB ** (-0.5)
            w1_s[l] = stack_left(w1)
            for off, rows, reach, dst, dst_t in ((OFF_W2, 32, HID, w2_s, w2t_ref), (OFF_W3, 64, HID, w3_s, w3t_ref)):
                packed = th_ref[o + off : o + off + rows, :] * reach ** (-0.5)
                tmp_s[pl.ds(0, rows, stride=2), :] = packed
                tmp_s[pl.ds(1, rows, stride=2), :] = pltpu.roll(packed, HID, 1)
                wide = tmp_s[: 2 * rows, :]
                w = wide[:, :HID]
                dst[l] = stack_left(w)
                if rows == 32:
                    wide = jnp.concatenate([wide, wide], axis=0)
                wt = jnp.transpose(wide)[:HID, : 2 * rows]
                dst_t[l] = stack_left(wt)
            mats, mats_t = [], []
            for off in (OFF_LIN, OFF_SQ, OFF_SKIP):
                w = th_ref[o + off : o + off + C, :] * C ** (-0.5)
                mats.append(w)
                mats_t.append(jnp.transpose(w))
            mix_s[l] = stack_left(jnp.concatenate(mats, axis=1))
            mixt_s[l] = stack_left(jnp.concatenate(mats_t, axis=0))
            w = th_ref[o + OFF_UP : o + OFF_UP + C, :] * C ** (-0.5)
            up_s[l] = stack_left(w)
            upt_s[l] = stack_left(jnp.transpose(w))
            read_s[l] = jnp.transpose(
                jnp.broadcast_to(th_ref[o + OFF_READ : o + OFF_READ + 1, :] * C ** (-0.5), (128, 128))
            )
        w = th_ref[ROW_HEAD : ROW_HEAD + RO, :] * C ** (-0.5)
        hd_s[...] = stack_left(w)
        wide = jnp.concatenate([w, jnp.zeros((128 - RO, 128), F32)], axis=0)
        hdt_s[...] = stack_left(jnp.transpose(wide)[:, :RO])
        out_s[...] = jnp.transpose(jnp.broadcast_to(th_ref[ROW_OUT : ROW_OUT + 1, :] * RO ** (-0.5), (128, 128)))[:RO, :]

    @pl.when(step < count_ref[0])
    def _():
        lam = lam_ref[step]
        nb = nb_ref[0]
        partner = jnp.maximum(nb, 0)
        present = nb >= 0
        r2 = jnp.full((K, ATOMS), SOFTENING, F32)
        for d in range(3):
            row = jnp.broadcast_to(pos_ref[0, d : d + 1, :], (K, ATOMS))
            delta = jnp.take_along_axis(row, partner, axis=1) - row
            r2 = r2 + delta * delta
        radius = jnp.sqrt(r2)
        ratio = radius * (1.0 / RADIUS_CUT)
        env = 1.0 - ratio * ratio
        env = jnp.where(present, env * env, 0.0) * (1.0 / K)
        atom = lax.broadcasted_iota(jnp.int32, (K, ATOMS), 1)
        crossing = (atom < SOLUTE) != (partner < SOLUTE)
        fac = jnp.where(crossing, lam * env, env)
        dfac = jnp.where(crossing, env, 0.0)
        fac_ref[0, 0] = fac
        fac_ref[0, 1] = dfac

        angle = ratio * math.pi
        s1 = jnp.sin(angle) * (math.sqrt(2.0 / RADIUS_CUT) / radius)
        twice = 2.0 * jnp.cos(angle)
        prev, cur = jnp.zeros_like(s1), s1
        for m in range(NB):
            dist_s[m * K : (m + 1) * K, :] = cur
            prev, cur = cur, twice * cur - prev
        basis = jnp.concatenate([dist_s[pl.ds(k, NB, stride=K), :] for k in range(SLOTS)], axis=1)
        bhi, blo = basis.astype(BF16).astype(F32), None
        blo = basis - bhi
        wide = jnp.concatenate([bhi, blo], axis=0).astype(BF16)
        basis_ref[0] = wide
        w1_rhs = jnp.concatenate([bhi, jnp.zeros_like(bhi), blo, jnp.zeros_like(bhi), bhi, jnp.zeros_like(bhi)], axis=0).astype(BF16)

        sub = lax.broadcasted_iota(jnp.int32, (ATOMS, ATOMS), 0)
        for k in range(SLOTS):
            hit = jnp.broadcast_to(partner[k : k + 1, :], (ATOMS, ATOMS)) == sub
            oh_s[:, k * ATOMS : (k + 1) * ATOMS] = jnp.where(hit, 1.0, 0.0).astype(BF16)

        for l in range(LAYERS):
            for k0, k1 in CHUNKS:
                e = slice(k0 * ATOMS, k1 * ATOMS)
                z1 = dot(w1_s[l], w1_rhs[:, e])
                v1, d1 = silu_parts(z1)
                h1, l1 = halves(v1)
                act_ref[0, l, 0, :HID, e] = h1
                act_ref[0, l, 0, HID:, e] = l1
                slope_ref[0, l, 0, :, e] = d1
                z2 = dot(w2_s[l], jnp.concatenate([h1, l1, h1], axis=0))
                v2, d2 = silu_parts(z2)
                h2, l2 = halves(v2)
                act_ref[0, l, 1, :HID, e] = h2
                act_ref[0, l, 1, HID:, e] = l2
                slope_ref[0, l, 1, :, e] = d2
                rad_s[l, :, e] = dot(w3_s[l], jnp.concatenate([h2, l2, h2], axis=0))

        rows16 = lax.broadcasted_iota(jnp.int32, (16, ATOMS), 0)
        spc = jnp.where(rows16 == jnp.broadcast_to(spc_ref[0], (16, ATOMS)), 1.0, 0.0)
        feat = mm(emb_s[...], spc)
        zero = jnp.zeros((C, ATOMS), F32)
        feat = jnp.concatenate([feat, zero], axis=1)
        deriv = jnp.zeros((), F32)
        pools = []
        for l in range(LAYERS):
            node_ref[0, (N_H0, N_H1)[l]] = feat
            if l == 0:
                lift = mm(up_s[l], feat[:, :ATOMS])
                lhs = jnp.concatenate(halves(lift), axis=1)
            else:
                lift = mm(up_s[l], feat)
                lhs = jnp.concatenate(
                    [jnp.concatenate(halves(lift[:, :ATOMS]), axis=1), jnp.concatenate(halves(lift[:, ATOMS:]), axis=1)],
                    axis=0,
                )
            pool, dpool = zero, zero
            for k0, k1 in CHUNKS:
                e = slice(k0 * ATOMS, k1 * ATOMS)
                oh = oh_s[:, e]
                g = dot(lhs, jnp.concatenate([oh, oh], axis=0))
                if l == 0:
                    gath_ref[0, 0, :, e] = g
                else:
                    gath_ref[0, 1, :, e] = g[:C]
                    gath_ref[0, 2, :, e] = g[C:]
                for k in range(k0, k1):
                    t = slice((k - k0) * ATOMS, (k - k0 + 1) * ATOMS)
                    rad = rad_s[l, :, k * ATOMS : (k + 1) * ATOMS]
                    rg = rad * g[:C, t]
                    pool = pool + fac[k : k + 1, :] * rg
                    dpool = dpool + dfac[k : k + 1, :] * rg
                    if l == 1:
                        dpool = dpool + fac[k : k + 1, :] * (rad * g[C:, t])
            node_ref[0, (N_P0, N_P1)[l]] = jnp.concatenate([pool, dpool], axis=1)
            pools.append((pool, dpool))
            x = jnp.concatenate(
                [
                    jnp.concatenate([pool, dpool], axis=1),
                    jnp.concatenate([pool * pool, 2.0 * pool * dpool], axis=1),
                    feat,
                ],
                axis=0,
            )
            feat = mm(mix_s[l], x)
            deriv = deriv + jnp.sum(read_s[l] * feat[:, ATOMS:])
        node_ref[0, N_H2] = feat
        q = mm(hd_s[...], feat)
        q0, q1 = q[:, :ATOMS], q[:, ATOMS:]
        sg = 0.5 * jnp.tanh(0.5 * q0) + 0.5
        val = q0 * sg
        first = sg + val * (1.0 - sg)
        second = sg * (1.0 - sg) * (2.0 + q0 * (1.0 - 2.0 * sg))
        tail = first * q1
        deriv = deriv + jnp.sum(out_s[...] * tail)
        deriv_ref[0] = jnp.full((8, 128), deriv, F32)
        head_ref[0, 1] = jnp.concatenate([val, tail], axis=1)
        co_q = jnp.concatenate([out_s[...] * first, out_s[...] * second * q1], axis=1)
        head_ref[0, 0] = co_q
        co = mm(hdt_s[...], co_q) + jnp.concatenate([read_s[1], zero], axis=1)
        for l in (1, 0):
            node_ref[0, (N_CH1, N_CH2)[l]] = co
            y = mm(mixt_s[l], co)
            pool, dpool = pools[l]
            ya, yb = y[:, :ATOMS], y[:, ATOMS:]
            ap = ya[:C] + 2.0 * pool * ya[C : 2 * C]
            bp = yb[:C] + 2.0 * pool * yb[C : 2 * C] + 2.0 * dpool * ya[C : 2 * C]
            node_ref[0, (N_CP0, N_CP1)[l]] = jnp.concatenate([ap, bp], axis=1)
            acc = None
            for k0, k1 in CHUNKS:
                parts = [[], [], [], []]
                for k in range(k0, k1):
                    rad = rad_s[l, :, k * ATOMS : (k + 1) * ATOMS]
                    f, df = fac[k : k + 1, :], dfac[k : k + 1, :]
                    ah, al = halves(rad * (f * ap))
                    bh, bl = halves(rad * (f * bp + df * ap))
                    for lst, v in zip(parts, (ah, al, bh, bl)):
                        lst.append(v)
                left = jnp.concatenate([jnp.concatenate(lst, axis=1) for lst in parts], axis=0)
                piece = dot_nt(left, oh_s[:, k0 * ATOMS : k1 * ATOMS])
                acc = piece if acc is None else acc + piece
            cl = jnp.concatenate([acc[:C] + acc[C : 2 * C], acc[2 * C : 3 * C] + acc[3 * C :]], axis=1)
            node_ref[0, (N_CL0, N_CL1)[l]] = cl
            co = y[2 * C :] + mm(upt_s[l], cl)
            if l == 1:
                co = co + jnp.concatenate([read_s[0], zero], axis=1)
        node_ref[0, N_CH0] = co


def backward_kernel(
    count_ref, ce_ref, sh_ref, spc_ref, basis_ref, fac_ref, act_ref, slope_ref, gath_ref, node_ref, head_ref, w3t_ref, w2t_ref,
    grad_ref,
    mix_a, up_a, w3_a, w2_a, w1_a, read_a, head_a, out_a, emb_a, tmp_s,
):
    step = pl.program_id(0)

    @pl.when(step == 0)
    def _():
        for ref in (mix_a, up_a, w3_a, w2_a, w1_a, read_a, head_a, out_a, emb_a):
            ref[...] = jnp.zeros(ref.shape, F32)

    @pl.when(step < count_ref[0])
    def _():
        ce, sh = ce_ref[step], sh_ref[step]
        fac, dfac = fac_ref[0, 0], fac_ref[0, 1]

        def pair(x):
            a, b = x[:, :ATOMS], x[:, ATOMS:]
            return jnp.concatenate([ce * a + sh * b, sh * a], axis=1)

        weights = jnp.concatenate([jnp.full((8, ATOMS), ce, F32), jnp.full((8, ATOMS), sh, F32)], axis=1)
        co0 = node_ref[0, N_CH0]
        a0 = ce * co0[:, :ATOMS] + sh * co0[:, ATOMS:]
        rows16 = lax.broadcasted_iota(jnp.int32, (16, ATOMS), 0)
        spc = jnp.where(rows16 == jnp.broadcast_to(spc_ref[0], (16, ATOMS)), 1.0, 0.0).astype(BF16)
        o = dot_nt(tall(a0), spc)
        emb_a[...] += o[:C] + o[C:]
        head_a[...] += nt(pair(head_ref[0, 0]), node_ref[0, N_H2])
        out_a[...] += nt(weights, head_ref[0, 1])
        for l in range(LAYERS):
            feat = node_ref[0, (N_H0, N_H1)[l]]
            pp = node_ref[0, (N_P0, N_P1)[l]]
            pool, dpool = pp[:, :ATOMS], pp[:, ATOMS:]
            x = jnp.concatenate([pp, jnp.concatenate([pool * pool, 2.0 * pool * dpool], axis=1), feat], axis=0)
            mix_a[l] += nt(pair(node_ref[0, (N_CH1, N_CH2)[l]]), x)
            up_a[l] += nt(pair(node_ref[0, (N_CL0, N_CL1)[l]]), feat)
            read_a[l] += nt(weights, node_ref[0, (N_H1, N_H2)[l]])
            cp = pair(node_ref[0, (N_CP0, N_CP1)[l]])
            ap, bp = cp[:, :ATOMS], cp[:, ATOMS:]
            for k0, k1 in CHUNKS:
                e = slice(k0 * ATOMS, k1 * ATOMS)
                parts = []
                for k in range(k0, k1):
                    t = slice(k * ATOMS, (k + 1) * ATOMS)
                    f, df = fac[k : k + 1, :], dfac[k : k + 1, :]
                    u = f * ap + df * bp
                    if l == 0:
                        parts.append(gath_ref[0, 0, :, t] * u)
                    else:
                        parts.append(gath_ref[0, 1, :, t] * u + gath_ref[0, 2, :, t] * (f * bp))
                rh, rl = halves(jnp.concatenate(parts, axis=1))
                w3_a[l] += nt_stacked(jnp.concatenate([rh, rl], axis=0), act_ref[0, l, 1, :, e])
                c2 = dot(w3t_ref[l], jnp.concatenate([rh, rl, rh], axis=0)) * slope_ref[0, l, 1, :, e]
                ch, cl = halves(c2)
                w2_a[l] += nt_stacked(jnp.concatenate([ch, cl], axis=0), act_ref[0, l, 0, :, e])
                c1 = dot(w2t_ref[l], jnp.concatenate([ch, cl, ch], axis=0)) * slope_ref[0, l, 0, :, e]
                o = dot_nt(tall(c1), basis_ref[0, :, e])
                w1_a[l] += o[:HID] + o[HID:]

    @pl.when(step == pl.num_programs(0) - 1)
    def _():
        grad_ref[USED_ROWS // 8 * 8 :, :] = jnp.zeros((ROWS - USED_ROWS // 8 * 8, 128), F32)
        for r, row in enumerate(flatten(emb_a[...], C, SPECIES, 10)):
            grad_ref[ROW_EMBED + r : ROW_EMBED + r + 1, :] = row
        for l in range(LAYERS):
            o = ROW_LAYER + l * LAYER_ROWS
            w1 = w1_a[l] * NB ** (-0.5)
            w1 = w1[:, :NB] + w1[:, NB:]
            w1 = jnp.concatenate([w1, jnp.zeros((HID, 8), F32)], axis=1)
            for r, row in enumerate(flatten(w1, HID, NB, 4)):
                grad_ref[o + OFF_W1 + r : o + OFF_W1 + r + 1, :] = row
            for off, rows, acc in ((OFF_W2, 32, w2_a), (OFF_W3, 64, w3_a)):
                w = acc[l] * HID ** (-0.5)
                tmp_s[: 2 * rows, :] = jnp.concatenate([w, jnp.zeros_like(w)], axis=1)
                even = tmp_s[pl.ds(0, rows, stride=2), :]
                odd = tmp_s[pl.ds(1, rows, stride=2), :]
                grad_ref[o + off : o + off + rows, :] = even + pltpu.roll(odd, HID, 1)
            for i, off in enumerate((OFF_LIN, OFF_SQ, OFF_SKIP)):
                grad_ref[o + off : o + off + C, :] = mix_a[l, :, i * C : (i + 1) * C] * C ** (-0.5)
            grad_ref[o + OFF_UP : o + OFF_UP + C, :] = up_a[l] * C ** (-0.5)
            grad_ref[o + OFF_READ : o + OFF_READ + 1, :] = read_a[l, :1, :] * C ** (-0.5)
        grad_ref[ROW_HEAD : ROW_HEAD + RO, :] = head_a[...] * C ** (-0.5)
        grad_ref[ROW_OUT : ROW_OUT + 1, :] = jnp.concatenate(
            [out_a[:1, :] * RO ** (-0.5), jnp.zeros((1, 128 - RO), F32)], axis=1
        )


def frame_spec(shape, memory_space=None):
    def index(i, count):
        return (jnp.minimum(i, count[0] - 1),) + (0,) * (len(shape) - 1)

    return pl.BlockSpec(shape, index)


def whole_spec(shape):
    return pl.BlockSpec(shape, lambda i, count: (0,) * len(shape))


SMEM_SPEC = pl.BlockSpec(memory_space=pltpu.SMEM)
SAVED = (
    ((2 * NB, EDGES), BF16),
    ((2, K, ATOMS), F32),
    ((LAYERS, 2, 2 * HID, EDGES), BF16),
    ((LAYERS, 2, HID, EDGES), F32),
    ((3, C, EDGES), F32),
    ((N_NODES, C, 2 * ATOMS), F32),
    ((2, RO, 2 * ATOMS), F32),
)
WEIGHTS = (((LAYERS, HID, 3 * C), BF16), ((LAYERS, HID, 3 * HID), BF16))


def run_forward(count, lam, theta, positions, species, neighbours):
    n = positions.shape[0]
    shapes = [((8, 128), F32)] + list(SAVED)
    return pl.pallas_call(
        forward_kernel,
        grid_spec=pltpu.PrefetchScalarGridSpec(
            num_scalar_prefetch=1,
            grid=(n,),
            in_specs=[
                SMEM_SPEC,
                whole_spec((ROWS, 128)),
                frame_spec((1, 3, ATOMS)),
                frame_spec((1, 1, ATOMS)),
                frame_spec((1, K, ATOMS)),
            ],
            out_specs=[frame_spec((1,) + s) for s, _ in shapes] + [whole_spec(s) for s, _ in WEIGHTS],
            scratch_shapes=[
                pltpu.VMEM((LAYERS, HID, 48), BF16),
                pltpu.VMEM((LAYERS, HID, 3 * HID), BF16),
                pltpu.VMEM((LAYERS, C, 3 * HID), BF16),
                pltpu.VMEM((LAYERS, C, 3 * C), BF16),
                pltpu.VMEM((LAYERS, C, 3 * C), BF16),
                pltpu.VMEM((LAYERS, C, 9 * C), BF16),
                pltpu.VMEM((LAYERS, 3 * C, 3 * C), BF16),
                pltpu.VMEM((RO, 3 * C), BF16),
                pltpu.VMEM((C, 3 * RO), BF16),
                pltpu.VMEM((C, 48), BF16),
                pltpu.VMEM((LAYERS, C, 128), F32),
                pltpu.VMEM((RO, 128), F32),
                pltpu.VMEM((128, 128), F32),
                pltpu.VMEM((128, 128), F32),
                pltpu.VMEM((ATOMS, EDGES), BF16),
                pltpu.VMEM((LAYERS, C, EDGES), F32),
                pltpu.VMEM((NB * K, ATOMS), F32),
            ],
        ),
        out_shape=[jax.ShapeDtypeStruct((n,) + s, t) for s, t in shapes]
        + [jax.ShapeDtypeStruct(s, t) for s, t in WEIGHTS],
        compiler_params=pltpu.CompilerParams(vmem_limit_bytes=56 * 2**20),
        name="forward",
    )(count, lam, theta, positions, species.reshape(n, 1, ATOMS), neighbours)


def run_backward(count, cot, share, species, saved):
    n = species.shape[0]
    return pl.pallas_call(
        backward_kernel,
        grid_spec=pltpu.PrefetchScalarGridSpec(
            num_scalar_prefetch=1,
            grid=(n,),
            in_specs=[SMEM_SPEC, SMEM_SPEC, frame_spec((1, 1, ATOMS))]
            + [frame_spec((1,) + s) for s, _ in SAVED]
            + [whole_spec(s) for s, _ in WEIGHTS],
            out_specs=whole_spec((ROWS, 128)),
            scratch_shapes=[
                pltpu.VMEM((LAYERS, C, 3 * C), F32),
                pltpu.VMEM((LAYERS, C, C), F32),
                pltpu.VMEM((LAYERS, C, HID), F32),
                pltpu.VMEM((LAYERS, HID, HID), F32),
                pltpu.VMEM((LAYERS, HID, 2 * NB), F32),
                pltpu.VMEM((LAYERS, 8, C), F32),
                pltpu.VMEM((RO, C), F32),
                pltpu.VMEM((8, RO), F32),
                pltpu.VMEM((C, 16), F32),
                pltpu.VMEM((128, 128), F32),
            ],
        ),
        out_shape=jax.ShapeDtypeStruct((ROWS, 128), F32),
        compiler_params=pltpu.CompilerParams(vmem_limit_bytes=56 * 2**20),
        name="backward",
    )(count, cot, share, species.reshape(n, 1, ATOMS), *saved)


def trapezoid():
    index = jnp.arange(WINDOWS, dtype=jnp.int32)
    edges = (index == 0) | (index == WINDOWS - 1)
    return jnp.where(edges, 0.5, 1.0).astype(jnp.float32) / (WINDOWS - 1)


def adam_step(params, first_moment, second_moment, unit):
    new_first = 0.9 * first_moment + 0.1 * unit
    new_second = 0.999 * second_moment + 0.001 * unit * unit
    unbiased_first = new_first / (1.0 - 0.9**10)
    unbiased_second = new_second / (1.0 - 0.999**10)
    new_params = params - 0.01 * unbiased_first / (jnp.sqrt(unbiased_second) + 1e-08)
    return (new_params, new_first, new_second)


def tally(window_ids, count):
    slot_ids = jnp.arange(window_ids.shape[0], dtype=jnp.int32)
    live = (slot_ids < count).astype(jnp.float32)
    onehot = (window_ids[:, None] == jnp.arange(WINDOWS, dtype=jnp.int32)[None, :]).astype(
        jnp.float32
    )
    return onehot * live[:, None]


AXES = {"x": 4, "y": 4, "z": 8, "core": 2}
CHIP = ("x", "y", "z")
CHIPS = 128


def swap_cores(v):
    return lax.ppermute(v, "core", [(0, 1), (1, 0)])


def sum_small(v):
    v = v + swap_cores(v)
    parts = lax.all_to_all(jnp.broadcast_to(v[None], (CHIPS, 8, 128)), CHIP, 0, 0, tiled=True)
    return jnp.sum(parts, axis=0)


def sum_large(v):
    half = ROWS // 2
    piece = half // CHIPS
    core = lax.axis_index("core")
    own = lax.dynamic_slice_in_dim(v, core * half, half)
    own = own + swap_cores(lax.dynamic_slice_in_dim(v, (1 - core) * half, half))
    parts = lax.all_to_all(own.reshape(CHIPS, piece, 128), CHIP, 0, 0, tiled=True)
    total = jnp.broadcast_to(jnp.sum(parts, axis=0)[None], (CHIPS, piece, 128))
    own = lax.all_to_all(total, CHIP, 0, 0, tiled=True).reshape(half, 128)
    other = swap_cores(own)
    first = core == 0
    return jnp.concatenate([jnp.where(first, own, other), jnp.where(first, other, own)], axis=0)


def on_device(
    params, first_moment, second_moment, positions, species, neighbours, window_of, frame_count
):
    count = frame_count[0]
    onehot = tally(window_of, count)
    couplings = window_of.astype(jnp.float32) / (WINDOWS - 1)
    theta = jnp.pad(params, (0, ROWS * 128 - NPAR)).reshape(ROWS, 128)
    out = run_forward(frame_count, couplings, theta, positions, species, neighbours)
    deriv = jnp.where(jnp.arange(positions.shape[0]) < count, out[0][:, 0, 0], 0.0)
    local = jnp.concatenate([jnp.sum(onehot, axis=0), jnp.sum(onehot * deriv[:, None], axis=0), jnp.zeros((64,), F32)])
    total = sum_small(jnp.broadcast_to(local[None], (8, 128)))[0]
    sizes, sums = total[:WINDOWS], total[WINDOWS : 2 * WINDOWS]
    means = sums / jnp.maximum(sizes, 1.0)
    share = jnp.sum(onehot * (trapezoid() / jnp.maximum(sizes, 1.0))[None, :], axis=1)
    centre = jnp.sum(onehot * means[None, :], axis=1)
    cot_energy = -share * (deriv - centre)
    grad = run_backward(frame_count, cot_energy, share, species, out[1:])
    summed = sum_large(grad).reshape(-1)[:NPAR]
    norm = jnp.sqrt(jnp.sum(summed * summed))
    unit = summed * (GRAD_SCALE * math.sqrt(NPAR) / (norm + 1e-06))
    new_params, new_first, new_second = adam_step(params, first_moment, second_moment, unit)
    return (new_params, new_first, new_second, means)


def solution(mesh):
    axes = tuple(AXES)
    split = Mesh(mesh.devices.reshape(tuple(AXES.values())), axes)
    in_specs = (
        P(),
        P(),
        P(),
        P(axes, None, None),
        P(axes, None),
        P(axes, None, None),
        P(axes),
        P(axes),
    )
    out_specs = (P(), P(), P(), P())
    return jax.shard_map(
        on_device, mesh=split, in_specs=in_specs, out_specs=out_specs, check_vma=False
    )
```

time: 2070 us -> 223 us (0.11); the launches traced: 2050 us -> 222 us
  waiting for transfers between devices: 885 us -> 23.2 us
  local copies, waits for them, and re-layouts: 344 us -> 6.18 us
  matrix products: 249 us -> 0 us
  blocking collectives: 289 us -> 58.1 us
  other arithmetic: 231 us -> 7.12 us
  Pallas kernels: 0 us -> 87.8 us
  starting transfers between devices: 0.04 us -> 37.4 us
  loops' own time: 34.2 us -> 0 us
    psum x1 -> x0, waiting for transfers between devices: 885 us -> none  [on_device(): summed = lax.psum(grad, ('dp', 'shard'))]
    psum x1 -> x0, blocking collectives: 289 us -> none  [on_device(): lax.psum((jnp.sum(onehot, axis=0), local_sums), ('dp', 'shard'))]
    dot_general x356 -> x0, matrix products: 249 us -> none  [mult(): jnp.dot(left, right, precision=lax.Precision.HIGHEST, preferred_element_t...]
    gather x56 -> x0, local copies, waits for them, and re-layouts: 224 us -> none  [the longest x48 180 us: frame_energy(): carried = jnp.take(lifted, partner, axis=1)]
    scatter-add x12 -> x0, other arithmetic: 146 us -> none  [frame_energy(): carried = jnp.take(lifted, partner, axis=1)]
    pallas_call x0 -> x2, Pallas kernels: none -> 87.8 us  [the longest x1 58.1 us: run_forward(): pl.pallas_call(forward_kernel, grid_spec=pltpu.PrefetchScalarGridSpec(num...]
    all_to_all x0 -> x2, blocking collectives: none -> 58.1 us  [the longest x1 33.7 us: sum_large(): lax.all_to_all(own.reshape(CHIPS, piece, 128), CHIP, 0, 0, tiled=True)]
    while x541 -> x0, local copies, waits for them, and re-layouts: 50.1 us -> none
  transfers between devices with their start and end apart: 1 -> 4, of which waited for: 1 -> 4; matrix products, arithmetic and copies ran while one was open for 0% -> 0% of each run, Pallas kernels for 0% -> 0%
where the time goes in v1:
time: 223 us; the launch traced here: 222 us
  Pallas kernels  87.8 us (39%)
  blocking collectives  58.1 us (26%)
  starting transfers between devices  37.4 us (17%)
  waiting for transfers between devices  23.2 us (10%)
  other arithmetic  7.12 us (3%)
  local copies, waits for them, and re-layouts  6.18 us (3%)
    pallas_call x1, Pallas kernels, run_forward(): pl.pallas_call(forward_kernel, grid_spec=pltpu.PrefetchScalarGridSpec(num...  58.1 us
    all_to_all x1, starting transfers between devices, sum_small(): lax.all_to_all(jnp.broadcast_to(v[None], (CHIPS, 8, 128)), CHIP, 0, 0, ti...  33.9 us
    all_to_all x1, blocking collectives, sum_large(): lax.all_to_all(own.reshape(CHIPS, piece, 128), CHIP, 0, 0, tiled=True)  33.7 us
    pallas_call x1, Pallas kernels, run_backward(): pl.pallas_call(backward_kernel, grid_spec=pltpu.PrefetchScalarGridSpec(nu...  29.7 us
    all_to_all x1, blocking collectives, sum_large(): own = lax.all_to_all(total, CHIP, 0, 0, tiled=True).reshape(half, 128)  24.5 us
    all_to_all x1, waiting for transfers between devices, sum_small(): lax.all_to_all(jnp.broadcast_to(v[None], (CHIPS, 8, 128)), CHIP, 0, 0, ti...  19.2 us
  transfers between devices with their start and end apart: 4, of which 4 were waited for; matrix products, arithmetic and copies ran while one was open for 0% of the time, Pallas kernels for 0%

profile of v1, /device:TPU:1, one launch (start us, length us, event | category | flops | bytes accessed | tf_op | source)
XLA Modules:
  0.0 222.0 jit_solution(4502079354135303574)
XLA Ops:
  1.3 2.0 pad_bitcast_fusion.th_ref
  3.2 1.3 copy.14.pos_ref
  4.5 1.2 convert_multiply_fusion.lam_ref
  5.7 58.1 %forward.1 = (f32[8,8,128]{2,1,0:T(8,128)}, bf16[8,16,1920]{2,1,0:T(8,128)(2,1)}, f32[8,2,16,128]{3,2,1,0:T(8,128)}, bf16[8,2,2,128,1920]{4,3,2,1,0:T(8,128)(2,1...) custom-call(s32[1]{0:T(128)} %copy.15.count_ref, ...), custom_call_target="tpu_custom_call" | custom-call | tf_op jit(solution)/shard_map/forward/pallas_call | solution.py:441
  63.9 0.9 slice_reduce_fusion
  64.8 0.7 select_reduce_fusion
  65.6 1.2 collective-permute-done
  66.8 0.8 broadcast_in_dim.44
  67.6 33.9 %all-to-all-start = ((f32[128,8,128]{2,1,0:T(8,128)}), f32[128,8,128]{2,1,0:T(8,128)S(1)}, u32[]{:S(2)}, u32[]{:S(2)}) async-start(f32[128,8,128]{2,1,0:T(8,128)} %broadcast_in_dim.44), calls=%async_computation | async-start | bytes 1048576 | tf_op jit(solution)/shard_map/all_to_all | solution.py:546
  101.5 19.2 %all-to-all-done = f32[128,8,128]{2,1,0:T(8,128)S(1)} async-done(((f32[128,8,128]{2,1,0:T(8,128)}), f32[128,8,128]{2,1,0:T(8,128)S(1)}, u32[]{:S(2)}, u32[]{:S(2)}) %all-to-all-start) | async-done | bytes 524320 | tf_op jit(solution)/shard_map/all_to_all | solution.py:546
  120.7 0.1 reduce_sum.65
  120.9 0.9 fusion.2
  121.8 0.5 subtract_multiply_fusion.ce_ref
  122.4 29.7 %backward.1 = f32[1280,128]{1,0:T(8,128)} custom-call(s32[1]{0:T(128)} %copy.15.count_ref, f32[8]{0:T(128)} %subtract_multiply_fusion.ce_ref, f32[8]{0:T(128)} %copy-done.3, s32[8,1,128]{2,1,0:T(1,128)} %bitcast.14, bf16[8,16,1920]{2,1,0:T(8,128)(2,1)} %get-tuple-element.15.basis_ref, f32[8,2,16,128]{3,2,1,0:T(8,128)} %get-tuple-element.16.fac_ref, ...), custom_call_target="tpu_custom_call" | custom-call | tf_op jit(solution)/shard_map/backward/pallas_call | solution.py:483
  152.1 1.0 constant_dynamic-slice_fusion
  153.2 1.6 collective-permute-done.1
  154.8 1.0 dynamic-slice_add_fusion
  155.9 33.7 %all_to_all.15 = f32[128,5,128]{2,1,0:T(8,128)S(1)} all-to-all(f32[128,5,128]{2,1,0:T(8,128)S(1)} %reshape.69), channel_id=1, replica_groups=mesh['x'=4,'y'=4,'z'=8,'core'=2] {'x','y','z'}, dimensions={0} | all-to-all | bytes 655360 | tf_op jit(solution)/shard_map/all_to_all | solution.py:556
  189.5 0.1 reduce_sum.68
  189.7 24.5 %all_to_all.16 = f32[128,5,128]{2,1,0:T(8,128)S(1)} all-to-all(f32[128,5,128]{2,1,0:T(8,128)S(1)} %broadcast_in_dim.45), channel_id=1, replica_groups=mesh['x'=4,'y'=4,'z'=8,'core'=2] {'x','y','z'}, dimensions={0} | all-to-all | bytes 655360 | tf_op jit(solution)/shard_map/all_to_all | solution.py:558
  214.2 3.4 %collective-permute-start.2 = (f32[640,128]{1,0:T(8,128)S(1)}, f32[640,128]{1,0:T(8,128)S(1)}, u32[]{:S(2)}, u32[]{:S(2)}) collective-permute-start(f32[640,128]{1,0:T(8,128)S(1)} %reshape.70), channel_id=1, source_target_pairs={{0,1},{1,0},{2,3},{3,2},{4,5},{5,4},{6,7},{7,6},{8,9},{9,8},{10,11... | collective-permute-start | bytes 983048 | tf_op jit(solution)/shard_map/ppermute | solution.py:541
  217.6 1.3 collective-permute-done.2
  219.0 0.8 multiply_reduce_fusion
  220.5 1.5 divide_subtract_fusion
  (24 shorter events, 0.6 us)
Async XLA Ops:
  65.6 1.2 collective-permute-start
  67.6 53.1 %all-to-all-start = ((f32[128,8,128]{2,1,0:T(8,128)}), f32[128,8,128]{2,1,0:T(8,128)S(1)}, u32[]{:S(2)}, u32[]{:S(2)}) async-start(f32[128,8,128]{2,1,0:T(8,128)} %broadcast_in_dim.44), calls=%async_computation | async-start | bytes 1048576 | tf_op jit(solution)/shard_map/all_to_all | solution.py:546
  120.9 31.1 %copy-start.4 = (f32[32]{0:T(128)}, f32[32]{0:T(128)S(1)}, u32[]{:S(2)}) copy-start(f32[32]{0:T(128)S(1)} %get-tuple-element.33) | copy-start | bytes 388
  121.8 0.5 copy-start.3
  122.4 98.1 %copy-start = (f32[160272]{0:T(1024)S(1)}, f32[160272]{0:T(1024)}, u32[]{:S(2)}) copy-start(f32[160272]{0:T(1024)} %param.8) | copy-start | bytes 1923268
  122.4 98.1 %copy-start.1 = (f32[160272]{0:T(1024)S(1)}, f32[160272]{0:T(1024)}, u32[]{:S(2)}) copy-start(f32[160272]{0:T(1024)} %param.9) | copy-start | bytes 1923268
  122.4 98.1 %copy-start.2 = (f32[160272]{0:T(1024)S(1)}, f32[160272]{0:T(1024)}, u32[]{:S(2)}) copy-start(f32[160272]{0:T(1024)} %param.10) | copy-start | bytes 1923268
  153.1 1.7 collective-permute-start.1
  214.2 4.7 %collective-permute-start.2 = (f32[640,128]{1,0:T(8,128)S(1)}, f32[640,128]{1,0:T(8,128)S(1)}, u32[]{:S(2)}, u32[]{:S(2)}) collective-permute-start(f32[640,128]{1,0:T(8,128)S(1)} %reshape.70), channel_id=1, source_target_pairs={{0,1},{1,0},{2,3},{3,2},{4,5},{5,4},{6,7},{7,6},{8,9},{9,8},{10,11... | collective-permute-start | bytes 983048 | tf_op jit(solution)/shard_map/ppermute | solution.py:541

commit v2 on v0

v2 whole, which is shorter than its diff:
```python
import math

import jax
import jax.numpy as jnp
from jax import lax
from jax.experimental import pallas as pl
from jax.experimental.pallas import tpu as pltpu
from jax.sharding import Mesh
from jax.sharding import PartitionSpec as P

C = 128
HID = 64
NB = 8
SPECIES = 10
RO = 16
LAYERS = 2
WINDOWS = 32
ATOMS = 128
SOLUTE = 16
K = 16
SLOTS = K - 1
EDGES = SLOTS * ATOMS
NPAR = 160272
ROWS = 1280

RADIUS_CUT = 8.0
SOFTENING = 0.01
GRAD_SCALE = 4.0

ROW_EMBED = 0
ROW_LAYER = 10
LAYER_ROWS = 613
OFF_W1, OFF_W2, OFF_W3, OFF_UP, OFF_LIN, OFF_SQ, OFF_SKIP, OFF_READ = 0, 4, 36, 100, 228, 356, 484, 612
ROW_HEAD = ROW_LAYER + LAYERS * LAYER_ROWS
ROW_OUT = ROW_HEAD + RO
USED_ROWS = ROW_OUT + 1

ROW_POS, ROW_SPECIES, ROW_META, FRAME_ROWS = SLOTS, SLOTS + 3, SLOTS + 4, 24
KEEP = 4
GROUP = 16
PLAN_COUNT, PLAN_OWN = 8, 9

CHUNKS = ((0, 4), (4, 8), (8, 12), (12, 15))
F32, BF16 = jnp.float32, jnp.bfloat16

N_H0, N_P0, N_CH1, N_CL0, N_CP0, N_H1, N_P1, N_CH2, N_CL1, N_CP1, N_H2, N_CH0 = range(12)
N_NODES = 12


def halves(x):
    hi = x.astype(BF16)
    return hi, (x - hi.astype(F32)).astype(BF16)


def stack_left(w):
    hi, lo = halves(w)
    return jnp.concatenate([hi, hi, lo], axis=1)


def dot(a, b):
    return jnp.dot(a, b, preferred_element_type=F32)


def dot_nt(a, b):
    return lax.dot_general(a, b, (((1,), (1,)), ((), ())), preferred_element_type=F32)


def mm(left, x):
    hi, lo = halves(x)
    return dot(left, jnp.concatenate([hi, lo, hi], axis=0))


def nt_stacked(xs, ys):
    m, n = xs.shape[0] // 2, ys.shape[0] // 2
    o = dot_nt(xs, ys)
    return o[:m, :n] + (o[:m, n:] + o[m:, :n])


def tall(x):
    return jnp.concatenate(halves(x), axis=0)


def nt(x, y):
    return nt_stacked(tall(x), tall(y))


def tile_rows(x, reps):
    return jnp.concatenate([x] * reps, axis=1)


def unflatten(rows, height, width):
    total = None
    for r, row in enumerate(rows):
        place = lax.broadcasted_iota(jnp.int32, (height, 128), 1) + 128 * r
        own = lax.broadcasted_iota(jnp.int32, (height, 128), 0)
        first = own * width
        kept = jnp.where((place >= first) & (place < first + width), jnp.broadcast_to(row, (height, 128)), 0.0)
        col = lax.broadcasted_iota(jnp.int32, (128, 16), 1)
        pos = (lax.broadcasted_iota(jnp.int32, (128, 16), 0) + 128 * r) % width
        pick = (col == pos).astype(BF16)
        a = kept.astype(BF16)
        rest = kept - a.astype(F32)
        b = rest.astype(BF16)
        c = (rest - b.astype(F32)).astype(BF16)
        piece = dot(a, pick) + (dot(b, pick) + dot(c, pick))
        total = piece if total is None else total + piece
    return total


def flatten(mat, height, width, n_rows):
    a = mat.astype(BF16)
    rest = mat - a.astype(F32)
    b = rest.astype(BF16)
    c = (rest - b.astype(F32)).astype(BF16)
    out = []
    for r in range(n_rows):
        col = lax.broadcasted_iota(jnp.int32, (16, 128), 0)
        pos = (lax.broadcasted_iota(jnp.int32, (16, 128), 1) + 128 * r) % width
        pick = (col == pos).astype(BF16)
        spread = dot(a, pick) + (dot(b, pick) + dot(c, pick))
        place = lax.broadcasted_iota(jnp.int32, (height, 128), 1) + 128 * r
        first = lax.broadcasted_iota(jnp.int32, (height, 128), 0) * width
        kept = jnp.where((place >= first) & (place < first + width), spread, 0.0)
        out.append(jnp.sum(kept, axis=0, keepdims=True))
    return out


def silu_parts(z):
    s = 0.5 * jnp.tanh(0.5 * z) + 0.5
    value = z * s
    return value, s + value * (1.0 - s)


def prepare(th_ref, w1_s, w2_s, w3_s, up_s, upt_s, mix_s, mixt_s, hd_s, hdt_s, emb_s, read_s, out_s, w3t_ref, w2t_ref, tmp_s):
    emb = unflatten([th_ref[ROW_EMBED + r : ROW_EMBED + r + 1, :] for r in range(10)], C, SPECIES)
    emb_s[...] = stack_left(emb)
    for l in range(LAYERS):
        o = ROW_LAYER + l * LAYER_ROWS
        w1 = unflatten([th_ref[o + OFF_W1 + r : o + OFF_W1 + r + 1, :] for r in range(4)], HID, NB) * NB ** (-0.5)
        w1_s[l] = stack_left(w1)
        for off, rows, reach, dst, dst_t in ((OFF_W2, 32, HID, w2_s, w2t_ref), (OFF_W3, 64, HID, w3_s, w3t_ref)):
            packed = th_ref[o + off : o + off + rows, :] * reach ** (-0.5)
            tmp_s[pl.ds(0, rows, stride=2), :] = packed
            tmp_s[pl.ds(1, rows, stride=2), :] = pltpu.roll(packed, HID, 1)
            wide = tmp_s[: 2 * rows, :]
            w = wide[:, :HID]
            dst[l] = stack_left(w)
            if rows == 32:
                wide = jnp.concatenate([wide, wide], axis=0)
            wt = jnp.transpose(wide)[:HID, : 2 * rows]
            dst_t[l] = jnp.concatenate(halves(wt), axis=1)
        mats, mats_t = [], []
        for off in (OFF_LIN, OFF_SQ, OFF_SKIP):
            w = th_ref[o + off : o + off + C, :] * C ** (-0.5)
            mats.append(w)
            mats_t.append(jnp.transpose(w))
        mix_s[l] = stack_left(jnp.concatenate(mats, axis=1))
        mixt_s[l] = stack_left(jnp.concatenate(mats_t, axis=0))
        w = th_ref[o + OFF_UP : o + OFF_UP + C, :] * C ** (-0.5)
        up_s[l] = stack_left(w)
        upt_s[l] = stack_left(jnp.transpose(w))
        read_s[l] = jnp.transpose(
            jnp.broadcast_to(th_ref[o + OFF_READ : o + OFF_READ + 1, :] * C ** (-0.5), (128, 128))
        )
    w = th_ref[ROW_HEAD : ROW_HEAD + RO, :] * C ** (-0.5)
    hd_s[...] = stack_left(w)
    wide = jnp.concatenate([w, jnp.zeros((128 - RO, 128), F32)], axis=0)
    hdt_s[...] = stack_left(jnp.transpose(wide)[:, :RO])
    out_s[...] = jnp.transpose(jnp.broadcast_to(th_ref[ROW_OUT : ROW_OUT + 1, :] * RO ** (-0.5), (128, 128)))[:RO, :]


def run_frame(
    x,
    w1_s, w2_s, w3_s, up_s, upt_s, mix_s, mixt_s, hd_s, hdt_s, emb_s, read_s, out_s,
    deriv_ref, basis_ref, fac_ref, act_ref, slope_ref, first_ref, gath_ref, node_ref, head_ref,
    oh_s, rad_s, dist_s,
):
    window = x[ROW_META : ROW_META + 1, :1]
    lam = window / (WINDOWS - 1)
    slot = lax.broadcasted_iota(jnp.int32, (K, ATOMS), 0)
    nb = jnp.where(slot < SLOTS, x[:K].astype(jnp.int32), -1)
    partner = jnp.maximum(nb, 0)
    present = nb >= 0
    species = x[ROW_SPECIES : ROW_SPECIES + 1, :]
    r2 = jnp.full((K, ATOMS), SOFTENING, F32)
    for d in range(3):
        row = jnp.broadcast_to(x[ROW_POS + d : ROW_POS + d + 1, :], (K, ATOMS))
        delta = jnp.take_along_axis(row, partner, axis=1) - row
        r2 = r2 + delta * delta
    radius = jnp.sqrt(r2)
    ratio = radius * (1.0 / RADIUS_CUT)
    env = 1.0 - ratio * ratio
    env = jnp.where(present, env * env, 0.0) * (1.0 / K)
    atom = lax.broadcasted_iota(jnp.int32, (K, ATOMS), 1)
    crossing = (atom < SOLUTE) != (partner < SOLUTE)
    fac = jnp.where(crossing, lam * env, env)
    dfac = jnp.where(crossing, env, 0.0)
    fac_ref[0, 0] = fac
    fac_ref[0, 1] = dfac
    fac_ref[0, 2] = jnp.broadcast_to(species, (K, ATOMS))

    angle = ratio * math.pi
    s1 = jnp.sin(angle) * (math.sqrt(2.0 / RADIUS_CUT) / radius)
    twice = 2.0 * jnp.cos(angle)
    prev, cur = jnp.zeros_like(s1), s1
    for m in range(NB):
        dist_s[m * K : (m + 1) * K, :] = cur
        prev, cur = cur, twice * cur - prev
    basis = jnp.concatenate([dist_s[pl.ds(k, NB, stride=K), :] for k in range(SLOTS)], axis=1)
    bhi, blo = basis.astype(BF16).astype(F32), None
    blo = basis - bhi
    wide = jnp.concatenate([bhi, blo], axis=0).astype(BF16)
    basis_ref[0] = wide
    w1_rhs = jnp.concatenate([bhi, jnp.zeros_like(bhi), blo, jnp.zeros_like(bhi), bhi, jnp.zeros_like(bhi)], axis=0).astype(BF16)

    sub = lax.broadcasted_iota(jnp.int32, (ATOMS, ATOMS), 0)
    for k in range(SLOTS):
        hit = jnp.broadcast_to(partner[k : k + 1, :], (ATOMS, ATOMS)) == sub
        oh_s[:, k * ATOMS : (k + 1) * ATOMS] = jnp.where(hit, 1.0, 0.0).astype(BF16)

    for l in range(LAYERS):
        for k0, k1 in CHUNKS:
            e = slice(k0 * ATOMS, k1 * ATOMS)
            z1 = dot(w1_s[l], w1_rhs[:, e])
            v1, d1 = silu_parts(z1)
            h1, l1 = halves(v1)
            act_ref[0, l, 0, :, e] = h1
            slope_ref[0, l, 0, :, e] = d1.astype(BF16)
            z2 = dot(w2_s[l], jnp.concatenate([h1, l1, h1], axis=0))
            v2, d2 = silu_parts(z2)
            h2, l2 = halves(v2)
            act_ref[0, l, 1, :, e] = h2
            slope_ref[0, l, 1, :, e] = d2.astype(BF16)
            rad_s[l, :, e] = dot(w3_s[l], jnp.concatenate([h2, l2, h2], axis=0))

    rows16 = lax.broadcasted_iota(jnp.int32, (16, ATOMS), 0)
    spc = jnp.where(rows16 == jnp.broadcast_to(species, (16, ATOMS)).astype(jnp.int32), 1.0, 0.0)
    feat = mm(emb_s[...], spc)
    zero = jnp.zeros((C, ATOMS), F32)
    feat = jnp.concatenate([feat, zero], axis=1)
    deriv = jnp.zeros((), F32)
    pools = []
    for l in range(LAYERS):
        node_ref[0, (N_H0, N_H1)[l]] = feat
        if l == 0:
            lift = mm(up_s[l], feat[:, :ATOMS])
            lhs = jnp.concatenate(halves(lift), axis=1)
        else:
            lift = mm(up_s[l], feat)
            lhs = jnp.concatenate(
                [jnp.concatenate(halves(lift[:, :ATOMS]), axis=1), jnp.concatenate(halves(lift[:, ATOMS:]), axis=1)],
                axis=0,
            )
        pool, dpool = zero, zero
        for k0, k1 in CHUNKS:
            e = slice(k0 * ATOMS, k1 * ATOMS)
            oh = oh_s[:, e]
            g = dot(lhs, jnp.concatenate([oh, oh], axis=0))
            if l == 0:
                first_ref[0, :, e] = g
            else:
                gath_ref[0, 0, :, e] = g[:C].astype(BF16)
                gath_ref[0, 1, :, e] = g[C:].astype(BF16)
            for k in range(k0, k1):
                t = slice((k - k0) * ATOMS, (k - k0 + 1) * ATOMS)
                rad = rad_s[l, :, k * ATOMS : (k + 1) * ATOMS]
                rg = rad * g[:C, t]
                pool = pool + fac[k : k + 1, :] * rg
                dpool = dpool + dfac[k : k + 1, :] * rg
                if l == 1:
                    dpool = dpool + fac[k : k + 1, :] * (rad * g[C:, t])
        node_ref[0, (N_P0, N_P1)[l]] = jnp.concatenate([pool, dpool], axis=1)
        pools.append((pool, dpool))
        x = jnp.concatenate(
            [
                jnp.concatenate([pool, dpool], axis=1),
                jnp.concatenate([pool * pool, 2.0 * pool * dpool], axis=1),
                feat,
            ],
            axis=0,
        )
        feat = mm(mix_s[l], x)
        deriv = deriv + jnp.sum(read_s[l] * feat[:, ATOMS:])
    node_ref[0, N_H2] = feat
    q = mm(hd_s[...], feat)
    q0, q1 = q[:, :ATOMS], q[:, ATOMS:]
    sg = 0.5 * jnp.tanh(0.5 * q0) + 0.5
    val = q0 * sg
    first = sg + val * (1.0 - sg)
    second = sg * (1.0 - sg) * (2.0 + q0 * (1.0 - 2.0 * sg))
    tail = first * q1
    deriv = deriv + jnp.sum(out_s[...] * tail)
    lane = lax.broadcasted_iota(jnp.int32, (8, 128), 1)
    deriv_ref[0] = jnp.where(lane == 0, deriv, jnp.broadcast_to(window, (8, 128)))
    head_ref[0, 1] = jnp.concatenate([val, tail], axis=1)
    co_q = jnp.concatenate([out_s[...] * first, out_s[...] * second * q1], axis=1)
    head_ref[0, 0] = co_q
    co = mm(hdt_s[...], co_q) + jnp.concatenate([read_s[1], zero], axis=1)
    for l in (1, 0):
        node_ref[0, (N_CH1, N_CH2)[l]] = co
        y = mm(mixt_s[l], co)
        pool, dpool = pools[l]
        ya, yb = y[:, :ATOMS], y[:, ATOMS:]
        ap = ya[:C] + 2.0 * pool * ya[C : 2 * C]
        bp = yb[:C] + 2.0 * pool * yb[C : 2 * C] + 2.0 * dpool * ya[C : 2 * C]
        node_ref[0, (N_CP0, N_CP1)[l]] = jnp.concatenate([ap, bp], axis=1)
        acc = None
        for k0, k1 in CHUNKS:
            parts = [[], []]
            for k in range(k0, k1):
                rad = rad_s[l, :, k * ATOMS : (k + 1) * ATOMS]
                f, df = fac[k : k + 1, :], dfac[k : k + 1, :]
                parts[0].append((rad * (f * ap)).astype(BF16))
                parts[1].append((rad * (f * bp + df * ap)).astype(BF16))
            left = jnp.concatenate([jnp.concatenate(lst, axis=1) for lst in parts], axis=0)
            piece = dot_nt(left, oh_s[:, k0 * ATOMS : k1 * ATOMS])
            acc = piece if acc is None else acc + piece
        cl = jnp.concatenate([acc[:C], acc[C:]], axis=1)
        node_ref[0, (N_CL0, N_CL1)[l]] = cl
        co = y[2 * C :] + mm(upt_s[l], cl)
        if l == 1:
            co = co + jnp.concatenate([read_s[0], zero], axis=1)
    node_ref[0, N_CH0] = co
    at = jnp.broadcast_to(window.astype(jnp.int32), (8, 128))
    return jnp.where(lane == at, 1.0, jnp.where(lane == at + WINDOWS, deriv, 0.0))


N_WEIGHTS = 12
N_SAVED = 9


def pack_kernel(count_ref, window_ref, pos_ref, spc_ref, nb_ref, own_ref, send_ref, wide_s):
    n = nb_ref.shape[0]
    lane = lax.broadcasted_iota(jnp.int32, (1, 128), 1)
    for f in range(n):
        own_ref[f, :SLOTS, :] = nb_ref[f, :SLOTS, :].astype(F32)
        for d in range(3):
            own_ref[f, ROW_POS + d : ROW_POS + d + 1, :] = pos_ref[d, f : f + 1, :]
        own_ref[f, ROW_SPECIES : ROW_SPECIES + 1, :] = spc_ref[f : f + 1, :].astype(F32)
        own_ref[f, ROW_META + 1 :, :] = jnp.zeros((FRAME_ROWS - ROW_META - 1, 128), F32)
        own_ref[f, ROW_META : ROW_META + 1, :] = jnp.where(lane == 0, window_ref[f], count_ref[0]).astype(F32)
    for f in range(KEEP, n):
        wide_s[(f - KEEP) * FRAME_ROWS : (f - KEEP + 1) * FRAME_ROWS, :] = own_ref[f]
    wide = wide_s[...]
    for g in range(GROUP):
        send_ref[g] = wide


def deal_kernel(me_ref, rows_ref, plan_ref):
    n = 8
    lane = lax.broadcasted_iota(jnp.int32, (GROUP, 128), 1)
    gid = lax.broadcasted_iota(jnp.int32, (GROUP, 128), 0)
    meta = rows_ref[:, ROW_META % 8, :]
    counts = jnp.broadcast_to(jnp.sum(jnp.where(lane == 1, meta, 0.0), axis=1, keepdims=True), (GROUP, 128))
    base = jnp.minimum(counts, float(KEEP))
    surplus = counts - base
    total = jnp.sum(surplus, axis=0, keepdims=True)
    lane_f = lane.astype(F32)
    room = jnp.sum(jnp.maximum(lane_f + 1.0 - base, 0.0), axis=0, keepdims=True)
    full = jnp.where((room <= total) & (lane[:1] < n), 1.0, 0.0)
    level = jnp.broadcast_to(jnp.sum(full, axis=1, keepdims=True), (GROUP, 128))
    taken = jnp.maximum(level - base, 0.0)
    left = total - jnp.sum(taken, axis=0, keepdims=True)
    tri_r = lax.broadcasted_iota(jnp.int32, (GROUP, GROUP), 0)
    tri_c = lax.broadcasted_iota(jnp.int32, (GROUP, GROUP), 1)
    before = jnp.where(tri_c < tri_r, 1.0, 0.0).astype(BF16)
    open_ = jnp.where(base <= level, 1.0, 0.0)
    rank = dot(before, open_.astype(BF16))
    taken = taken + jnp.where(rank < left, open_, 0.0)
    offset = dot(before, surplus.astype(BF16))
    me = me_ref[0]
    start = jnp.sum(jnp.where(gid < me, taken, 0.0), axis=0, keepdims=True)
    mine = jnp.sum(jnp.where(gid == me, base + taken, 0.0), axis=0, keepdims=True)
    held = jnp.sum(jnp.where(gid == me, base, 0.0), axis=0, keepdims=True)
    order = jnp.where(lane_f < surplus, offset + lane_f, -1.0)
    place = (gid * (n - KEEP) + lane).astype(F32)
    for j in range(n):
        hit = jnp.where(order == start + float(j), place, 0.0)
        one = jnp.sum(jnp.sum(hit, axis=0, keepdims=True), axis=1, keepdims=True)
        plan_ref[j : j + 1, :] = jnp.broadcast_to(one, (1, 128)).astype(jnp.int32)
    plan_ref[n : n + 1, :] = mine.astype(jnp.int32)
    plan_ref[n + 1 : n + 2, :] = held.astype(jnp.int32)
    plan_ref[n + 2 :, :] = jnp.zeros((GROUP - n - 2, 128), jnp.int32)


def first_kernel(th_ref, own_ref, *refs):
    weights, spare = refs[:N_WEIGHTS], refs[N_WEIGHTS : N_WEIGHTS + 2]
    saved = refs[N_WEIGHTS + 2 : N_WEIGHTS + 2 + N_SAVED]
    tally_ref, oh_s, rad_s, dist_s, tmp_s = refs[N_WEIGHTS + 2 + N_SAVED :]
    prepare(th_ref, *weights, *spare, tmp_s)
    tally_ref[...] = run_frame(own_ref[0], *weights, *saved, oh_s, rad_s, dist_s)


def rest_kernel(plan_ref, own_ref, other_ref, first_ref, *refs):
    weights = refs[:N_WEIGHTS]
    saved = refs[N_WEIGHTS + N_SAVED : N_WEIGHTS + 2 * N_SAVED]
    tally_ref, oh_s, rad_s, dist_s = refs[N_WEIGHTS + 2 * N_SAVED :]
    step = pl.program_id(0)

    @pl.when(step == 0)
    def _():
        tally_ref[...] = first_ref[...]

    @pl.when(step + 1 < plan_ref[PLAN_COUNT, 0])
    def _():
        x = jnp.where(step + 1 < plan_ref[PLAN_OWN, 0], own_ref[0], other_ref[0])
        tally_ref[...] += run_frame(x, *weights, *saved, oh_s, rad_s, dist_s)


def backward_kernel(
    plan_ref, core_ref, parts_ref, deriv_ref, basis_ref, fac_ref, act_ref, slope_ref, first_ref, gath_ref, node_ref, head_ref, w3t_ref, w2t_ref,
    mine_ref, other_ref, means_ref,
    grad_ref, window_s, mix_a, up_a, w3_a, w2_a, w1_a, read_a, head_a, out_a, emb_a, tmp_s,
):
    step = pl.program_id(0)

    @pl.when(step == 0)
    def _():
        for ref in (mix_a, up_a, w3_a, w2_a, w1_a, read_a, head_a, out_a, emb_a):
            ref[...] = jnp.zeros(ref.shape, F32)
        total = jnp.broadcast_to(jnp.sum(parts_ref[...], axis=0, keepdims=True), (8, 128))
        lane = lax.broadcasted_iota(jnp.int32, (8, 128), 1)
        sizes = jnp.maximum(total, 1.0)
        means = pltpu.roll(total, 128 - WINDOWS, 1) / sizes
        ends = (lane == 0) | (lane == WINDOWS - 1)
        weight = jnp.where(ends, 0.5, 1.0) / (WINDOWS - 1)
        means_ref[...] = means
        window_s[0] = means
        window_s[1] = weight / sizes

    @pl.when(step < plan_ref[PLAN_COUNT, 0])
    def _():
        mine = lax.broadcasted_iota(jnp.int32, (1, 128), 1) == deriv_ref[0, :1, 1:2].astype(jnp.int32)
        centre = jnp.sum(jnp.where(mine, window_s[0, :1], 0.0), axis=1, keepdims=True)
        sh = jnp.sum(jnp.where(mine, window_s[1, :1], 0.0), axis=1, keepdims=True)
        ce = -sh * (deriv_ref[0, :1, :1] - centre)
        fac, dfac = fac_ref[0, 0], fac_ref[0, 1]

        def pair(x):
            a, b = x[:, :ATOMS], x[:, ATOMS:]
            return jnp.concatenate([ce * a + sh * b, sh * a], axis=1)

        weights = jnp.concatenate([jnp.broadcast_to(ce, (8, ATOMS)), jnp.broadcast_to(sh, (8, ATOMS))], axis=1)
        co0 = node_ref[0, N_CH0]
        a0 = ce * co0[:, :ATOMS] + sh * co0[:, ATOMS:]
        rows16 = lax.broadcasted_iota(jnp.int32, (16, ATOMS), 0)
        spc = jnp.where(rows16 == fac_ref[0, 2].astype(jnp.int32), 1.0, 0.0).astype(BF16)
        o = dot_nt(tall(a0), spc)
        emb_a[...] += o[:C] + o[C:]
        head_a[...] += nt(pair(head_ref[0, 0]), node_ref[0, N_H2])
        out_a[...] += nt(weights, head_ref[0, 1])
        for l in range(LAYERS):
            feat = node_ref[0, (N_H0, N_H1)[l]]
            pp = node_ref[0, (N_P0, N_P1)[l]]
            pool, dpool = pp[:, :ATOMS], pp[:, ATOMS:]
            x = jnp.concatenate([pp, jnp.concatenate([pool * pool, 2.0 * pool * dpool], axis=1), feat], axis=0)
            mix_a[l] += nt(pair(node_ref[0, (N_CH1, N_CH2)[l]]), x)
            up_a[l] += nt(pair(node_ref[0, (N_CL0, N_CL1)[l]]), feat)
            read_a[l] += nt(weights, node_ref[0, (N_H1, N_H2)[l]])
            cp = pair(node_ref[0, (N_CP0, N_CP1)[l]])
            ap, bp = cp[:, :ATOMS], cp[:, ATOMS:]
            for k0, k1 in CHUNKS:
                e = slice(k0 * ATOMS, k1 * ATOMS)
                parts = []
                for k in range(k0, k1):
                    t = slice(k * ATOMS, (k + 1) * ATOMS)
                    f, df = fac[k : k + 1, :], dfac[k : k + 1, :]
                    u = f * ap + df * bp
                    if l == 0:
                        r = first_ref[0, :, t] * u
                    else:
                        r = gath_ref[0, 0, :, t].astype(F32) * u + gath_ref[0, 1, :, t].astype(F32) * (f * bp)
                    parts.append(r.astype(BF16))
                rh = jnp.concatenate(parts, axis=1)
                w3_a[l] += dot_nt(rh, act_ref[0, l, 1, :, e])
                c2 = (dot(w3t_ref[l], jnp.concatenate([rh, rh], axis=0)) * slope_ref[0, l, 1, :, e].astype(F32)).astype(BF16)
                w2_a[l] += dot_nt(c2, act_ref[0, l, 0, :, e])
                c1 = (dot(w2t_ref[l], jnp.concatenate([c2, c2], axis=0)) * slope_ref[0, l, 0, :, e].astype(F32)).astype(BF16)
                w1_a[l] += dot_nt(c1, basis_ref[0, :, e])

    @pl.when(step == pl.num_programs(0) - 1)
    def _():
        grad_ref[USED_ROWS // 8 * 8 :, :] = jnp.zeros((ROWS - USED_ROWS // 8 * 8, 128), F32)
        for r, row in enumerate(flatten(emb_a[...], C, SPECIES, 10)):
            grad_ref[ROW_EMBED + r : ROW_EMBED + r + 1, :] = row
        for l in range(LAYERS):
            o = ROW_LAYER + l * LAYER_ROWS
            w1 = w1_a[l] * NB ** (-0.5)
            w1 = w1[:, :NB] + w1[:, NB:]
            w1 = jnp.concatenate([w1, jnp.zeros((HID, 8), F32)], axis=1)
            for r, row in enumerate(flatten(w1, HID, NB, 4)):
                grad_ref[o + OFF_W1 + r : o + OFF_W1 + r + 1, :] = row
            for off, rows, acc in ((OFF_W2, 32, w2_a), (OFF_W3, 64, w3_a)):
                w = acc[l] * HID ** (-0.5)
                tmp_s[: 2 * rows, :] = jnp.concatenate([w, jnp.zeros_like(w)], axis=1)
                even = tmp_s[pl.ds(0, rows, stride=2), :]
                odd = tmp_s[pl.ds(1, rows, stride=2), :]
                grad_ref[o + off : o + off + rows, :] = even + pltpu.roll(odd, HID, 1)
            for i, off in enumerate((OFF_LIN, OFF_SQ, OFF_SKIP)):
                grad_ref[o + off : o + off + C, :] = mix_a[l, :, i * C : (i + 1) * C] * C ** (-0.5)
            grad_ref[o + OFF_UP : o + OFF_UP + C, :] = up_a[l] * C ** (-0.5)
            grad_ref[o + OFF_READ : o + OFF_READ + 1, :] = read_a[l, :1, :] * C ** (-0.5)
        grad_ref[ROW_HEAD : ROW_HEAD + RO, :] = head_a[...] * C ** (-0.5)
        grad_ref[ROW_OUT : ROW_OUT + 1, :] = jnp.concatenate(
            [out_a[:1, :] * RO ** (-0.5), jnp.zeros((1, 128 - RO), F32)], axis=1
        )
        half = ROWS // 2
        core = core_ref[0]
        mine_ref[...] = grad_ref[pl.ds(pl.multiple_of(core * half, half), half), :]
        other_ref[...] = grad_ref[pl.ds(pl.multiple_of((1 - core) * half, half), half), :]


def whole_spec(shape):
    return pl.BlockSpec(shape, lambda i, *_: (0,) * len(shape))


SMEM_SPEC = pl.BlockSpec(memory_space=pltpu.SMEM)
SAVED = (
    ((8, 128), F32),
    ((2 * NB, EDGES), BF16),
    ((3, K, ATOMS), F32),
    ((LAYERS, 2, HID, EDGES), BF16),
    ((LAYERS, 2, HID, EDGES), BF16),
    ((C, EDGES), F32),
    ((2, C, EDGES), BF16),
    ((N_NODES, C, 2 * ATOMS), F32),
    ((2, RO, 2 * ATOMS), F32),
)
WEIGHTS = (
    ((LAYERS, HID, 48), BF16),
    ((LAYERS, HID, 3 * HID), BF16),
    ((LAYERS, C, 3 * HID), BF16),
    ((LAYERS, C, 3 * C), BF16),
    ((LAYERS, C, 3 * C), BF16),
    ((LAYERS, C, 9 * C), BF16),
    ((LAYERS, 3 * C, 3 * C), BF16),
    ((RO, 3 * C), BF16),
    ((C, 3 * RO), BF16),
    ((C, 48), BF16),
    ((LAYERS, C, 128), F32),
    ((RO, 128), F32),
)
SPARE = (((LAYERS, HID, 2 * C), BF16), ((LAYERS, HID, 2 * HID), BF16))
FRAME_SCRATCH = [
    pltpu.VMEM((ATOMS, EDGES), BF16),
    pltpu.VMEM((LAYERS, C, EDGES), F32),
    pltpu.VMEM((NB * K, ATOMS), F32),
]
LIMIT = pltpu.CompilerParams(vmem_limit_bytes=56 * 2**20)


TALLY = jax.ShapeDtypeStruct((8, 128), F32)


def run_pack(count, window_of, positions, species, neighbours):
    n = positions.shape[0]
    return pl.pallas_call(
        pack_kernel,
        in_specs=[SMEM_SPEC, SMEM_SPEC] + [pl.BlockSpec(memory_space=pltpu.VMEM)] * 3,
        out_specs=[pl.BlockSpec(memory_space=pltpu.VMEM)] * 2,
        scratch_shapes=[pltpu.VMEM(((n - KEEP) * FRAME_ROWS, 128), F32)],
        out_shape=[
            jax.ShapeDtypeStruct((n, FRAME_ROWS, 128), F32),
            jax.ShapeDtypeStruct((GROUP, (n - KEEP) * FRAME_ROWS, 128), F32),
        ],
        name="pack",
    )(count, window_of, jnp.transpose(positions, (1, 0, 2)), species, neighbours)


def run_deal(me, sent):
    return pl.pallas_call(
        deal_kernel,
        grid=(1,),
        in_specs=[SMEM_SPEC, pl.BlockSpec((GROUP, 8, 128), lambda i: (0, ROW_META // 8, 0))],
        out_specs=whole_spec((GROUP, 128)),
        out_shape=jax.ShapeDtypeStruct((GROUP, 128), jnp.int32),
        name="deal",
    )(me, sent)


def run_first(theta, own):
    n = own.shape[0]
    held = WEIGHTS + SPARE
    out = pl.pallas_call(
        first_kernel,
        grid=(1,),
        in_specs=[whole_spec((ROWS, 128)), whole_spec((1, FRAME_ROWS, 128))],
        out_specs=[whole_spec(s) for s, _ in held] + [whole_spec((1,) + s) for s, _ in SAVED] + [whole_spec(TALLY.shape)],
        scratch_shapes=FRAME_SCRATCH + [pltpu.VMEM((128, 128), F32)],
        out_shape=[jax.ShapeDtypeStruct(s, t) for s, t in held]
        + [jax.ShapeDtypeStruct((n,) + s, t) for s, t in SAVED]
        + [TALLY],
        compiler_params=LIMIT,
        cost_estimate=pl.CostEstimate(flops=10**9, bytes_accessed=4 * 10**7, transcendentals=10**6),
        name="first_frame",
    )(theta, own)
    return out[:N_WEIGHTS], out[N_WEIGHTS : N_WEIGHTS + 2], out[N_WEIGHTS + 2 : -1], out[-1]


def run_rest(plan, own, others, tally, weights, saved):
    n = own.shape[0]

    def own_index(i, plan):
        return (jnp.minimum(i + 1, plan[PLAN_OWN, 0] - 1), 0, 0)

    def other_index(i, plan):
        return (plan[jnp.maximum(i + 1 - plan[PLAN_OWN, 0], 0), 0], 0, 0)

    def saved_spec(shape):
        def index(i, plan):
            return (jnp.maximum(jnp.minimum(i + 1, plan[PLAN_COUNT, 0] - 1), 1),) + (0,) * len(shape)

        return pl.BlockSpec((1,) + shape, index)

    frame = (1, FRAME_ROWS, 128)
    first_saved = 4 + N_WEIGHTS
    out = pl.pallas_call(
        rest_kernel,
        grid_spec=pltpu.PrefetchScalarGridSpec(
            num_scalar_prefetch=1,
            grid=(n - 1,),
            in_specs=[pl.BlockSpec(frame, own_index), pl.BlockSpec(frame, other_index), whole_spec(TALLY.shape)]
            + [whole_spec(s) for s, _ in WEIGHTS]
            + [pl.BlockSpec(memory_space=pl.ANY)] * N_SAVED,
            out_specs=[saved_spec(s) for s, _ in SAVED] + [whole_spec(TALLY.shape)],
            scratch_shapes=FRAME_SCRATCH,
        ),
        out_shape=[jax.ShapeDtypeStruct((n,) + s, t) for s, t in SAVED] + [TALLY],
        input_output_aliases={first_saved + k: k for k in range(N_SAVED)},
        compiler_params=LIMIT,
        name="other_frames",
    )(plan, own, others, tally, *weights, *saved)
    return out[:-1], out[-1]


def run_backward(plan, core, parts, saved, spare):
    n = saved[0].shape[0]

    def saved_spec(shape):
        return pl.BlockSpec((1,) + shape, lambda i, plan: (jnp.minimum(i, plan[PLAN_COUNT, 0] - 1),) + (0,) * len(shape))

    half = (ROWS // 2, 128)
    return pl.pallas_call(
        backward_kernel,
        grid_spec=pltpu.PrefetchScalarGridSpec(
            num_scalar_prefetch=1,
            grid=(n,),
            in_specs=[SMEM_SPEC, whole_spec(parts.shape)]
            + [saved_spec(s) for s, _ in SAVED]
            + [whole_spec(s) for s, _ in SPARE],
            out_specs=[whole_spec(half), whole_spec(half), whole_spec(TALLY.shape)],
            scratch_shapes=[
                pltpu.VMEM((ROWS, 128), F32),
                pltpu.VMEM((2, 8, 128), F32),
                pltpu.VMEM((LAYERS, C, 3 * C), F32),
                pltpu.VMEM((LAYERS, C, C), F32),
                pltpu.VMEM((LAYERS, C, HID), F32),
                pltpu.VMEM((LAYERS, HID, HID), F32),
                pltpu.VMEM((LAYERS, HID, 2 * NB), F32),
                pltpu.VMEM((LAYERS, 8, C), F32),
                pltpu.VMEM((RO, C), F32),
                pltpu.VMEM((8, RO), F32),
                pltpu.VMEM((C, 16), F32),
                pltpu.VMEM((128, 128), F32),
            ],
        ),
        out_shape=[jax.ShapeDtypeStruct(half, F32), jax.ShapeDtypeStruct(half, F32), TALLY],
        compiler_params=LIMIT,
        name="backward",
    )(plan, core, parts, *saved, *spare)


def adam_step(params, first_moment, second_moment, unit):
    new_first = 0.9 * first_moment + 0.1 * unit
    new_second = 0.999 * second_moment + 0.001 * unit * unit
    unbiased_first = new_first / (1.0 - 0.9**10)
    unbiased_second = new_second / (1.0 - 0.999**10)
    new_params = params - 0.01 * unbiased_first / (jnp.sqrt(unbiased_second) + 1e-08)
    return (new_params, new_first, new_second)


AXES = {"x": 4, "y": 4, "z": 8, "core": 2}
PLANE = ("x", "y")
CHIPS = 128
DEPTH = 8


def swap_cores(v):
    return lax.ppermute(v, "core", [(0, 1), (1, 0)])


def gather_tallies(v):
    v = v[:1]
    v = v + swap_cores(v)
    return lax.all_to_all(jnp.broadcast_to(v, (CHIPS, 128)), PLANE + ("z",), 0, 0, tiled=True)


def to_all(v, axes, size):
    return lax.all_to_all(jnp.broadcast_to(v[None], (size,) + v.shape), axes, 0, 0, tiled=True)


def sum_large(mine, other, core):
    half = mine.shape[0]
    piece = half // GROUP
    own = mine + swap_cores(other)
    own = jnp.sum(lax.all_to_all(own.reshape(GROUP, piece, 128), PLANE, 0, 0, tiled=True), axis=0)
    own = jnp.sum(to_all(own, "z", DEPTH), axis=0)
    own = to_all(own, PLANE, GROUP).reshape(half, 128)
    other = swap_cores(own)
    first = core == 0
    return jnp.concatenate([jnp.where(first, own, other), jnp.where(first, other, own)], axis=0)


def on_device(
    params, first_moment, second_moment, positions, species, neighbours, window_of, frame_count
):
    n = positions.shape[0]
    core = lax.axis_index("core")
    own, send = run_pack(frame_count, window_of, positions, species, neighbours)
    sent = lax.all_to_all(send, PLANE, 0, 0, tiled=True)
    theta = jnp.pad(params, (0, ROWS * 128 - NPAR)).reshape(ROWS, 128)
    weights, spare, saved, tally = run_first(theta, own)
    plan = run_deal(lax.axis_index(PLANE)[None], sent)
    others = sent.reshape(GROUP * (n - KEEP), FRAME_ROWS, 128)
    saved, tally = run_rest(plan, own, others, tally, weights, saved)
    mine, other, means = run_backward(plan, core[None], gather_tallies(tally), saved, spare)
    summed = sum_large(mine, other, core).reshape(-1)[:NPAR]
    norm = jnp.sqrt(jnp.sum(summed * summed))
    unit = summed * (GRAD_SCALE * math.sqrt(NPAR) / (norm + 1e-06))
    new_params, new_first, new_second = adam_step(params, first_moment, second_moment, unit)
    return (new_params, new_first, new_second, means[0, :WINDOWS])


def solution(mesh):
    axes = tuple(AXES)
    split = Mesh(mesh.devices.reshape(tuple(AXES.values())), axes)
    in_specs = (
        P(),
        P(),
        P(),
        P(axes, None, None),
        P(axes, None),
        P(axes, None, None),
        P(axes),
        P(axes),
    )
    out_specs = (P(), P(), P(), P())
    return jax.shard_map(
        on_device, mesh=split, in_specs=in_specs, out_specs=out_specs, check_vma=False
    )
```

time: 2070 us -> 154 us (0.07); the launches traced: 2050 us -> 153 us
  waiting for transfers between devices: 885 us -> 13.5 us
  local copies, waits for them, and re-layouts: 344 us -> 6.03 us
  blocking collectives: 289 us -> 35.3 us
  matrix products: 249 us -> 0 us
  other arithmetic: 231 us -> 4.14 us
  Pallas kernels: 0 us -> 65.5 us
  loops' own time: 34.2 us -> 0 us
  starting transfers between devices: 0.04 us -> 26.4 us
    psum x1 -> x0, waiting for transfers between devices: 885 us -> none  [on_device(): summed = lax.psum(grad, ('dp', 'shard'))]
    psum x1 -> x0, blocking collectives: 289 us -> none  [on_device(): lax.psum((jnp.sum(onehot, axis=0), local_sums), ('dp', 'shard'))]
    dot_general x356 -> x0, matrix products: 249 us -> none  [mult(): jnp.dot(left, right, precision=lax.Precision.HIGHEST, preferred_element_t...]
    gather x56 -> x0, local copies, waits for them, and re-layouts: 224 us -> none  [the longest x48 180 us: frame_energy(): carried = jnp.take(lifted, partner, axis=1)]
    scatter-add x12 -> x0, other arithmetic: 146 us -> none  [frame_energy(): carried = jnp.take(lifted, partner, axis=1)]
    pallas_call x0 -> x5, Pallas kernels: none -> 65.5 us  [the longest x1 29.9 us: run_rest(): pl.pallas_call(rest_kernel, grid_spec=pltpu.PrefetchScalarGridSpec(num_sc...]
    while x541 -> x0, local copies, waits for them, and re-layouts: 50.1 us -> none
    mul x93 -> x0, other arithmetic: 48.1 us -> none  [the longest x8 22.2 us: frame_energy(): message = radial * carried * factor[None, :]]
  transfers between devices with their start and end apart: 1 -> 5, of which waited for: 1 -> 4; matrix products, arithmetic and copies ran while one was open for 0% -> 2% of each run, Pallas kernels for 0% -> 8%
where the time goes in v2:
time: 154 us; the launch traced here: 153 us
  Pallas kernels  65.5 us (43%)
  blocking collectives  35.3 us (23%)
  starting transfers between devices  26.4 us (17%)
  waiting for transfers between devices  13.5 us (9%)
  local copies, waits for them, and re-layouts  6.03 us (4%)
  other arithmetic  4.14 us (3%)
  between operations  2.14 us (1%)
    pallas_call x1, Pallas kernels, run_rest(): pl.pallas_call(rest_kernel, grid_spec=pltpu.PrefetchScalarGridSpec(num_sc...  29.9 us
    all_to_all x2, blocking collectives, to_all(): lax.all_to_all(jnp.broadcast_to(v[None], (size,) + v.shape), axes, 0, 0,...  23.4 us
    pallas_call x1, Pallas kernels, run_backward(): pl.pallas_call(backward_kernel, grid_spec=pltpu.PrefetchScalarGridSpec(nu...  20.3 us
    all_to_all x1, starting transfers between devices, gather_tallies(): lax.all_to_all(jnp.broadcast_to(v, (CHIPS, 128)), PLANE + ('z',), 0, 0, t...  14.7 us
    all_to_all x1, blocking collectives, sum_large(): lax.all_to_all(own.reshape(GROUP, piece, 128), PLANE, 0, 0, tiled=True)  11.9 us
    pallas_call x1, Pallas kernels, run_first(): pl.pallas_call(first_kernel, grid=(1,), in_specs=[whole_spec((ROWS, 128))...  11.6 us
    all_to_all x1, waiting for transfers between devices, gather_tallies(): lax.all_to_all(jnp.broadcast_to(v, (CHIPS, 128)), PLANE + ('z',), 0, 0, t...  10.5 us
    all_to_all x1, starting transfers between devices, on_device(): sent = lax.all_to_all(send, PLANE, 0, 0, tiled=True)  7.58 us
  transfers between devices with their start and end apart: 5, of which 4 were waited for; matrix products, arithmetic and copies ran while one was open for 2% of the time, Pallas kernels for 8%

profile of v2, /device:TPU:1, one launch (start us, length us, event | category | flops | bytes accessed | tf_op | source)
XLA Modules:
  0.0 153.0 jit_solution(13902201341335575097)
XLA Ops:
  1.3 1.9 %pack.1 = (f32[8,24,128]{2,1,0:T(8,128)}, f32[16,96,128]{2,1,0:T(8,128)}) custom-call(s32[1]{0:T(128)S(6)} %copy.30.count_ref, s32[8]{0:T(128)} %window_ref.1, f32[3,8,128]{2,1,0:T(8,128)} %bitcast.21, s32[8,128]{1,0:T(8,128)} %spc_ref.1, s32[8,16,128]{2,1,0:T(8,128)} %nb_ref.1), custom_call_target="tpu_custom_call" | custom-call | tf_op jit(solution)/shard_map/pack/pallas_call | solution.py:557
  3.1 7.6 %all-to-all-start = ((f32[16,96,128]{2,1,0:T(8,128)}), f32[16,96,128]{2,1,0:T(8,128)S(1)}, u32[]{:S(2)}, u32[]{:S(2)}) async-start(f32[16,96,128]{2,1,0:T(8,128)} %get-tuple-element.43), calls=%async_computation | async-start | bytes 1572864 | tf_op jit(solution)/shard_map/all_to_all | solution.py:720
  10.7 2.0 %pad_bitcast_fusion.th_ref = f32[1280,128]{1,0:T(8,128)} fusion(f32[160272]{0:T(1024)} %param.8), kind=kLoop, calls=%fused_computation.2 | loop fusion | bytes 1296448 | tf_op jit(solution)/shard_map/reshape | solution.py:721
  12.7 11.6 %first_frame.1 = (bf16[2,64,48]{2,1,0:T(8,128)(2,1)}, bf16[2,64,192]{2,1,0:T(8,128)(2,1)}, bf16[2,128,192]{2,1,0:T(8,128)(2,1)}, bf16[2,128,384]{2,1,0:T(8,128)(...) custom-call(f32[1280,128]{1,0:T(8,128)} %pad_bitcast_fusion.th_ref, ...), custom_call_target="tpu_custom_call" | custom-call | flops 1000000000 | bytes 40000000 | tf_op jit(solution)/shard_map/first_frame/pallas_call | solution.py:584
  24.3 0.9 copy-done
  25.2 1.8 %deal.1.plan_ref = s32[16,128]{1,0:T(8,128)} custom-call(s32[1]{0:T(128)} %bitcast.me_ref, f32[16,96,128]{2,1,0:T(8,128)} %copy-done), custom_call_target="tpu_custom_call" | custom-call | tf_op jit(solution)/shard_map/deal/pallas_call | solution.py:571
  27.0 29.9 %other_frames.1 = (f32[8,8,128]{2,1,0:T(8,128)}, bf16[8,16,1920]{2,1,0:T(8,128)(2,1)}, f32[8,3,16,128]{3,2,1,0:T(8,128)}, bf16[8,2,2,64,1920]{4,3,2,1,0:T(8,128)...) custom-call(s32[16,128]{1,0:T(8,128)} %deal.1.plan_ref, ...), custom_call_target="tpu_custom_call", output_to_operand_aliasing={{0}: (16, {}), {1}: (17, {}), {2}: (18, {}), {3}: (19, {}),... | custom-call | tf_op jit(solution)/shard_map/other_frames/pallas_call | solution.py:617
  56.9 0.7 slice.9
  57.6 1.1 collective-permute-done
  58.7 0.7 add_bitcast_fusion
  59.4 0.7 broadcast_in_dim.12
  60.1 14.7 %all-to-all-start.1 = ((f32[128,1,128]{2,1,0:T(1,128)}), f32[128,1,128]{2,1,0:T(1,128)S(1)}, u32[]{:S(2)}, u32[]{:S(2)}) async-start(f32[128,1,128]{2,1,0:T(1,128)} %broadcast_in_dim.12), calls=%async_computation.1 | async-start | bytes 131072 | tf_op jit(solution)/shard_map/all_to_all | solution.py:695
  74.8 10.5 %all-to-all-done.1 = f32[128,1,128]{2,1,0:T(1,128)S(1)} async-done(((f32[128,1,128]{2,1,0:T(1,128)}), f32[128,1,128]{2,1,0:T(1,128)S(1)}, u32[]{:S(2)}, u32[]{:S(2)}) %all-to-all-start.1) | async-done | bytes 65568 | tf_op jit(solution)/shard_map/all_to_all | solution.py:695
  85.3 0.6 copy-done.4
  85.9 20.3 %backward.1 = (f32[640,128]{1,0:T(8,128)}, f32[640,128]{1,0:T(8,128)}, f32[8,128]{1,0:T(8,128)}) custom-call(s32[16,128]{1,0:T(8,128)} %deal.1.plan_ref, s32[1]{0:T(128)} %bitcast.2.core_ref, f32[128,128]{1,0:T(8,128)} %bitcast.20, f32[8,8,128]{2,1,0:T(8,128)} %get-tuple-element.68.deriv_ref, bf16[8,16,1920]{2,1,0:T(8,128)(2,1)} %get-tuple-element.69.basis_ref, ...), custom_call_target="tpu_custom_call" | custom-call | tf_op jit(solution)/shard_map/backward/pallas_call | solution.py:643
  106.3 1.8 %collective-permute-done.1 = f32[640,128]{1,0:T(8,128)S(1)} collective-permute-done((f32[640,128]{1,0:T(8,128)}, f32[640,128]{1,0:T(8,128)S(1)}, u32[]{:S(2)}, u32[]{:S(2)}) %collective-permute-start.1) | collective-permute-done | bytes 327712 | tf_op jit(solution)/shard_map/ppermute | solution.py:689
  108.1 1.0 add.31
  109.1 11.9 %all_to_all.28 = f32[16,40,128]{2,1,0:T(8,128)S(1)} all-to-all(f32[16,40,128]{2,1,0:T(8,128)S(1)} %bitcast.19), channel_id=1, replica_groups=mesh['x'=4,'y'=4,'z'=8,'core'=2] {'x','y'}, dimensions={0} | all-to-all | bytes 655360 | tf_op jit(solution)/shard_map/all_to_all | solution.py:706
  121.1 12.1 %all_to_all.29 = f32[8,40,128]{2,1,0:T(8,128)S(1)} all-to-all(f32[8,40,128]{2,1,0:T(8,128)S(1)} %broadcast_in_dim.26), channel_id=1, replica_groups=mesh['x'=4,'y'=4,'z'=8,'core'=2] {'z'}, dimensions={0} | all-to-all | bytes 327680 | tf_op jit(solution)/shard_map/all_to_all | solution.py:699
  133.3 11.3 %all_to_all.30 = f32[16,40,128]{2,1,0:T(8,128)S(1)} all-to-all(f32[16,40,128]{2,1,0:T(8,128)S(1)} %broadcast_in_dim.27), channel_id=1, replica_groups=mesh['x'=4,'y'=4,'z'=8,'core'=2] {'x','y'}, dimensions={0} | all-to-all | bytes 655360 | tf_op jit(solution)/shard_map/all_to_all | solution.py:699
  144.6 4.0 %collective-permute-start.2 = (f32[640,128]{1,0:T(8,128)S(1)}, f32[640,128]{1,0:T(8,128)S(1)}, u32[]{:S(2)}, u32[]{:S(2)}) collective-permute-start(f32[640,128]{1,0:T(8,128)S(1)} %bitcast.18), channel_id=1, source_target_pairs={{0,1},{1,0},{2,3},{3,2},{4,5},{5,4},{6,7},{7,6},{8,9},{9,8},{10,11... | collective-permute-start | bytes 983048 | tf_op jit(solution)/shard_map/ppermute | solution.py:689
  148.6 1.2 slice_bitcast_fusion
  149.9 0.8 multiply_reduce_fusion
  151.5 1.5 %divide_subtract_fusion = (f32[160272]{0:T(1024)}, f32[160272]{0:T(1024)}, f32[160272]{0:T(1024)}) fusion(f32[160272]{0:T(1024)S(1)} %copy-done.1, f32[]{:T(128)S(6)} %div.14, f32[163840]{0:T(1024)S(1)} %maximum_bitcast_fusion, f32[160272]{0:T(1024)S(1)} %copy-done.2, f32[160272]{0:T(1024)S(1)} %copy-done.3), kind=kLoop, calls=%fused_computation.4 | loop fusion | flops 2083536 | bytes 4487620 | tf_op jit(solution)/shard_map/sub | solution.py:678
  (18 shorter events, 0.3 us)
Async XLA Ops:
  3.1 21.2 %all-to-all-start = ((f32[16,96,128]{2,1,0:T(8,128)}), f32[16,96,128]{2,1,0:T(8,128)S(1)}, u32[]{:S(2)}, u32[]{:S(2)}) async-start(f32[16,96,128]{2,1,0:T(8,128)} %get-tuple-element.43), calls=%async_computation | async-start | bytes 1572864 | tf_op jit(solution)/shard_map/all_to_all | solution.py:720
  24.3 0.9 copy-start
  57.6 1.1 collective-permute-start
  60.1 25.2 %all-to-all-start.1 = ((f32[128,1,128]{2,1,0:T(1,128)}), f32[128,1,128]{2,1,0:T(1,128)S(1)}, u32[]{:S(2)}, u32[]{:S(2)}) async-start(f32[128,1,128]{2,1,0:T(1,128)} %broadcast_in_dim.12), calls=%async_computation.1 | async-start | bytes 131072 | tf_op jit(solution)/shard_map/all_to_all | solution.py:695
  85.3 0.6 copy-start.4
  85.9 65.5 %copy-start.1 = (f32[160272]{0:T(1024)S(1)}, f32[160272]{0:T(1024)}, u32[]{:S(2)}) copy-start(f32[160272]{0:T(1024)} %param.8) | copy-start | bytes 1923268
  85.9 65.5 %copy-start.2 = (f32[160272]{0:T(1024)S(1)}, f32[160272]{0:T(1024)}, u32[]{:S(2)}) copy-start(f32[160272]{0:T(1024)} %param.9) | copy-start | bytes 1923268
  85.9 65.6 %copy-start.3 = (f32[160272]{0:T(1024)S(1)}, f32[160272]{0:T(1024)}, u32[]{:S(2)}) copy-start(f32[160272]{0:T(1024)} %param.10) | copy-start | bytes 1923268
  106.2 1.9 %collective-permute-start.1 = (f32[640,128]{1,0:T(8,128)}, f32[640,128]{1,0:T(8,128)S(1)}, u32[]{:S(2)}, u32[]{:S(2)}) collective-permute-start(f32[640,128]{1,0:T(8,128)} %get-tuple-element.80), channel_id=1, source_target_pairs={{0,1},{1,0},{2,3},{3,2},{4,5},{5,4},{6,7},{7,6},{8,9},{9,8},{10,11... | collective-permute-start | bytes 983048 | tf_op jit(solution)/shard_map/ppermute | solution.py:689
  144.6 5.2 %collective-permute-start.2 = (f32[640,128]{1,0:T(8,128)S(1)}, f32[640,128]{1,0:T(8,128)S(1)}, u32[]{:S(2)}, u32[]{:S(2)}) collective-permute-start(f32[640,128]{1,0:T(8,128)S(1)} %bitcast.18), channel_id=1, source_target_pairs={{0,1},{1,0},{2,3},{3,2},{4,5},{5,4},{6,7},{7,6},{8,9},{9,8},{10,11... | collective-permute-start | bytes 983048 | tf_op jit(solution)/shard_map/ppermute | solution.py:689

commit v3 on v2

--- a/solution.py
+++ b/solution.py
@@ -37,10 +37,17 @@
 
 ROW_POS, ROW_SPECIES, ROW_META, FRAME_ROWS = SLOTS, SLOTS + 3, SLOTS + 4, 24
 KEEP = 4
-GROUP = 16
+GROUP = 32
+PLAN_ROWS = 16
 PLAN_COUNT, PLAN_OWN = 8, 9
 
-CHUNKS = ((0, 4), (4, 8), (8, 12), (12, 15))
+AXES = {"x": 4, "y": 4, "z": 8, "core": 2}
+PLANE = ("x", "y")
+PLANE_CHIPS = 16
+CHIPS = 128
+DEPTH = 8
+
+CHUNKS = ((0, SLOTS),)
 F32, BF16 = jnp.float32, jnp.bfloat16
 
 N_H0, N_P0, N_CH1, N_CL0, N_CP0, N_H1, N_P1, N_CH2, N_CL1, N_CP1, N_H2, N_CH0 = range(12)
@@ -342,15 +349,17 @@
     for f in range(KEEP, n):
         wide_s[(f - KEEP) * FRAME_ROWS : (f - KEEP + 1) * FRAME_ROWS, :] = own_ref[f]
     wide = wide_s[...]
-    for g in range(GROUP):
+    for g in range(PLANE_CHIPS):
         send_ref[g] = wide
 
 
-def deal_kernel(me_ref, rows_ref, plan_ref):
+def deal_kernel(me_ref, here_ref, there_ref, plan_ref):
     n = 8
     lane = lax.broadcasted_iota(jnp.int32, (GROUP, 128), 1)
     gid = lax.broadcasted_iota(jnp.int32, (GROUP, 128), 0)
-    meta = rows_ref[:, ROW_META % 8, :]
+    core = me_ref[0] // PLANE_CHIPS
+    here, there = here_ref[:, ROW_META % 8, :], there_ref[:, ROW_META % 8, :]
+    meta = jnp.concatenate([jnp.where(core == 0, here, there), jnp.where(core == 0, there, here)], axis=0)
     counts = jnp.broadcast_to(jnp.sum(jnp.where(lane == 1, meta, 0.0), axis=1, keepdims=True), (GROUP, 128))
     base = jnp.minimum(counts, float(KEEP))
     surplus = counts - base
@@ -373,14 +382,16 @@
     mine = jnp.sum(jnp.where(gid == me, base + taken, 0.0), axis=0, keepdims=True)
     held = jnp.sum(jnp.where(gid == me, base, 0.0), axis=0, keepdims=True)
     order = jnp.where(lane_f < surplus, offset + lane_f, -1.0)
-    place = (gid * (n - KEEP) + lane).astype(F32)
+    place = ((gid % PLANE_CHIPS) * (n - KEEP) + lane).astype(F32)
+    away = jnp.where(gid // PLANE_CHIPS == core, 0.0, 1.0)
     for j in range(n):
-        hit = jnp.where(order == start + float(j), place, 0.0)
-        one = jnp.sum(jnp.sum(hit, axis=0, keepdims=True), axis=1, keepdims=True)
-        plan_ref[j : j + 1, :] = jnp.broadcast_to(one, (1, 128)).astype(jnp.int32)
+        hit = order == start + float(j)
+        one = jnp.sum(jnp.sum(jnp.where(hit, place, 0.0), axis=0, keepdims=True), axis=1, keepdims=True)
+        two = jnp.sum(jnp.sum(jnp.where(hit, away, 0.0), axis=0, keepdims=True), axis=1, keepdims=True)
+        plan_ref[j : j + 1, :] = jnp.where(lane[:1] == 0, one, two).astype(jnp.int32)
     plan_ref[n : n + 1, :] = mine.astype(jnp.int32)
     plan_ref[n + 1 : n + 2, :] = held.astype(jnp.int32)
-    plan_ref[n + 2 :, :] = jnp.zeros((GROUP - n - 2, 128), jnp.int32)
+    plan_ref[n + 2 :, :] = jnp.zeros((PLAN_ROWS - n - 2, 128), jnp.int32)
 
 
 def first_kernel(th_ref, own_ref, *refs):
@@ -391,24 +402,30 @@
     tally_ref[...] = run_frame(own_ref[0], *weights, *saved, oh_s, rad_s, dist_s)
 
 
-def rest_kernel(plan_ref, own_ref, other_ref, first_ref, *refs):
+def rest_kernel(plan_ref, own_ref, here_ref, there_ref, first_ref, *refs):
     weights = refs[:N_WEIGHTS]
     saved = refs[N_WEIGHTS + N_SAVED : N_WEIGHTS + 2 * N_SAVED]
-    tally_ref, oh_s, rad_s, dist_s = refs[N_WEIGHTS + 2 * N_SAVED :]
+    tally_ref, oh_s, rad_s, dist_s, sum_s = refs[N_WEIGHTS + 2 * N_SAVED :]
     step = pl.program_id(0)
 
     @pl.when(step == 0)
     def _():
-        tally_ref[...] = first_ref[...]
+        sum_s[...] = first_ref[...]
 
     @pl.when(step + 1 < plan_ref[PLAN_COUNT, 0])
     def _():
-        x = jnp.where(step + 1 < plan_ref[PLAN_OWN, 0], own_ref[0], other_ref[0])
-        tally_ref[...] += run_frame(x, *weights, *saved, oh_s, rad_s, dist_s)
+        own = plan_ref[PLAN_OWN, 0]
+        away = plan_ref[jnp.maximum(step + 1 - own, 0), 1]
+        x = jnp.where(step + 1 < own, own_ref[0], jnp.where(away == 0, here_ref[0], there_ref[0]))
+        sum_s[...] += run_frame(x, *weights, *saved, oh_s, rad_s, dist_s)
+
+    @pl.when(step == pl.num_programs(0) - 1)
+    def _():
+        tally_ref[...] = jnp.broadcast_to(sum_s[:1, :], (CHIPS, 128))
 
 
 def backward_kernel(
-    plan_ref, core_ref, parts_ref, deriv_ref, basis_ref, fac_ref, act_ref, slope_ref, first_ref, gath_ref, node_ref, head_ref, w3t_ref, w2t_ref,
+    plan_ref, core_ref, parts_ref, more_ref, deriv_ref, basis_ref, fac_ref, act_ref, slope_ref, first_ref, gath_ref, node_ref, head_ref, w3t_ref, w2t_ref,
     mine_ref, other_ref, means_ref,
     grad_ref, window_s, mix_a, up_a, w3_a, w2_a, w1_a, read_a, head_a, out_a, emb_a, tmp_s,
 ):
@@ -418,7 +435,7 @@
     def _():
         for ref in (mix_a, up_a, w3_a, w2_a, w1_a, read_a, head_a, out_a, emb_a):
             ref[...] = jnp.zeros(ref.shape, F32)
-        total = jnp.broadcast_to(jnp.sum(parts_ref[...], axis=0, keepdims=True), (8, 128))
+        total = jnp.broadcast_to(jnp.sum(parts_ref[...] + more_ref[...], axis=0, keepdims=True), (8, 128))
         lane = lax.broadcasted_iota(jnp.int32, (8, 128), 1)
         sizes = jnp.maximum(total, 1.0)
         means = pltpu.roll(total, 128 - WINDOWS, 1) / sizes
@@ -561,21 +578,21 @@
         scratch_shapes=[pltpu.VMEM(((n - KEEP) * FRAME_ROWS, 128), F32)],
         out_shape=[
             jax.ShapeDtypeStruct((n, FRAME_ROWS, 128), F32),
-            jax.ShapeDtypeStruct((GROUP, (n - KEEP) * FRAME_ROWS, 128), F32),
+            jax.ShapeDtypeStruct((PLANE_CHIPS, (n - KEEP) * FRAME_ROWS, 128), F32),
         ],
         name="pack",
     )(count, window_of, jnp.transpose(positions, (1, 0, 2)), species, neighbours)
 
 
-def run_deal(me, sent):
+def run_deal(me, here, there):
     return pl.pallas_call(
         deal_kernel,
         grid=(1,),
-        in_specs=[SMEM_SPEC, pl.BlockSpec((GROUP, 8, 128), lambda i: (0, ROW_META // 8, 0))],
-        out_specs=whole_spec((GROUP, 128)),
-        out_shape=jax.ShapeDtypeStruct((GROUP, 128), jnp.int32),
+        in_specs=[SMEM_SPEC] + [pl.BlockSpec((PLANE_CHIPS, 8, 128), lambda i: (0, ROW_META // 8, 0))] * 2,
+        out_specs=whole_spec((PLAN_ROWS, 128)),
+        out_shape=jax.ShapeDtypeStruct((PLAN_ROWS, 128), jnp.int32),
         name="deal",
-    )(me, sent)
+    )(me, here, there)
 
 
 def run_first(theta, own):
@@ -597,7 +614,7 @@
     return out[:N_WEIGHTS], out[N_WEIGHTS : N_WEIGHTS + 2], out[N_WEIGHTS + 2 : -1], out[-1]
 
 
-def run_rest(plan, own, others, tally, weights, saved):
+def run_rest(plan, own, here, there, tally, weights, saved):
     n = own.shape[0]
 
     def own_index(i, plan):
@@ -613,27 +630,28 @@
         return pl.BlockSpec((1,) + shape, index)
 
     frame = (1, FRAME_ROWS, 128)
-    first_saved = 4 + N_WEIGHTS
+    first_saved = 5 + N_WEIGHTS
     out = pl.pallas_call(
         rest_kernel,
         grid_spec=pltpu.PrefetchScalarGridSpec(
             num_scalar_prefetch=1,
             grid=(n - 1,),
-            in_specs=[pl.BlockSpec(frame, own_index), pl.BlockSpec(frame, other_index), whole_spec(TALLY.shape)]
+            in_specs=[pl.BlockSpec(frame, own_index), pl.BlockSpec(frame, other_index), pl.BlockSpec(frame, other_index)]
+            + [whole_spec(TALLY.shape)]
             + [whole_spec(s) for s, _ in WEIGHTS]
             + [pl.BlockSpec(memory_space=pl.ANY)] * N_SAVED,
-            out_specs=[saved_spec(s) for s, _ in SAVED] + [whole_spec(TALLY.shape)],
-            scratch_shapes=FRAME_SCRATCH,
+            out_specs=[saved_spec(s) for s, _ in SAVED] + [whole_spec((CHIPS, 128))],
+            scratch_shapes=FRAME_SCRATCH + [pltpu.VMEM(TALLY.shape, F32)],
         ),
-        out_shape=[jax.ShapeDtypeStruct((n,) + s, t) for s, t in SAVED] + [TALLY],
+        out_shape=[jax.ShapeDtypeStruct((n,) + s, t) for s, t in SAVED] + [jax.ShapeDtypeStruct((CHIPS, 128), F32)],
         input_output_aliases={first_saved + k: k for k in range(N_SAVED)},
         compiler_params=LIMIT,
         name="other_frames",
-    )(plan, own, others, tally, *weights, *saved)
+    )(plan, own, here, there, tally, *weights, *saved)
     return out[:-1], out[-1]
 
 
-def run_backward(plan, core, parts, saved, spare):
+def run_backward(plan, core, parts, more, saved, spare):
     n = saved[0].shape[0]
 
     def saved_spec(shape):
@@ -645,7 +663,7 @@
         grid_spec=pltpu.PrefetchScalarGridSpec(
             num_scalar_prefetch=1,
             grid=(n,),
-            in_specs=[SMEM_SPEC, whole_spec(parts.shape)]
+            in_specs=[SMEM_SPEC, whole_spec(parts.shape), whole_spec(parts.shape)]
             + [saved_spec(s) for s, _ in SAVED]
             + [whole_spec(s) for s, _ in SPARE],
             out_specs=[whole_spec(half), whole_spec(half), whole_spec(TALLY.shape)],
@@ -667,7 +685,7 @@
         out_shape=[jax.ShapeDtypeStruct(half, F32), jax.ShapeDtypeStruct(half, F32), TALLY],
         compiler_params=LIMIT,
         name="backward",
-    )(plan, core, parts, *saved, *spare)
+    )(plan, core, parts, more, *saved, *spare)
 
 
 def adam_step(params, first_moment, second_moment, unit):
@@ -679,20 +697,13 @@
     return (new_params, new_first, new_second)
 
 
-AXES = {"x": 4, "y": 4, "z": 8, "core": 2}
-PLANE = ("x", "y")
-CHIPS = 128
-DEPTH = 8
-
-
 def swap_cores(v):
     return lax.ppermute(v, "core", [(0, 1), (1, 0)])
 
 
 def gather_tallies(v):
-    v = v[:1]
-    v = v + swap_cores(v)
-    return lax.all_to_all(jnp.broadcast_to(v, (CHIPS, 128)), PLANE + ("z",), 0, 0, tiled=True)
+    own = lax.all_to_all(v, PLANE + ("z",), 0, 0, tiled=True)
+    return own, swap_cores(own)
 
 
 def to_all(v, axes, size):
@@ -701,11 +712,11 @@
 
 def sum_large(mine, other, core):
     half = mine.shape[0]
-    piece = half // GROUP
+    piece = half // PLANE_CHIPS
     own = mine + swap_cores(other)
-    own = jnp.sum(lax.all_to_all(own.reshape(GROUP, piece, 128), PLANE, 0, 0, tiled=True), axis=0)
+    own = jnp.sum(lax.all_to_all(own.reshape(PLANE_CHIPS, piece, 128), PLANE, 0, 0, tiled=True), axis=0)
     own = jnp.sum(to_all(own, "z", DEPTH), axis=0)
-    own = to_all(own, PLANE, GROUP).reshape(half, 128)
+    own = to_all(own, PLANE, PLANE_CHIPS).reshape(half, 128)
     other = swap_cores(own)
     first = core == 0
     return jnp.concatenate([jnp.where(first, own, other), jnp.where(first, other, own)], axis=0)
@@ -717,13 +728,15 @@
     n = positions.shape[0]
     core = lax.axis_index("core")
     own, send = run_pack(frame_count, window_of, positions, species, neighbours)
-    sent = lax.all_to_all(send, PLANE, 0, 0, tiled=True)
+    here = lax.all_to_all(send, PLANE, 0, 0, tiled=True)
     theta = jnp.pad(params, (0, ROWS * 128 - NPAR)).reshape(ROWS, 128)
     weights, spare, saved, tally = run_first(theta, own)
-    plan = run_deal(lax.axis_index(PLANE)[None], sent)
-    others = sent.reshape(GROUP * (n - KEEP), FRAME_ROWS, 128)
-    saved, tally = run_rest(plan, own, others, tally, weights, saved)
-    mine, other, means = run_backward(plan, core[None], gather_tallies(tally), saved, spare)
+    here, tally = lax.optimization_barrier((here, tally))
+    there = swap_cores(here)
+    plan = run_deal((core * PLANE_CHIPS + lax.axis_index(PLANE))[None], here, there)
+    here, there = (v.reshape(PLANE_CHIPS * (n - KEEP), FRAME_ROWS, 128) for v in (here, there))
+    saved, tally = run_rest(plan, own, here, there, tally, weights, saved)
+    mine, other, means = run_backward(plan, core[None], *gather_tallies(tally), saved, spare)
     summed = sum_large(mine, other, core).reshape(-1)[:NPAR]
     norm = jnp.sqrt(jnp.sum(summed * summed))
     unit = summed * (GRAD_SCALE * math.sqrt(NPAR) / (norm + 1e-06))

time: 154 us -> 143 us (0.929)
  blocking collectives: 35.3 us -> 56.6 us
  Pallas kernels: 65.5 us -> 53.3 us
  starting transfers between devices: 26.4 us -> 15.8 us
  waiting for transfers between devices: 13.5 us -> 5.68 us
    all_to_all x1 -> x2, blocking collectives: 11.9 us -> 34.3 us  [the longest x1 23.7 us: gather_tallies(): own = lax.all_to_all(v, PLANE + ('z',), 0, 0, tiled=True)]
    all_to_all x2 -> x1, starting transfers between devices: 22.3 us -> 7.58 us  [on_device(): here = lax.all_to_all(send, PLANE, 0, 0, tiled=True)]
    all_to_all x2 -> x1, waiting for transfers between devices: 10.5 us -> 0.98 us  [on_device(): here = lax.all_to_all(send, PLANE, 0, 0, tiled=True)]
    pallas_call x1, Pallas kernels: 29.9 us -> 23.7 us  [run_rest(): pl.pallas_call(rest_kernel, grid_spec=pltpu.PrefetchScalarGridSpec(num_sc...]
    pallas_call x1, Pallas kernels: 20.3 us -> 15.9 us  [run_backward(): pl.pallas_call(backward_kernel, grid_spec=pltpu.PrefetchScalarGridSpec(nu...]
    ppermute x3 -> x4, starting transfers between devices: 4.08 us -> 8.26 us  [swap_cores(): return lax.ppermute(v, 'core', [(0, 1), (1, 0)])]
    pallas_call x1, Pallas kernels: 11.6 us -> 9.84 us  [run_first(): pl.pallas_call(first_kernel, grid=(1,), in_specs=[whole_spec((ROWS, 128))...]
    ppermute x3 -> x4, waiting for transfers between devices: 3.02 us -> 4.7 us  [swap_cores(): return lax.ppermute(v, 'core', [(0, 1), (1, 0)])]
  transfers between devices with their start and end apart: 5 -> 5, of which waited for: 4 -> 5; matrix products, arithmetic and copies ran while one was open for 2% -> 2% of each run, Pallas kernels for 8% -> 7%
where the time goes in v3:
time: 143 us; the launch traced here: 142 us
  blocking collectives  56.6 us (40%)
  Pallas kernels  53.3 us (37%)
  starting transfers between devices  15.8 us (11%)
  waiting for transfers between devices  5.68 us (4%)
  local copies, waits for them, and re-layouts  4.69 us (3%)
  other arithmetic  3.46 us (2%)
  between operations  2.11 us (1%)
    pallas_call x1, Pallas kernels, run_rest(): pl.pallas_call(rest_kernel, grid_spec=pltpu.PrefetchScalarGridSpec(num_sc...  23.7 us
    all_to_all x1, blocking collectives, gather_tallies(): own = lax.all_to_all(v, PLANE + ('z',), 0, 0, tiled=True)  23.7 us
    all_to_all x2, blocking collectives, to_all(): lax.all_to_all(jnp.broadcast_to(v[None], (size,) + v.shape), axes, 0, 0,...  22.2 us
    pallas_call x1, Pallas kernels, run_backward(): pl.pallas_call(backward_kernel, grid_spec=pltpu.PrefetchScalarGridSpec(nu...  15.9 us
    all_to_all x1, blocking collectives, sum_large(): lax.all_to_all(own.reshape(PLANE_CHIPS, piece, 128), PLANE, 0, 0, tiled=T...  10.7 us
    pallas_call x1, Pallas kernels, run_first(): pl.pallas_call(first_kernel, grid=(1,), in_specs=[whole_spec((ROWS, 128))...  9.84 us
    ppermute x4, starting transfers between devices, swap_cores(): return lax.ppermute(v, 'core', [(0, 1), (1, 0)])  8.26 us
    all_to_all x1, starting transfers between devices, on_device(): here = lax.all_to_all(send, PLANE, 0, 0, tiled=True)  7.58 us
  transfers between devices with their start and end apart: 5, of which 5 were waited for; matrix products, arithmetic and copies ran while one was open for 2% of the time, Pallas kernels for 7%

profile of v3, /device:TPU:1, one launch (start us, length us, event | category | flops | bytes accessed | tf_op | source)
XLA Modules:
  0.0 141.6 jit_solution(161547038615028415)
XLA Ops:
  1.3 1.9 %pack.1 = (f32[8,24,128]{2,1,0:T(8,128)}, f32[16,96,128]{2,1,0:T(8,128)}) custom-call(s32[1]{0:T(128)S(6)} %copy.32.count_ref, s32[8]{0:T(128)} %window_ref.1, f32[3,8,128]{2,1,0:T(8,128)} %bitcast.26, s32[8,128]{1,0:T(8,128)} %spc_ref.1, s32[8,16,128]{2,1,0:T(8,128)} %nb_ref.1), custom_call_target="tpu_custom_call" | custom-call | tf_op jit(solution)/shard_map/pack/pallas_call | solution.py:574
  3.1 7.6 %all-to-all-start = ((f32[16,96,128]{2,1,0:T(8,128)}), f32[16,96,128]{2,1,0:T(8,128)S(1)}, u32[]{:S(2)}, u32[]{:S(2)}) async-start(f32[16,96,128]{2,1,0:T(8,128)} %get-tuple-element.45), calls=%async_computation | async-start | bytes 1572864 | tf_op jit(solution)/shard_map/all_to_all | solution.py:731
  10.7 2.0 %pad_bitcast_fusion.th_ref = f32[1280,128]{1,0:T(8,128)} fusion(f32[160272]{0:T(1024)} %param.8), kind=kLoop, calls=%fused_computation.2 | loop fusion | bytes 1296448 | tf_op jit(solution)/shard_map/reshape | solution.py:732
  12.7 9.8 %first_frame.1 = (bf16[2,64,48]{2,1,0:T(8,128)(2,1)}, bf16[2,64,192]{2,1,0:T(8,128)(2,1)}, bf16[2,128,192]{2,1,0:T(8,128)(2,1)}, bf16[2,128,384]{2,1,0:T(8,128)(...) custom-call(f32[1280,128]{1,0:T(8,128)} %pad_bitcast_fusion.th_ref, ...), custom_call_target="tpu_custom_call" | custom-call | flops 1000000000 | bytes 40000000 | tf_op jit(solution)/shard_map/first_frame/pallas_call | solution.py:601
  22.5 1.0 all-to-all-done.here_ref
  23.5 2.5 %collective-permute-start = (f32[16,96,128]{2,1,0:T(8,128)S(1)}, f32[16,96,128]{2,1,0:T(8,128)S(1)}, u32[]{:S(2)}, u32[]{:S(2)}) collective-permute-start(f32[16,96,128]{2,1,0:T(8,128)S(1)} %all-to-all-done.here_ref), channel_id=1, source_target_pairs={{0,1},{1,0},{2,3},{3,2},{4,5},{5,4},{6,7},{7,6},{8,9},{9,8},{10,11... | collective-permute-start | bytes 2359304 | tf_op jit(solution)/shard_map/ppermute | solution.py:701
  26.1 1.9 %collective-permute-done.there_ref = f32[16,96,128]{2,1,0:T(8,128)S(1)} collective-permute-done((f32[16,96,128]{2,1,0:T(8,128)S(1)}, f32[16,96,128]{2,1,0:T(8,128)S(1)}, u32[]{:S(2)}, u32[]{:S(2)}) %collective-permute-start) | collective-permute-done | bytes 786464 | tf_op jit(solution)/shard_map/ppermute | solution.py:701
  28.0 0.9 copy-done.1
  28.9 1.9 %deal.1.plan_ref = s32[16,128]{1,0:T(8,128)} custom-call(s32[1]{0:T(128)} %bitcast.me_ref, f32[16,96,128]{2,1,0:T(8,128)} %copy-done, f32[16,96,128]{2,1,0:T(8,128)} %copy-done.1), custom_call_target="tpu_custom_call" | custom-call | tf_op jit(solution)/shard_map/deal/pallas_call | solution.py:588
  30.8 23.7 %other_frames.1 = (f32[8,8,128]{2,1,0:T(8,128)}, bf16[8,16,1920]{2,1,0:T(8,128)(2,1)}, f32[8,3,16,128]{3,2,1,0:T(8,128)}, bf16[8,2,2,64,1920]{4,3,2,1,0:T(8,128)...) custom-call(s32[16,128]{1,0:T(8,128)} %deal.1.plan_ref, ...), custom_call_target="tpu_custom_call", output_to_operand_aliasing={{0}: (17, {}), {1}: (18, {}), {2}: (19, {}), {3}: (20, {}),... | custom-call | tf_op jit(solution)/shard_map/other_frames/pallas_call | solution.py:634
  54.5 23.7 %all_to_all.31 = f32[128,1,128]{2,1,0:T(1,128)S(1)} all-to-all(f32[128,1,128]{2,1,0:T(1,128)} %bitcast.25), channel_id=1, replica_groups=mesh['x'=4,'y'=4,'z'=8,'core'=2] {'x','y','z'}, dimensions={0} | all-to-all | bytes 131072 | tf_op jit(solution)/shard_map/all_to_all | solution.py:705
  78.2 1.7 %collective-permute-start.1 = (f32[128,128]{1,0:T(8,128)S(1)}, f32[128,128]{1,0:T(8,128)S(1)}, u32[]{:S(2)}, u32[]{:S(2)}) collective-permute-start(f32[128,128]{1,0:T(8,128)S(1)} %bitcast.23), channel_id=1, source_target_pairs={{0,1},{1,0},{2,3},{3,2},{4,5},{5,4},{6,7},{7,6},{8,9},{9,8},{10,11... | collective-permute-start | bytes 196616 | tf_op jit(solution)/shard_map/ppermute | solution.py:701
  79.8 0.9 collective-permute-done.1.more_ref
  80.7 0.6 copy-done.6
  81.3 15.9 %backward.1 = (f32[640,128]{1,0:T(8,128)}, f32[640,128]{1,0:T(8,128)}, f32[8,128]{1,0:T(8,128)}) custom-call(s32[16,128]{1,0:T(8,128)} %deal.1.plan_ref, s32[1]{0:T(128)} %bitcast.3.core_ref, f32[128,128]{1,0:T(8,128)} %bitcast.24, f32[128,128]{1,0:T(8,128)} %copy-done.6, f32[8,8,128]{2,1,0:T(8,128)} %get-tuple-element.72.deriv_ref, ...), custom_call_target="tpu_custom_call" | custom-call | tf_op jit(solution)/shard_map/backward/pallas_call | solution.py:661
  97.4 1.8 %collective-permute-done.2 = f32[640,128]{1,0:T(8,128)S(1)} collective-permute-done((f32[640,128]{1,0:T(8,128)}, f32[640,128]{1,0:T(8,128)S(1)}, u32[]{:S(2)}, u32[]{:S(2)}) %collective-permute-start.2) | collective-permute-done | bytes 327712 | tf_op jit(solution)/shard_map/ppermute | solution.py:701
  99.2 1.0 add.28
  100.2 10.7 %all_to_all.32 = f32[16,40,128]{2,1,0:T(8,128)S(1)} all-to-all(f32[16,40,128]{2,1,0:T(8,128)S(1)} %bitcast.22), channel_id=1, replica_groups=mesh['x'=4,'y'=4,'z'=8,'core'=2] {'x','y'}, dimensions={0} | all-to-all | bytes 655360 | tf_op jit(solution)/shard_map/all_to_all | solution.py:717
  110.9 10.7 %all_to_all.33 = f32[8,40,128]{2,1,0:T(8,128)S(1)} all-to-all(f32[8,40,128]{2,1,0:T(8,128)S(1)} %broadcast_in_dim.20), channel_id=1, replica_groups=mesh['x'=4,'y'=4,'z'=8,'core'=2] {'z'}, dimensions={0} | all-to-all | bytes 327680 | tf_op jit(solution)/shard_map/all_to_all | solution.py:710
  121.7 11.5 %all_to_all.34 = f32[16,40,128]{2,1,0:T(8,128)S(1)} all-to-all(f32[16,40,128]{2,1,0:T(8,128)S(1)} %broadcast_in_dim.21), channel_id=1, replica_groups=mesh['x'=4,'y'=4,'z'=8,'core'=2] {'x','y'}, dimensions={0} | all-to-all | bytes 655360 | tf_op jit(solution)/shard_map/all_to_all | solution.py:710
  133.2 4.0 %collective-permute-start.3 = (f32[640,128]{1,0:T(8,128)S(1)}, f32[640,128]{1,0:T(8,128)S(1)}, u32[]{:S(2)}, u32[]{:S(2)}) collective-permute-start(f32[640,128]{1,0:T(8,128)S(1)} %bitcast.21), channel_id=1, source_target_pairs={{0,1},{1,0},{2,3},{3,2},{4,5},{5,4},{6,7},{7,6},{8,9},{9,8},{10,11... | collective-permute-start | bytes 983048 | tf_op jit(solution)/shard_map/ppermute | solution.py:701
  137.2 1.2 slice_bitcast_fusion
  138.5 0.8 multiply_reduce_fusion
  140.1 1.5 %divide_subtract_fusion = (f32[160272]{0:T(1024)}, f32[160272]{0:T(1024)}, f32[160272]{0:T(1024)}) fusion(f32[160272]{0:T(1024)S(1)} %copy-done.2, f32[]{:T(128)S(6)} %div.14, f32[163840]{0:T(1024)S(1)} %maximum_bitcast_fusion, f32[160272]{0:T(1024)S(1)} %copy-done.3, f32[160272]{0:T(1024)S(1)} %copy-done.4), kind=kLoop, calls=%fused_computation.4 | loop fusion | flops 2083536 | bytes 4487620 | tf_op jit(solution)/shard_map/sub | solution.py:696
  (20 shorter events, 0.3 us)
Async XLA Ops:
  3.1 20.4 %all-to-all-start = ((f32[16,96,128]{2,1,0:T(8,128)}), f32[16,96,128]{2,1,0:T(8,128)S(1)}, u32[]{:S(2)}, u32[]{:S(2)}) async-start(f32[16,96,128]{2,1,0:T(8,128)} %get-tuple-element.45), calls=%async_computation | async-start | bytes 1572864 | tf_op jit(solution)/shard_map/all_to_all | solution.py:731
  23.5 4.5 %copy-start = (f32[16,96,128]{2,1,0:T(8,128)}, f32[16,96,128]{2,1,0:T(8,128)S(1)}, u32[]{:S(2)}) copy-start(f32[16,96,128]{2,1,0:T(8,128)S(1)} %all-to-all-done.here_ref) | copy-start | bytes 2359300
  23.5 4.5 %collective-permute-start = (f32[16,96,128]{2,1,0:T(8,128)S(1)}, f32[16,96,128]{2,1,0:T(8,128)S(1)}, u32[]{:S(2)}, u32[]{:S(2)}) collective-permute-start(f32[16,96,128]{2,1,0:T(8,128)S(1)} %all-to-all-done.here_ref), channel_id=1, source_target_pairs={{0,1},{1,0},{2,3},{3,2},{4,5},{5,4},{6,7},{7,6},{8,9},{9,8},{10,11... | collective-permute-start | bytes 2359304 | tf_op jit(solution)/shard_map/ppermute | solution.py:701
  28.0 0.9 copy-start.1
  78.2 2.6 %copy-start.5 = (f32[128,1,128]{2,1,0:T(1,128)}, f32[128,1,128]{2,1,0:T(1,128)S(1)}, u32[]{:S(2)}) copy-start(f32[128,1,128]{2,1,0:T(1,128)S(1)} %all_to_all.31) | copy-start | bytes 196612
  78.2 2.6 %collective-permute-start.1 = (f32[128,128]{1,0:T(8,128)S(1)}, f32[128,128]{1,0:T(8,128)S(1)}, u32[]{:S(2)}, u32[]{:S(2)}) collective-permute-start(f32[128,128]{1,0:T(8,128)S(1)} %bitcast.23), channel_id=1, source_target_pairs={{0,1},{1,0},{2,3},{3,2},{4,5},{5,4},{6,7},{7,6},{8,9},{9,8},{10,11... | collective-permute-start | bytes 196616 | tf_op jit(solution)/shard_map/ppermute | solution.py:701
  80.7 0.6 copy-start.6
  81.3 58.7 %copy-start.2 = (f32[160272]{0:T(1024)S(1)}, f32[160272]{0:T(1024)}, u32[]{:S(2)}) copy-start(f32[160272]{0:T(1024)} %param.8) | copy-start | bytes 1923268
  81.3 58.7 %copy-start.3 = (f32[160272]{0:T(1024)S(1)}, f32[160272]{0:T(1024)}, u32[]{:S(2)}) copy-start(f32[160272]{0:T(1024)} %param.9) | copy-start | bytes 1923268
  81.3 58.7 %copy-start.4 = (f32[160272]{0:T(1024)S(1)}, f32[160272]{0:T(1024)}, u32[]{:S(2)}) copy-start(f32[160272]{0:T(1024)} %param.10) | copy-start | bytes 1923268
  97.3 1.9 %collective-permute-start.2 = (f32[640,128]{1,0:T(8,128)}, f32[640,128]{1,0:T(8,128)S(1)}, u32[]{:S(2)}, u32[]{:S(2)}) collective-permute-start(f32[640,128]{1,0:T(8,128)} %get-tuple-element.84), channel_id=1, source_target_pairs={{0,1},{1,0},{2,3},{3,2},{4,5},{5,4},{6,7},{7,6},{8,9},{9,8},{10,11... | collective-permute-start | bytes 983048 | tf_op jit(solution)/shard_map/ppermute | solution.py:701
  133.2 5.2 %collective-permute-start.3 = (f32[640,128]{1,0:T(8,128)S(1)}, f32[640,128]{1,0:T(8,128)S(1)}, u32[]{:S(2)}, u32[]{:S(2)}) collective-permute-start(f32[640,128]{1,0:T(8,128)S(1)} %bitcast.21), channel_id=1, source_target_pairs={{0,1},{1,0},{2,3},{3,2},{4,5},{5,4},{6,7},{7,6},{8,9},{9,8},{10,11... | collective-permute-start | bytes 983048 | tf_op jit(solution)/shard_map/ppermute | solution.py:701

commit v4 on v3

v4 whole, which is shorter than its diff:
```python
import math

import jax
import jax.numpy as jnp
from jax import lax
from jax.experimental import pallas as pl
from jax.experimental.pallas import tpu as pltpu
from jax.sharding import Mesh
from jax.sharding import PartitionSpec as P

C = 128
HID = 64
NB = 8
SPECIES = 10
RO = 16
LAYERS = 2
WINDOWS = 32
ATOMS = 128
SOLUTE = 16
K = 16
SLOTS = K - 1
EDGES = SLOTS * ATOMS
NPAR = 160272
ROWS = 1280

RADIUS_CUT = 8.0
SOFTENING = 0.01
GRAD_SCALE = 4.0

ROW_EMBED = 0
ROW_LAYER = 10
LAYER_ROWS = 613
OFF_W1, OFF_W2, OFF_W3, OFF_UP, OFF_LIN, OFF_SQ, OFF_SKIP, OFF_READ = 0, 4, 36, 100, 228, 356, 484, 612
ROW_HEAD = ROW_LAYER + LAYERS * LAYER_ROWS
ROW_OUT = ROW_HEAD + RO
USED_ROWS = ROW_OUT + 1

ROW_POS, ROW_SPECIES, ROW_META, FRAME_ROWS = SLOTS, SLOTS + 3, SLOTS + 4, 24
KEEP = 4
GROUP = 32
PLAN_ROWS = 16
PLAN_COUNT, PLAN_OWN = 8, 9

AXES = {"x": 4, "y": 4, "z": 8, "core": 2}
PLANE = ("x", "y")
PLANE_CHIPS = 16
CHIPS = 128
DEPTH = 8

F32, BF16 = jnp.float32, jnp.bfloat16


def halves(x):
    hi = x.astype(BF16)
    return hi, (x - hi.astype(F32)).astype(BF16)


def stack_left(w):
    hi, lo = halves(w)
    return jnp.concatenate([hi, hi, lo], axis=1)


def dot(a, b):
    return jnp.dot(a, b, preferred_element_type=F32)


def dot_nt(a, b):
    return lax.dot_general(a, b, (((1,), (1,)), ((), ())), preferred_element_type=F32)


def mm(left, x):
    hi, lo = halves(x)
    return dot(left, jnp.concatenate([hi, lo, hi], axis=0))


def nt_stacked(xs, ys):
    m, n = xs.shape[0] // 2, ys.shape[0] // 2
    o = dot_nt(xs, ys)
    return o[:m, :n] + (o[:m, n:] + o[m:, :n])


def tall(x):
    return jnp.concatenate(halves(x), axis=0)


def nt(x, y):
    return nt_stacked(tall(x), tall(y))


def tile_rows(x, reps):
    return jnp.concatenate([x] * reps, axis=1)


def unflatten(rows, height, width):
    total = None
    for r, row in enumerate(rows):
        place = lax.broadcasted_iota(jnp.int32, (height, 128), 1) + 128 * r
        own = lax.broadcasted_iota(jnp.int32, (height, 128), 0)
        first = own * width
        kept = jnp.where((place >= first) & (place < first + width), jnp.broadcast_to(row, (height, 128)), 0.0)
        col = lax.broadcasted_iota(jnp.int32, (128, 16), 1)
        pos = (lax.broadcasted_iota(jnp.int32, (128, 16), 0) + 128 * r) % width
        pick = (col == pos).astype(BF16)
        a = kept.astype(BF16)
        rest = kept - a.astype(F32)
        b = rest.astype(BF16)
        c = (rest - b.astype(F32)).astype(BF16)
        piece = dot(a, pick) + (dot(b, pick) + dot(c, pick))
        total = piece if total is None else total + piece
    return total


def flatten(mat, height, width, n_rows):
    a = mat.astype(BF16)
    rest = mat - a.astype(F32)
    b = rest.astype(BF16)
    c = (rest - b.astype(F32)).astype(BF16)
    out = []
    for r in range(n_rows):
        col = lax.broadcasted_iota(jnp.int32, (16, 128), 0)
        pos = (lax.broadcasted_iota(jnp.int32, (16, 128), 1) + 128 * r) % width
        pick = (col == pos).astype(BF16)
        spread = dot(a, pick) + (dot(b, pick) + dot(c, pick))
        place = lax.broadcasted_iota(jnp.int32, (height, 128), 1) + 128 * r
        first = lax.broadcasted_iota(jnp.int32, (height, 128), 0) * width
        kept = jnp.where((place >= first) & (place < first + width), spread, 0.0)
        out.append(jnp.sum(kept, axis=0, keepdims=True))
    return out


def silu_parts(z):
    s = 0.5 * jnp.tanh(0.5 * z) + 0.5
    value = z * s
    return value, s + value * (1.0 - s)


def prepare(th_ref, w1_s, w2_s, w3_s, up_s, upt_s, mix_s, mixt_s, hd_s, hdt_s, emb_s, read_s, out_s, w3t_ref, w2t_ref, tmp_s):
    emb = unflatten([th_ref[ROW_EMBED + r : ROW_EMBED + r + 1, :] for r in range(10)], C, SPECIES)
    emb_s[...] = stack_left(emb)
    for l in range(LAYERS):
        o = ROW_LAYER + l * LAYER_ROWS
        w1 = unflatten([th_ref[o + OFF_W1 + r : o + OFF_W1 + r + 1, :] for r in range(4)], HID, NB) * NB ** (-0.5)
        w1_s[l] = stack_left(w1)
        for off, rows, reach, dst, dst_t in ((OFF_W2, 32, HID, w2_s, w2t_ref), (OFF_W3, 64, HID, w3_s, w3t_ref)):
            packed = th_ref[o + off : o + off + rows, :] * reach ** (-0.5)
            tmp_s[pl.ds(0, rows, stride=2), :] = packed
            tmp_s[pl.ds(1, rows, stride=2), :] = pltpu.roll(packed, HID, 1)
            wide = tmp_s[: 2 * rows, :]
            w = wide[:, :HID]
            dst[l] = stack_left(w)
            if rows == 32:
                wide = jnp.concatenate([wide, wide], axis=0)
            wt = jnp.transpose(wide)[:HID, : 2 * rows]
            dst_t[l] = jnp.concatenate(halves(wt), axis=1)
        mats, mats_t = [], []
        for off in (OFF_LIN, OFF_SQ, OFF_SKIP):
            w = th_ref[o + off : o + off + C, :] * C ** (-0.5)
            mats.append(w)
            mats_t.append(jnp.transpose(w))
        mix_s[l] = stack_left(jnp.concatenate(mats, axis=1))
        mixt_s[l] = stack_left(jnp.concatenate(mats_t, axis=0))
        w = th_ref[o + OFF_UP : o + OFF_UP + C, :] * C ** (-0.5)
        up_s[l] = stack_left(w)
        upt_s[l] = stack_left(jnp.transpose(w))
        read_s[l] = jnp.transpose(
            jnp.broadcast_to(th_ref[o + OFF_READ : o + OFF_READ + 1, :] * C ** (-0.5), (128, 128))
        )
    w = th_ref[ROW_HEAD : ROW_HEAD + RO, :] * C ** (-0.5)
    hd_s[...] = stack_left(w)
    wide = jnp.concatenate([w, jnp.zeros((128 - RO, 128), F32)], axis=0)
    hdt_s[...] = stack_left(jnp.transpose(wide)[:, :RO])
    out_s[...] = jnp.transpose(jnp.broadcast_to(th_ref[ROW_OUT : ROW_OUT + 1, :] * RO ** (-0.5), (128, 128)))[:RO, :]


def pair_products(co, x):
    m = co.shape[0]
    a, b = co[:, :ATOMS], co[:, ATOMS:]
    left = jnp.concatenate([jnp.concatenate([a, jnp.zeros_like(a)], axis=1), jnp.concatenate([b, a], axis=1)], axis=0)
    o = nt(left, x)
    return o[:m], o[m:]


def pair_sums(x):
    n = x.shape[0]
    row = lax.broadcasted_iota(jnp.int32, (16, 2 * ATOMS), 0)
    col = lax.broadcasted_iota(jnp.int32, (16, 2 * ATOMS), 1)
    o = dot_nt(jnp.where((row < 8) == (col < ATOMS), 1.0, 0.0).astype(BF16), tall(x))
    return o[:, :n] + o[:, n:]


def wide(x):
    return jnp.concatenate([x, jnp.zeros((x.shape[0], 128 - x.shape[1]), x.dtype)], axis=1)


def run_frame(x, weights, spare, deriv_ref, grad_ref, scratch):
    w1_s, w2_s, w3_s, up_s, upt_s, mix_s, mixt_s, hd_s, hdt_s, emb_s, read_s, out_s = weights
    w3t_s, w2t_s = spare
    oh_s, rad_s, act_s, slope_s, first_s, gath_s, dist_s = scratch
    window = x[ROW_META : ROW_META + 1, :1]
    lam = window / (WINDOWS - 1)
    slot = lax.broadcasted_iota(jnp.int32, (K, ATOMS), 0)
    nb = jnp.where(slot < SLOTS, x[:K].astype(jnp.int32), -1)
    partner = jnp.maximum(nb, 0)
    present = nb >= 0
    species = x[ROW_SPECIES : ROW_SPECIES + 1, :]
    r2 = jnp.full((K, ATOMS), SOFTENING, F32)
    for d in range(3):
        row = jnp.broadcast_to(x[ROW_POS + d : ROW_POS + d + 1, :], (K, ATOMS))
        delta = jnp.take_along_axis(row, partner, axis=1) - row
        r2 = r2 + delta * delta
    radius = jnp.sqrt(r2)
    ratio = radius * (1.0 / RADIUS_CUT)
    env = 1.0 - ratio * ratio
    env = jnp.where(present, env * env, 0.0) * (1.0 / K)
    atom = lax.broadcasted_iota(jnp.int32, (K, ATOMS), 1)
    crossing = (atom < SOLUTE) != (partner < SOLUTE)
    fac = jnp.where(crossing, lam * env, env)
    dfac = jnp.where(crossing, env, 0.0)
    angle = ratio * math.pi
    s1 = jnp.sin(angle) * (math.sqrt(2.0 / RADIUS_CUT) / radius)
    twice = 2.0 * jnp.cos(angle)
    prev, cur = jnp.zeros_like(s1), s1
    for m in range(NB):
        dist_s[m * K : (m + 1) * K, :] = cur
        prev, cur = cur, twice * cur - prev
    basis = jnp.concatenate([dist_s[pl.ds(k, NB, stride=K), :] for k in range(SLOTS)], axis=1)
    bhi = basis.astype(BF16).astype(F32)
    blo = basis - bhi
    basis = jnp.concatenate([bhi, blo], axis=0).astype(BF16)
    none = jnp.zeros_like(bhi)
    w1_rhs = jnp.concatenate([bhi, none, blo, none, bhi, none], axis=0).astype(BF16)
    yield
    sub = lax.broadcasted_iota(jnp.int32, (ATOMS, ATOMS), 0)
    for k in range(SLOTS):
        hit = jnp.broadcast_to(partner[k : k + 1, :], (ATOMS, ATOMS)) == sub
        oh_s[:, k * ATOMS : (k + 1) * ATOMS] = jnp.where(hit, 1.0, 0.0).astype(BF16)
    yield
    for l in range(LAYERS):
        z1 = dot(w1_s[l], w1_rhs)
        v1, d1 = silu_parts(z1)
        h1, l1 = halves(v1)
        act_s[l, 0] = h1
        slope_s[l, 0] = d1.astype(BF16)
        yield
        z2 = dot(w2_s[l], jnp.concatenate([h1, l1, h1], axis=0))
        v2, d2 = silu_parts(z2)
        h2, l2 = halves(v2)
        act_s[l, 1] = h2
        slope_s[l, 1] = d2.astype(BF16)
        yield
        rad_s[l] = dot(w3_s[l], jnp.concatenate([h2, l2, h2], axis=0))
        yield

    rows16 = lax.broadcasted_iota(jnp.int32, (16, ATOMS), 0)
    spc = jnp.where(rows16 == jnp.broadcast_to(species, (16, ATOMS)).astype(jnp.int32), 1.0, 0.0)
    feat = mm(emb_s[...], spc)
    zero = jnp.zeros((C, ATOMS), F32)
    feat = jnp.concatenate([feat, zero], axis=1)
    yield
    deriv = jnp.zeros((), F32)
    pools, feats = [], [feat]
    for l in range(LAYERS):
        if l == 0:
            lift = mm(up_s[l], feat[:, :ATOMS])
            lhs = jnp.concatenate(halves(lift), axis=1)
        else:
            lift = mm(up_s[l], feat)
            lhs = jnp.concatenate(
                [jnp.concatenate(halves(lift[:, :ATOMS]), axis=1), jnp.concatenate(halves(lift[:, ATOMS:]), axis=1)],
                axis=0,
            )
        yield
        oh = oh_s[...]
        g = dot(lhs, jnp.concatenate([oh, oh], axis=0))
        if l == 0:
            first_s[...] = g
        else:
            gath_s[0] = g[:C].astype(BF16)
            gath_s[1] = g[C:].astype(BF16)
        yield
        pool, dpool = zero, zero
        for k in range(SLOTS):
            t = slice(k * ATOMS, (k + 1) * ATOMS)
            rad = rad_s[l, :, t]
            rg = rad * g[:C, t]
            pool = pool + fac[k : k + 1, :] * rg
            dpool = dpool + dfac[k : k + 1, :] * rg
            if l == 1:
                dpool = dpool + fac[k : k + 1, :] * (rad * g[C:, t])
        pools.append((pool, dpool))
        yield
        x = jnp.concatenate(
            [
                jnp.concatenate([pool, dpool], axis=1),
                jnp.concatenate([pool * pool, 2.0 * pool * dpool], axis=1),
                feat,
            ],
            axis=0,
        )
        feat = mm(mix_s[l], x)
        feats.append(feat)
        deriv = deriv + jnp.sum(read_s[l] * feat[:, ATOMS:])
        yield
    q = mm(hd_s[...], feat)
    q0, q1 = q[:, :ATOMS], q[:, ATOMS:]
    sg = 0.5 * jnp.tanh(0.5 * q0) + 0.5
    val = q0 * sg
    first = sg + val * (1.0 - sg)
    second = sg * (1.0 - sg) * (2.0 + q0 * (1.0 - 2.0 * sg))
    tail = first * q1
    deriv = deriv + jnp.sum(out_s[...] * tail)
    lane = lax.broadcasted_iota(jnp.int32, (8, 128), 1)
    deriv_ref[...] = jnp.where(lane == 0, deriv, jnp.broadcast_to(window, (8, 128)))
    at = jnp.broadcast_to(window.astype(jnp.int32), (8, 128))
    tally = jnp.where(lane == at, 1.0, jnp.where(lane == at + WINDOWS, deriv, 0.0))

    def put(row, a, b):
        grad_ref[0, row : row + a.shape[0], :] = a
        grad_ref[1, row : row + b.shape[0], :] = b

    co_q = jnp.concatenate([out_s[...] * first, out_s[...] * second * q1], axis=1)
    co = mm(hdt_s[...], co_q) + jnp.concatenate([read_s[1], zero], axis=1)
    yield
    put(G_HEAD, *pair_products(co_q, feat))
    o = wide(pair_sums(jnp.concatenate([val, tail], axis=1)))
    put(G_OUT, o[:8], o[8:])
    for l in range(LAYERS):
        o = pair_sums(feats[l + 1])
        put(G_READ + 8 * l, o[:8], o[8:])
    yield
    w3_parts, w2_parts, w1_parts = {}, {}, {}
    for l in (1, 0):
        y = mm(mixt_s[l], co)
        pool, dpool = pools[l]
        ya, yb = y[:, :ATOMS], y[:, ATOMS:]
        ap = ya[:C] + 2.0 * pool * ya[C : 2 * C]
        bp = yb[:C] + 2.0 * pool * yb[C : 2 * C] + 2.0 * dpool * ya[C : 2 * C]
        yield
        lefts, rights = [[], []], [[], []]
        for k in range(SLOTS):
            t = slice(k * ATOMS, (k + 1) * ATOMS)
            f, df = fac[k : k + 1, :], dfac[k : k + 1, :]
            u, v = f * ap, f * bp + df * ap
            rad = rad_s[l, :, t]
            lefts[0].append((rad * u).astype(BF16))
            lefts[1].append((rad * v).astype(BF16))
            if l == 0:
                g = first_s[:, t]
                rights[0].append((g * u).astype(BF16))
                rights[1].append((g * v).astype(BF16))
            else:
                g = gath_s[0, :, t].astype(F32)
                rights[0].append((g * u).astype(BF16))
                rights[1].append((g * v + gath_s[1, :, t].astype(F32) * u).astype(BF16))
        left = jnp.concatenate([jnp.concatenate(lst, axis=1) for lst in lefts], axis=0)
        yield
        acc = dot_nt(left, oh_s[...])
        cl = jnp.concatenate([acc[:C], acc[C:]], axis=1)
        yield
        co_in, co = co, y[2 * C :] + mm(upt_s[l], cl)
        if l == 1:
            co = co + jnp.concatenate([read_s[0], zero], axis=1)
        yield
        right = [jnp.concatenate(lst, axis=1) for lst in rights]
        o = dot_nt(jnp.concatenate(right, axis=0), act_s[l, 1])
        w3_parts[l] = o
        c2 = [(dot(w3t_s[l], jnp.concatenate([r, r], axis=0)) * slope_s[l, 1].astype(F32)).astype(BF16) for r in right]
        yield
        w2_parts[l] = dot_nt(jnp.concatenate(c2, axis=0), act_s[l, 0])
        c1 = [(dot(w2t_s[l], jnp.concatenate([r, r], axis=0)) * slope_s[l, 0].astype(F32)).astype(BF16) for r in c2]
        yield
        w1_parts[l] = dot_nt(jnp.concatenate(c1, axis=0), basis)
        yield
        x = jnp.concatenate(
            [
                jnp.concatenate([pool, dpool], axis=1),
                jnp.concatenate([pool * pool, 2.0 * pool * dpool], axis=1),
                feats[l],
            ],
            axis=0,
        )
        a, b = pair_products(co_in, x)
        for i in range(3):
            put(G_MIX + (3 * l + i) * C, a[:, i * C : (i + 1) * C], b[:, i * C : (i + 1) * C])
        yield
        put(G_UP + l * C, *pair_products(cl, feats[l]))
        yield
    o = dot_nt(tall(jnp.concatenate([co[:, :ATOMS], co[:, ATOMS:]], axis=0)), spc.astype(BF16))
    emb = o[: 2 * C] + o[2 * C :]
    w3 = jnp.concatenate([w3_parts[0], w3_parts[1]], axis=1)
    put(G_W3, w3[:C], w3[C:])
    w2 = jnp.concatenate([w2_parts[0], w2_parts[1]], axis=1)
    put(G_W2, w2[:HID], w2[HID:])
    low = [jnp.concatenate([w1_parts[0][h], w1_parts[1][h]], axis=0) for h in (slice(0, HID), slice(HID, 2 * HID))]
    put(
        G_MISC,
        wide(jnp.concatenate([emb[:C], low[0]], axis=1)),
        wide(jnp.concatenate([emb[C:], low[1]], axis=1)),
    )
    return tally


def in_turns(frames):
    results = [None] * len(frames)
    waiting = list(range(len(frames)))
    for i, frame in enumerate(frames):
        for _ in range(2 * (len(frames) - 1 - i)):
            next(frame)
    while waiting:
        for i in list(waiting):
            try:
                next(frames[i])
            except StopIteration as end:
                results[i] = end.value
                waiting.remove(i)
    return results


N_WEIGHTS = 12
G_MIX, G_UP, G_W3, G_W2, G_MISC, G_HEAD, G_READ, G_OUT = 0, 768, 1024, 1152, 1216, 1344, 1360, 1376
G_ROWS = 1384
BATCH = 3


def pack_kernel(count_ref, window_ref, pos_ref, spc_ref, nb_ref, own_ref, send_ref, wide_s):
    n = nb_ref.shape[0]
    lane = lax.broadcasted_iota(jnp.int32, (1, 128), 1)
    for f in range(n):
        own_ref[f, :SLOTS, :] = nb_ref[f, :SLOTS, :].astype(F32)
        for d in range(3):
            own_ref[f, ROW_POS + d : ROW_POS + d + 1, :] = pos_ref[d, f : f + 1, :]
        own_ref[f, ROW_SPECIES : ROW_SPECIES + 1, :] = spc_ref[f : f + 1, :].astype(F32)
        own_ref[f, ROW_META + 1 :, :] = jnp.zeros((FRAME_ROWS - ROW_META - 1, 128), F32)
        own_ref[f, ROW_META : ROW_META + 1, :] = jnp.where(lane == 0, window_ref[f], count_ref[0]).astype(F32)
    for f in range(KEEP, n):
        wide_s[(f - KEEP) * FRAME_ROWS : (f - KEEP + 1) * FRAME_ROWS, :] = own_ref[f]
    wide = wide_s[...]
    for g in range(PLANE_CHIPS):
        send_ref[g] = wide


def deal_kernel(me_ref, here_ref, there_ref, plan_ref):
    n = 8
    lane = lax.broadcasted_iota(jnp.int32, (GROUP, 128), 1)
    gid = lax.broadcasted_iota(jnp.int32, (GROUP, 128), 0)
    core = me_ref[0] // PLANE_CHIPS
    here, there = here_ref[:, ROW_META % 8, :], there_ref[:, ROW_META % 8, :]
    meta = jnp.concatenate([jnp.where(core == 0, here, there), jnp.where(core == 0, there, here)], axis=0)
    counts = jnp.broadcast_to(jnp.sum(jnp.where(lane == 1, meta, 0.0), axis=1, keepdims=True), (GROUP, 128))
    base = jnp.minimum(counts, float(KEEP))
    surplus = counts - base
    total = jnp.sum(surplus, axis=0, keepdims=True)
    lane_f = lane.astype(F32)
    room = jnp.sum(jnp.maximum(lane_f + 1.0 - base, 0.0), axis=0, keepdims=True)
    full = jnp.where((room <= total) & (lane[:1] < n), 1.0, 0.0)
    level = jnp.broadcast_to(jnp.sum(full, axis=1, keepdims=True), (GROUP, 128))
    taken = jnp.maximum(level - base, 0.0)
    left = total - jnp.sum(taken, axis=0, keepdims=True)
    tri_r = lax.broadcasted_iota(jnp.int32, (GROUP, GROUP), 0)
    tri_c = lax.broadcasted_iota(jnp.int32, (GROUP, GROUP), 1)
    before = jnp.where(tri_c < tri_r, 1.0, 0.0).astype(BF16)
    open_ = jnp.where(base <= level, 1.0, 0.0)
    rank = dot(before, open_.astype(BF16))
    taken = taken + jnp.where(rank < left, open_, 0.0)
    offset = dot(before, surplus.astype(BF16))
    me = me_ref[0]
    start = jnp.sum(jnp.where(gid < me, taken, 0.0), axis=0, keepdims=True)
    mine = jnp.sum(jnp.where(gid == me, base + taken, 0.0), axis=0, keepdims=True)
    held = jnp.sum(jnp.where(gid == me, base, 0.0), axis=0, keepdims=True)
    order = jnp.where(lane_f < surplus, offset + lane_f, -1.0)
    place = ((gid % PLANE_CHIPS) * (n - KEEP) + lane).astype(F32)
    away = jnp.where(gid // PLANE_CHIPS == core, 0.0, 1.0)
    for j in range(n):
        hit = order == start + float(j)
        one = jnp.sum(jnp.sum(jnp.where(hit, place, 0.0), axis=0, keepdims=True), axis=1, keepdims=True)
        two = jnp.sum(jnp.sum(jnp.where(hit, away, 0.0), axis=0, keepdims=True), axis=1, keepdims=True)
        plan_ref[j : j + 1, :] = jnp.where(lane[:1] == 0, one, two).astype(jnp.int32)
    plan_ref[n : n + 1, :] = mine.astype(jnp.int32)
    plan_ref[n + 1 : n + 2, :] = held.astype(jnp.int32)
    plan_ref[n + 2 :, :] = jnp.zeros((PLAN_ROWS - n - 2, 128), jnp.int32)


def first_kernel(th_ref, own_ref, *refs):
    weights, spare = refs[:N_WEIGHTS], refs[N_WEIGHTS : N_WEIGHTS + 2]
    deriv_ref, grad_ref, tally_ref, tmp_s, *scratch = refs[N_WEIGHTS + 2 :]
    prepare(th_ref, *weights, *spare, tmp_s)
    frame = run_frame(own_ref[0], weights, spare, deriv_ref.at[0], grad_ref.at[0], [ref.at[0] for ref in scratch])
    tally_ref[...] = in_turns([frame])[0]


def rest_kernel(plan_ref, own_ref, *refs):
    here, there = refs[:BATCH], refs[BATCH : 2 * BATCH]
    first_ref, *refs = refs[2 * BATCH :]
    weights, spare = refs[:N_WEIGHTS], refs[N_WEIGHTS : N_WEIGHTS + 2]
    deriv_ref, grad_ref, tally_ref, sum_s, *scratch = refs[N_WEIGHTS + 2 :]
    step = pl.program_id(0)
    count, own = plan_ref[PLAN_COUNT, 0], plan_ref[PLAN_OWN, 0]

    @pl.when(step == 0)
    def _():
        sum_s[...] = first_ref[...]

    @pl.when(step * BATCH + 1 < count)
    def _():
        frames = []
        for j in range(BATCH):
            at = step * BATCH + 1 + j
            away = plan_ref[jnp.clip(at - own, 0, 7), 1]
            taken = jnp.where(away == 0, here[j][0], there[j][0])
            kept = own_ref[jnp.where(at < own, at, 0)]
            x = jnp.where((at >= own) & (at < count), taken, kept)
            frames.append(
                run_frame(x, weights, spare, deriv_ref.at[j], grad_ref.at[j], [ref.at[j] for ref in scratch])
            )
        total = sum_s[...]
        for j, row in enumerate(in_turns(frames)):
            total = total + jnp.where(step * BATCH + 1 + j < count, row, 0.0)
        sum_s[...] = total

    @pl.when(step == pl.num_programs(0) - 1)
    def _():
        tally_ref[...] = jnp.broadcast_to(sum_s[:1, :], (CHIPS, 128))


def combine_kernel(
    plan_ref, core_ref, parts_ref, more_ref, deriv0_ref, grad0_ref, deriv_ref, grad_ref,
    mine_ref, other_ref, means_ref,
    all_s, acc_s, window_s, tmp_s,
):
    step = pl.program_id(0)

    def scaled(deriv, grads):
        mine = lax.broadcasted_iota(jnp.int32, (1, 128), 1) == deriv[:1, 1:2].astype(jnp.int32)
        centre = jnp.sum(jnp.where(mine, window_s[0, :1], 0.0), axis=1, keepdims=True)
        share = jnp.sum(jnp.where(mine, window_s[1, :1], 0.0), axis=1, keepdims=True)
        return share * grads[1] - share * (deriv[:1, :1] - centre) * grads[0]

    @pl.when(step == 0)
    def _():
        total = jnp.broadcast_to(jnp.sum(parts_ref[...] + more_ref[...], axis=0, keepdims=True), (8, 128))
        lane = lax.broadcasted_iota(jnp.int32, (8, 128), 1)
        sizes = jnp.maximum(total, 1.0)
        means = pltpu.roll(total, 128 - WINDOWS, 1) / sizes
        ends = (lane == 0) | (lane == WINDOWS - 1)
        weight = jnp.where(ends, 0.5, 1.0) / (WINDOWS - 1)
        means_ref[...] = means
        window_s[0] = means
        window_s[1] = weight / sizes
        acc_s[...] = scaled(deriv0_ref[0], grad0_ref[0])

    @pl.when((step > 0) & (step < plan_ref[PLAN_COUNT, 0]))
    def _():
        acc_s[...] += scaled(deriv_ref[0], grad_ref[0])

    @pl.when(step == pl.num_programs(0) - 1)
    def _():
        all_s[USED_ROWS // 8 * 8 :, :] = jnp.zeros((ROWS - USED_ROWS // 8 * 8, 128), F32)
        misc = acc_s[G_MISC : G_MISC + C, :]
        for r, row in enumerate(flatten(misc[:, :16], C, SPECIES, 10)):
            all_s[ROW_EMBED + r : ROW_EMBED + r + 1, :] = row
        for l in range(LAYERS):
            o = ROW_LAYER + l * LAYER_ROWS
            w1 = misc[l * HID : (l + 1) * HID, 16:32] * NB ** (-0.5)
            w1 = w1[:, :NB] + w1[:, NB:]
            w1 = jnp.concatenate([w1, jnp.zeros((HID, 8), F32)], axis=1)
            for r, row in enumerate(flatten(w1, HID, NB, 4)):
                all_s[o + OFF_W1 + r : o + OFF_W1 + r + 1, :] = row
            for off, rows, at in ((OFF_W2, 32, G_W2), (OFF_W3, 64, G_W3)):
                tmp_s[: 2 * rows, :] = acc_s[at : at + 2 * rows, :] * HID ** (-0.5)
                even = tmp_s[pl.ds(0, rows, stride=2), :]
                odd = tmp_s[pl.ds(1, rows, stride=2), :]
                left = lax.broadcasted_iota(jnp.int32, (rows, 128), 1) < HID
                if l == 0:
                    both = jnp.where(left, even, pltpu.roll(odd, HID, 1))
                else:
                    both = jnp.where(left, pltpu.roll(even, HID, 1), odd)
                all_s[o + off : o + off + rows, :] = both
            for i, off in enumerate((OFF_LIN, OFF_SQ, OFF_SKIP)):
                at = G_MIX + (3 * l + i) * C
                all_s[o + off : o + off + C, :] = acc_s[at : at + C, :] * C ** (-0.5)
            all_s[o + OFF_UP : o + OFF_UP + C, :] = acc_s[G_UP + l * C : G_UP + (l + 1) * C, :] * C ** (-0.5)
            all_s[o + OFF_READ : o + OFF_READ + 1, :] = acc_s[G_READ + 8 * l : G_READ + 8 * l + 1, :] * C ** (-0.5)
        all_s[ROW_HEAD : ROW_HEAD + RO, :] = acc_s[G_HEAD : G_HEAD + RO, :] * C ** (-0.5)
        all_s[ROW_OUT : ROW_OUT + 1, :] = acc_s[G_OUT : G_OUT + 1, :] * RO ** (-0.5)
        half = ROWS // 2
        core = core_ref[0]
        mine_ref[...] = all_s[pl.ds(pl.multiple_of(core * half, half), half), :]
        other_ref[...] = all_s[pl.ds(pl.multiple_of((1 - core) * half, half), half), :]


def whole_spec(shape):
    return pl.BlockSpec(shape, lambda i, *_: (0,) * len(shape))


SMEM_SPEC = pl.BlockSpec(memory_space=pltpu.SMEM)
WEIGHTS = (
    ((LAYERS, HID, 48), BF16),
    ((LAYERS, HID, 3 * HID), BF16),
    ((LAYERS, C, 3 * HID), BF16),
    ((LAYERS, C, 3 * C), BF16),
    ((LAYERS, C, 3 * C), BF16),
    ((LAYERS, C, 9 * C), BF16),
    ((LAYERS, 3 * C, 3 * C), BF16),
    ((RO, 3 * C), BF16),
    ((C, 3 * RO), BF16),
    ((C, 48), BF16),
    ((LAYERS, C, 128), F32),
    ((RO, 128), F32),
)
SPARE = (((LAYERS, HID, 2 * C), BF16), ((LAYERS, HID, 2 * HID), BF16))


def frame_scratch(n):
    return [
        pltpu.VMEM((n, ATOMS, EDGES), BF16),
        pltpu.VMEM((n, LAYERS, C, EDGES), F32),
        pltpu.VMEM((n, LAYERS, 2, HID, EDGES), BF16),
        pltpu.VMEM((n, LAYERS, 2, HID, EDGES), BF16),
        pltpu.VMEM((n, C, EDGES), F32),
        pltpu.VMEM((n, 2, C, EDGES), BF16),
        pltpu.VMEM((n, NB * K, ATOMS), F32),
    ]


LIMIT = pltpu.CompilerParams(vmem_limit_bytes=56 * 2**20)


TALLY = jax.ShapeDtypeStruct((8, 128), F32)


def run_pack(count, window_of, positions, species, neighbours):
    n = positions.shape[0]
    return pl.pallas_call(
        pack_kernel,
        in_specs=[SMEM_SPEC, SMEM_SPEC] + [pl.BlockSpec(memory_space=pltpu.VMEM)] * 3,
        out_specs=[pl.BlockSpec(memory_space=pltpu.VMEM)] * 2,
        scratch_shapes=[pltpu.VMEM(((n - KEEP) * FRAME_ROWS, 128), F32)],
        out_shape=[
            jax.ShapeDtypeStruct((n, FRAME_ROWS, 128), F32),
            jax.ShapeDtypeStruct((PLANE_CHIPS, (n - KEEP) * FRAME_ROWS, 128), F32),
        ],
        name="pack",
    )(count, window_of, jnp.transpose(positions, (1, 0, 2)), species, neighbours)


def run_deal(me, here, there):
    return pl.pallas_call(
        deal_kernel,
        grid=(1,),
        in_specs=[SMEM_SPEC] + [pl.BlockSpec((PLANE_CHIPS, 8, 128), lambda i: (0, ROW_META // 8, 0))] * 2,
        out_specs=whole_spec((PLAN_ROWS, 128)),
        out_shape=jax.ShapeDtypeStruct((PLAN_ROWS, 128), jnp.int32),
        name="deal",
    )(me, here, there)


def run_first(theta, own):
    held = WEIGHTS + SPARE
    shapes = [(s, t) for s, t in held] + [((1, 8, 128), F32), ((1, 2, G_ROWS, 128), F32), (TALLY.shape, F32)]
    out = pl.pallas_call(
        first_kernel,
        grid=(1,),
        in_specs=[whole_spec((ROWS, 128)), whole_spec((1, FRAME_ROWS, 128))],
        out_specs=[whole_spec(s) for s, _ in shapes],
        scratch_shapes=[pltpu.VMEM((128, 128), F32)] + frame_scratch(1),
        out_shape=[jax.ShapeDtypeStruct(s, t) for s, t in shapes],
        compiler_params=LIMIT,
        cost_estimate=pl.CostEstimate(flops=10**9, bytes_accessed=4 * 10**7, transcendentals=10**6),
        name="first_frame",
    )(theta, own)
    return out[: N_WEIGHTS + 2], out[N_WEIGHTS + 2], out[N_WEIGHTS + 3], out[N_WEIGHTS + 4]


def run_rest(plan, own, here, there, tally, held):
    n = own.shape[0]
    steps = -(-(n - 1) // BATCH)

    def taken_spec(j):
        def index(i, plan):
            return (plan[jnp.clip(i * BATCH + 1 + j - plan[PLAN_OWN, 0], 0, 7), 0], 0, 0)

        return pl.BlockSpec((1, FRAME_ROWS, 128), index)

    def result_spec(shape):
        def index(i, plan):
            return (jnp.minimum(i, jnp.maximum((plan[PLAN_COUNT, 0] + BATCH - 2) // BATCH - 1, 0)),) + (0,) * len(shape)

        return pl.BlockSpec((BATCH,) + shape, index)

    results = ((8, 128), (2, G_ROWS, 128))
    return pl.pallas_call(
        rest_kernel,
        grid_spec=pltpu.PrefetchScalarGridSpec(
            num_scalar_prefetch=1,
            grid=(steps,),
            in_specs=[whole_spec(own.shape)]
            + [taken_spec(j) for j in range(BATCH)] * 2
            + [whole_spec(TALLY.shape)]
            + [whole_spec(s) for s, _ in WEIGHTS + SPARE],
            out_specs=[result_spec(s) for s in results] + [whole_spec((CHIPS, 128))],
            scratch_shapes=[pltpu.VMEM(TALLY.shape, F32)] + frame_scratch(BATCH),
        ),
        out_shape=[jax.ShapeDtypeStruct((steps * BATCH,) + s, F32) for s in results]
        + [jax.ShapeDtypeStruct((CHIPS, 128), F32)],
        compiler_params=LIMIT,
        name="other_frames",
    )(plan, own, *[here] * BATCH, *[there] * BATCH, tally, *held)


def run_combine(plan, core, parts, more, deriv0, grad0, deriv, grad, n):
    def rest_spec(shape):
        def index(i, plan):
            return (jnp.clip(i - 1, 0, jnp.maximum(plan[PLAN_COUNT, 0] - 2, 0)),) + (0,) * len(shape)

        return pl.BlockSpec((1,) + shape, index)

    half = (ROWS // 2, 128)
    return pl.pallas_call(
        combine_kernel,
        grid_spec=pltpu.PrefetchScalarGridSpec(
            num_scalar_prefetch=1,
            grid=(n,),
            in_specs=[SMEM_SPEC]
            + [whole_spec(v.shape) for v in (parts, more, deriv0, grad0)]
            + [rest_spec(v.shape[1:]) for v in (deriv, grad)],
            out_specs=[whole_spec(half), whole_spec(half), whole_spec(TALLY.shape)],
            scratch_shapes=[
                pltpu.VMEM((ROWS, 128), F32),
                pltpu.VMEM((G_ROWS, 128), F32),
                pltpu.VMEM((2, 8, 128), F32),
                pltpu.VMEM((128, 128), F32),
            ],
        ),
        out_shape=[jax.ShapeDtypeStruct(half, F32), jax.ShapeDtypeStruct(half, F32), TALLY],
        compiler_params=LIMIT,
        name="combine",
    )(plan, core, parts, more, deriv0, grad0, deriv, grad)


def adam_step(params, first_moment, second_moment, unit):
    new_first = 0.9 * first_moment + 0.1 * unit
    new_second = 0.999 * second_moment + 0.001 * unit * unit
    unbiased_first = new_first / (1.0 - 0.9**10)
    unbiased_second = new_second / (1.0 - 0.999**10)
    new_params = params - 0.01 * unbiased_first / (jnp.sqrt(unbiased_second) + 1e-08)
    return (new_params, new_first, new_second)


def swap_cores(v):
    return lax.ppermute(v, "core", [(0, 1), (1, 0)])


def gather_tallies(v):
    own = lax.all_to_all(v, PLANE + ("z",), 0, 0, tiled=True)
    return own, swap_cores(own)


def to_all(v, axes, size):
    return lax.all_to_all(jnp.broadcast_to(v[None], (size,) + v.shape), axes, 0, 0, tiled=True)


def sum_large(mine, other, core):
    half = mine.shape[0]
    piece = half // PLANE_CHIPS
    own = mine + swap_cores(other)
    own = jnp.sum(lax.all_to_all(own.reshape(PLANE_CHIPS, piece, 128), PLANE, 0, 0, tiled=True), axis=0)
    own = jnp.sum(to_all(own, "z", DEPTH), axis=0)
    own = to_all(own, PLANE, PLANE_CHIPS).reshape(half, 128)
    other = swap_cores(own)
    first = core == 0
    return jnp.concatenate([jnp.where(first, own, other), jnp.where(first, other, own)], axis=0)


def on_device(
    params, first_moment, second_moment, positions, species, neighbours, window_of, frame_count
):
    n = positions.shape[0]
    core = lax.axis_index("core")
    own, send = run_pack(frame_count, window_of, positions, species, neighbours)
    here = lax.all_to_all(send, PLANE, 0, 0, tiled=True)
    theta = jnp.pad(params, (0, ROWS * 128 - NPAR)).reshape(ROWS, 128)
    held, deriv0, grad0, tally = run_first(theta, own)
    here, tally = lax.optimization_barrier((here, tally))
    there = swap_cores(here)
    plan = run_deal((core * PLANE_CHIPS + lax.axis_index(PLANE))[None], here, there)
    here, there = (v.reshape(PLANE_CHIPS * (n - KEEP), FRAME_ROWS, 128) for v in (here, there))
    deriv, grad, tally = run_rest(plan, own, here, there, tally, held)
    mine, other, means = run_combine(plan, core[None], *gather_tallies(tally), deriv0, grad0, deriv, grad, n)
    summed = sum_large(mine, other, core).reshape(-1)[:NPAR]
    norm = jnp.sqrt(jnp.sum(summed * summed))
    unit = summed * (GRAD_SCALE * math.sqrt(NPAR) / (norm + 1e-06))
    new_params, new_first, new_second = adam_step(params, first_moment, second_moment, unit)
    return (new_params, new_first, new_second, means[0, :WINDOWS])


def solution(mesh):
    axes = tuple(AXES)
    split = Mesh(mesh.devices.reshape(tuple(AXES.values())), axes)
    in_specs = (
        P(),
        P(),
        P(),
        P(axes, None, None),
        P(axes, None),
        P(axes, None, None),
        P(axes),
        P(axes),
    )
    out_specs = (P(), P(), P(), P())
    return jax.shard_map(
        on_device, mesh=split, in_specs=in_specs, out_specs=out_specs, check_vma=False
    )
```

time: 143 us -> 136 us (0.951)
  Pallas kernels: 53.3 us -> 44.9 us
  blocking collectives: 56.6 us -> 59.1 us
    pallas_call x1, Pallas kernels: 15.9 us -> 5.24 us  [run_combine(): pl.pallas_call(combine_kernel, grid_spec=pltpu.PrefetchScalarGridSpec(num...]
    all_to_all x1, blocking collectives: 23.7 us -> 25.8 us  [gather_tallies(): own = lax.all_to_all(v, PLANE + ('z',), 0, 0, tiled=True)]
    pallas_call x1, Pallas kernels: 9.84 us -> 11.9 us  [run_first(): pl.pallas_call(first_kernel, grid=(1,), in_specs=[whole_spec((ROWS, 128))...]
  transfers between devices with their start and end apart: 5 -> 5, of which waited for: 5 -> 4; matrix products, arithmetic and copies ran while one was open for 2% -> 2% of each run, Pallas kernels for 7% -> 9%
where the time goes in v4:
time: 136 us; the launch traced here: 135 us
  blocking collectives  59.1 us (43%)
  Pallas kernels  44.9 us (33%)
  starting transfers between devices  16.5 us (12%)
  local copies, waits for them, and re-layouts  4.75 us (3%)
  waiting for transfers between devices  4.35 us (3%)
  other arithmetic  3.46 us (3%)
  between operations  2.11 us (2%)
    all_to_all x1, blocking collectives, gather_tallies(): own = lax.all_to_all(v, PLANE + ('z',), 0, 0, tiled=True)  25.8 us
    pallas_call x1, Pallas kernels, run_rest(): pl.pallas_call(rest_kernel, grid_spec=pltpu.PrefetchScalarGridSpec(num_sc...  23.9 us
    all_to_all x2, blocking collectives, to_all(): lax.all_to_all(jnp.broadcast_to(v[None], (size,) + v.shape), axes, 0, 0,...  22.3 us
    pallas_call x1, Pallas kernels, run_first(): pl.pallas_call(first_kernel, grid=(1,), in_specs=[whole_spec((ROWS, 128))...  11.9 us
    all_to_all x1, blocking collectives, sum_large(): lax.all_to_all(own.reshape(PLANE_CHIPS, piece, 128), PLANE, 0, 0, tiled=T...  11 us
    ppermute x4, starting transfers between devices, swap_cores(): return lax.ppermute(v, 'core', [(0, 1), (1, 0)])  8.87 us
    all_to_all x1, starting transfers between devices, on_device(): here = lax.all_to_all(send, PLANE, 0, 0, tiled=True)  7.58 us
    pallas_call x1, Pallas kernels, run_combine(): pl.pallas_call(combine_kernel, grid_spec=pltpu.PrefetchScalarGridSpec(num...  5.24 us
  transfers between devices with their start and end apart: 5, of which 4 were waited for; matrix products, arithmetic and copies ran while one was open for 2% of the time, Pallas kernels for 9%

profile of v4, /device:TPU:1, one launch (start us, length us, event | category | flops | bytes accessed | tf_op | source)
XLA Modules:
  0.0 135.1 jit_solution(1802818396655320727)
XLA Ops:
  1.3 1.9 %pack.1 = (f32[8,24,128]{2,1,0:T(8,128)}, f32[16,96,128]{2,1,0:T(8,128)}) custom-call(s32[1]{0:T(128)S(6)} %copy.14.count_ref, s32[8]{0:T(128)} %window_ref.1, f32[3,8,128]{2,1,0:T(8,128)} %bitcast.30, s32[8,128]{1,0:T(8,128)} %spc_ref.1, s32[8,16,128]{2,1,0:T(8,128)} %nb_ref.1), custom_call_target="tpu_custom_call" | custom-call | tf_op jit(solution)/shard_map/pack/pallas_call | solution.py:633
  3.1 7.6 %all-to-all-start = ((f32[16,96,128]{2,1,0:T(8,128)}), f32[16,96,128]{2,1,0:T(8,128)S(1)}, u32[]{:S(2)}, u32[]{:S(2)}) async-start(f32[16,96,128]{2,1,0:T(8,128)} %get-tuple-element.31), calls=%async_computation | async-start | bytes 1572864 | tf_op jit(solution)/shard_map/all_to_all | solution.py:780
  10.7 2.0 %pad_bitcast_fusion.th_ref = f32[1280,128]{1,0:T(8,128)} fusion(f32[160272]{0:T(1024)} %param.8), kind=kLoop, calls=%fused_computation.2 | loop fusion | bytes 1296448 | tf_op jit(solution)/shard_map/reshape | solution.py:781
  12.7 11.9 %first_frame.1 = (bf16[2,64,48]{2,1,0:T(8,128)(2,1)}, bf16[2,64,192]{2,1,0:T(8,128)(2,1)}, bf16[2,128,192]{2,1,0:T(8,128)(2,1)}, bf16[2,128,384]{2,1,0:T(8,128)(...) custom-call(f32[1280,128]{1,0:T(8,128)} %pad_bitcast_fusion.th_ref, ...), custom_call_target="tpu_custom_call" | custom-call | flops 1000000000 | bytes 40000000 | tf_op jit(solution)/shard_map/first_frame/pallas_call | solution.py:660
  24.6 1.4 %collective-permute-start = (f32[16,96,128]{2,1,0:T(8,128)S(1)}, f32[16,96,128]{2,1,0:T(8,128)S(1)}, u32[]{:S(2)}, u32[]{:S(2)}) collective-permute-start(f32[16,96,128]{2,1,0:T(8,128)S(1)} %all-to-all-done.here_ref), channel_id=1, source_target_pairs={{0,1},{1,0},{2,3},{3,2},{4,5},{5,4},{6,7},{7,6},{8,9},{9,8},{10,11... | collective-permute-start | bytes 2359304 | tf_op jit(solution)/shard_map/ppermute | solution.py:750
  26.1 1.9 %collective-permute-done.there_ref = f32[16,96,128]{2,1,0:T(8,128)S(1)} collective-permute-done((f32[16,96,128]{2,1,0:T(8,128)S(1)}, f32[16,96,128]{2,1,0:T(8,128)S(1)}, u32[]{:S(2)}, u32[]{:S(2)}) %collective-permute-start) | collective-permute-done | bytes 786464 | tf_op jit(solution)/shard_map/ppermute | solution.py:750
  28.0 0.9 copy-done.1
  28.9 1.9 %deal.1.plan_ref = s32[16,128]{1,0:T(8,128)} custom-call(s32[1]{0:T(128)} %bitcast.me_ref, f32[16,96,128]{2,1,0:T(8,128)} %copy-done, f32[16,96,128]{2,1,0:T(8,128)} %copy-done.1), custom_call_target="tpu_custom_call" | custom-call | tf_op jit(solution)/shard_map/deal/pallas_call | solution.py:647
  30.8 23.9 %other_frames.1 = (f32[9,8,128]{2,1,0:T(8,128)}, f32[9,2,1384,128]{3,2,1,0:T(8,128)}, f32[128,128]{1,0:T(8,128)}) custom-call(s32[16,128]{1,0:T(8,128)} %deal.1.plan_ref, f32[8,24,128]{2,1,0:T(8,128)} %get-tuple-element.32.own_ref, f32[64,24,128]{2,1,0:T(8,128)} %bitcast.19, f32[64,24,128]{2,1,0:T(8,128)} %bitcast.20, f32[64,24,128]{2,1,0:T(8,128)} %bitcast.21, ...), custom_call_target="tpu_custom_call" | custom-call | tf_op jit(solution)/shard_map/other_frames/pallas_call | solution.py:691
  54.7 25.8 %all_to_all.31 = f32[128,1,128]{2,1,0:T(1,128)S(1)} all-to-all(f32[128,1,128]{2,1,0:T(1,128)} %bitcast.29), channel_id=1, replica_groups=mesh['x'=4,'y'=4,'z'=8,'core'=2] {'x','y','z'}, dimensions={0} | all-to-all | bytes 131072 | tf_op jit(solution)/shard_map/all_to_all | solution.py:754
  80.5 1.8 %collective-permute-start.1 = (f32[128,128]{1,0:T(8,128)S(1)}, f32[128,128]{1,0:T(8,128)S(1)}, u32[]{:S(2)}, u32[]{:S(2)}) collective-permute-start(f32[128,128]{1,0:T(8,128)S(1)} %bitcast.27), channel_id=1, source_target_pairs={{0,1},{1,0},{2,3},{3,2},{4,5},{5,4},{6,7},{7,6},{8,9},{9,8},{10,11... | collective-permute-start | bytes 196616 | tf_op jit(solution)/shard_map/ppermute | solution.py:750
  82.4 0.9 collective-permute-done.1.more_ref
  83.3 0.6 copy-done.6
  83.9 5.2 %combine.1 = (f32[640,128]{1,0:T(8,128)}, f32[640,128]{1,0:T(8,128)}, f32[8,128]{1,0:T(8,128)}) custom-call(s32[16,128]{1,0:T(8,128)} %deal.1.plan_ref, s32[1]{0:T(128)} %bitcast.3.core_ref, f32[128,128]{1,0:T(8,128)} %bitcast.28, f32[128,128]{1,0:T(8,128)} %copy-done.6, f32[1,8,128]{2,1,0:T(8,128)} %get-tuple-element.51.deriv0_ref, ...), custom_call_target="tpu_custom_call" | custom-call | tf_op jit(solution)/shard_map/combine/pallas_call | solution.py:718
  89.1 1.6 %collective-permute-start.2 = (f32[640,128]{1,0:T(8,128)}, f32[640,128]{1,0:T(8,128)S(1)}, u32[]{:S(2)}, u32[]{:S(2)}) collective-permute-start(f32[640,128]{1,0:T(8,128)} %get-tuple-element.56), channel_id=1, source_target_pairs={{0,1},{1,0},{2,3},{3,2},{4,5},{5,4},{6,7},{7,6},{8,9},{9,8},{10,11... | collective-permute-start | bytes 983048 | tf_op jit(solution)/shard_map/ppermute | solution.py:750
  90.8 1.5 %collective-permute-done.2 = f32[640,128]{1,0:T(8,128)S(1)} collective-permute-done((f32[640,128]{1,0:T(8,128)}, f32[640,128]{1,0:T(8,128)S(1)}, u32[]{:S(2)}, u32[]{:S(2)}) %collective-permute-start.2) | collective-permute-done | bytes 327712 | tf_op jit(solution)/shard_map/ppermute | solution.py:750
  92.2 1.0 add.28
  93.2 11.0 %all_to_all.32 = f32[16,40,128]{2,1,0:T(8,128)S(1)} all-to-all(f32[16,40,128]{2,1,0:T(8,128)S(1)} %bitcast.26), channel_id=1, replica_groups=mesh['x'=4,'y'=4,'z'=8,'core'=2] {'x','y'}, dimensions={0} | all-to-all | bytes 655360 | tf_op jit(solution)/shard_map/all_to_all | solution.py:766
  104.3 10.8 %all_to_all.33 = f32[8,40,128]{2,1,0:T(8,128)S(1)} all-to-all(f32[8,40,128]{2,1,0:T(8,128)S(1)} %broadcast_in_dim.20), channel_id=1, replica_groups=mesh['x'=4,'y'=4,'z'=8,'core'=2] {'z'}, dimensions={0} | all-to-all | bytes 327680 | tf_op jit(solution)/shard_map/all_to_all | solution.py:759
  115.1 11.5 %all_to_all.34 = f32[16,40,128]{2,1,0:T(8,128)S(1)} all-to-all(f32[16,40,128]{2,1,0:T(8,128)S(1)} %broadcast_in_dim.21), channel_id=1, replica_groups=mesh['x'=4,'y'=4,'z'=8,'core'=2] {'x','y'}, dimensions={0} | all-to-all | bytes 655360 | tf_op jit(solution)/shard_map/all_to_all | solution.py:759
  126.7 4.0 %collective-permute-start.3 = (f32[640,128]{1,0:T(8,128)S(1)}, f32[640,128]{1,0:T(8,128)S(1)}, u32[]{:S(2)}, u32[]{:S(2)}) collective-permute-start(f32[640,128]{1,0:T(8,128)S(1)} %bitcast.25), channel_id=1, source_target_pairs={{0,1},{1,0},{2,3},{3,2},{4,5},{5,4},{6,7},{7,6},{8,9},{9,8},{10,11... | collective-permute-start | bytes 983048 | tf_op jit(solution)/shard_map/ppermute | solution.py:750
  130.6 1.2 slice_bitcast_fusion
  132.0 0.8 multiply_reduce_fusion
  133.5 1.5 %divide_subtract_fusion = (f32[160272]{0:T(1024)}, f32[160272]{0:T(1024)}, f32[160272]{0:T(1024)}) fusion(f32[160272]{0:T(1024)S(1)} %copy-done.2, f32[]{:T(128)S(6)} %div.14, f32[163840]{0:T(1024)S(1)} %maximum_bitcast_fusion, f32[160272]{0:T(1024)S(1)} %copy-done.3, f32[160272]{0:T(1024)S(1)} %copy-done.4), kind=kLoop, calls=%fused_computation.4 | loop fusion | flops 2083536 | bytes 4487620 | tf_op jit(solution)/shard_map/sub | solution.py:745
  (20 shorter events, 0.3 us)
Async XLA Ops:
  3.1 21.5 %all-to-all-start = ((f32[16,96,128]{2,1,0:T(8,128)}), f32[16,96,128]{2,1,0:T(8,128)S(1)}, u32[]{:S(2)}, u32[]{:S(2)}) async-start(f32[16,96,128]{2,1,0:T(8,128)} %get-tuple-element.31), calls=%async_computation | async-start | bytes 1572864 | tf_op jit(solution)/shard_map/all_to_all | solution.py:780
  24.6 3.3 %copy-start = (f32[16,96,128]{2,1,0:T(8,128)}, f32[16,96,128]{2,1,0:T(8,128)S(1)}, u32[]{:S(2)}) copy-start(f32[16,96,128]{2,1,0:T(8,128)S(1)} %all-to-all-done.here_ref) | copy-start | bytes 2359300
  24.6 3.3 %collective-permute-start = (f32[16,96,128]{2,1,0:T(8,128)S(1)}, f32[16,96,128]{2,1,0:T(8,128)S(1)}, u32[]{:S(2)}, u32[]{:S(2)}) collective-permute-start(f32[16,96,128]{2,1,0:T(8,128)S(1)} %all-to-all-done.here_ref), channel_id=1, source_target_pairs={{0,1},{1,0},{2,3},{3,2},{4,5},{5,4},{6,7},{7,6},{8,9},{9,8},{10,11... | collective-permute-start | bytes 2359304 | tf_op jit(solution)/shard_map/ppermute | solution.py:750
  28.0 0.9 copy-start.1
  30.8 102.7 %copy-start.2 = (f32[160272]{0:T(1024)S(1)}, f32[160272]{0:T(1024)}, u32[]{:S(2)}) copy-start(f32[160272]{0:T(1024)} %param.8) | copy-start | bytes 1923268
  30.8 102.7 %copy-start.3 = (f32[160272]{0:T(1024)S(1)}, f32[160272]{0:T(1024)}, u32[]{:S(2)}) copy-start(f32[160272]{0:T(1024)} %param.9) | copy-start | bytes 1923268
  30.8 102.8 %copy-start.4 = (f32[160272]{0:T(1024)S(1)}, f32[160272]{0:T(1024)}, u32[]{:S(2)}) copy-start(f32[160272]{0:T(1024)} %param.10) | copy-start | bytes 1923268
  80.5 2.8 %copy-start.5 = (f32[128,1,128]{2,1,0:T(1,128)}, f32[128,1,128]{2,1,0:T(1,128)S(1)}, u32[]{:S(2)}) copy-start(f32[128,1,128]{2,1,0:T(1,128)S(1)} %all_to_all.31) | copy-start | bytes 196612
  80.5 2.8 %collective-permute-start.1 = (f32[128,128]{1,0:T(8,128)S(1)}, f32[128,128]{1,0:T(8,128)S(1)}, u32[]{:S(2)}, u32[]{:S(2)}) collective-permute-start(f32[128,128]{1,0:T(8,128)S(1)} %bitcast.27), channel_id=1, source_target_pairs={{0,1},{1,0},{2,3},{3,2},{4,5},{5,4},{6,7},{7,6},{8,9},{9,8},{10,11... | collective-permute-start | bytes 196616 | tf_op jit(solution)/shard_map/ppermute | solution.py:750
  83.3 0.6 copy-start.6
  89.1 3.1 %collective-permute-start.2 = (f32[640,128]{1,0:T(8,128)}, f32[640,128]{1,0:T(8,128)S(1)}, u32[]{:S(2)}, u32[]{:S(2)}) collective-permute-start(f32[640,128]{1,0:T(8,128)} %get-tuple-element.56), channel_id=1, source_target_pairs={{0,1},{1,0},{2,3},{3,2},{4,5},{5,4},{6,7},{7,6},{8,9},{9,8},{10,11... | collective-permute-start | bytes 983048 | tf_op jit(solution)/shard_map/ppermute | solution.py:750
  126.7 5.2 %collective-permute-start.3 = (f32[640,128]{1,0:T(8,128)S(1)}, f32[640,128]{1,0:T(8,128)S(1)}, u32[]{:S(2)}, u32[]{:S(2)}) collective-permute-start(f32[640,128]{1,0:T(8,128)S(1)} %bitcast.25), channel_id=1, source_target_pairs={{0,1},{1,0},{2,3},{3,2},{4,5},{5,4},{6,7},{7,6},{8,9},{9,8},{10,11... | collective-permute-start | bytes 983048 | tf_op jit(solution)/shard_map/ppermute | solution.py:750

commit v5 on v4

--- a/solution.py
+++ b/solution.py
@@ -623,6 +623,7 @@
 
 
 LIMIT = pltpu.CompilerParams(vmem_limit_bytes=56 * 2**20)
+SMALL_LIMIT = pltpu.CompilerParams(vmem_limit_bytes=4 * 2**20)
 
 
 TALLY = jax.ShapeDtypeStruct((8, 128), F32)
@@ -650,6 +651,7 @@
         in_specs=[SMEM_SPEC] + [pl.BlockSpec((PLANE_CHIPS, 8, 128), lambda i: (0, ROW_META // 8, 0))] * 2,
         out_specs=whole_spec((PLAN_ROWS, 128)),
         out_shape=jax.ShapeDtypeStruct((PLAN_ROWS, 128), jnp.int32),
+        compiler_params=SMALL_LIMIT,
         name="deal",
     )(me, here, there)
 

time: 136 us -> 134 us (0.985)
    pallas_call x1, Pallas kernels: 1.9 us -> 0.45 us  [run_deal(): pl.pallas_call(deal_kernel, grid=(1,), in_specs=[SMEM_SPEC] + [pl.BlockSp...]
where the time goes in v5:
time: 134 us; the launch traced here: 133 us
  blocking collectives  58.6 us (44%)
  Pallas kernels  44.7 us (33%)
  starting transfers between devices  15.7 us (12%)
  local copies, waits for them, and re-layouts  4.42 us (3%)
  waiting for transfers between devices  4.36 us (3%)
  other arithmetic  3.46 us (3%)
  between operations  2.13 us (2%)
    all_to_all x1, blocking collectives, gather_tallies(): own = lax.all_to_all(v, PLANE + ('z',), 0, 0, tiled=True)  25.8 us
    pallas_call x1, Pallas kernels, run_rest(): pl.pallas_call(rest_kernel, grid_spec=pltpu.PrefetchScalarGridSpec(num_sc...  24 us
    all_to_all x2, blocking collectives, to_all(): lax.all_to_all(jnp.broadcast_to(v[None], (size,) + v.shape), axes, 0, 0,...  21.6 us
    pallas_call x1, Pallas kernels, run_first(): pl.pallas_call(first_kernel, grid=(1,), in_specs=[whole_spec((ROWS, 128))...  11.9 us
    all_to_all x1, blocking collectives, sum_large(): lax.all_to_all(own.reshape(PLANE_CHIPS, piece, 128), PLANE, 0, 0, tiled=T...  11.2 us
    ppermute x4, starting transfers between devices, swap_cores(): return lax.ppermute(v, 'core', [(0, 1), (1, 0)])  8.13 us
    all_to_all x1, starting transfers between devices, on_device(): here = lax.all_to_all(send, PLANE, 0, 0, tiled=True)  7.58 us
    pallas_call x1, Pallas kernels, run_combine(): pl.pallas_call(combine_kernel, grid_spec=pltpu.PrefetchScalarGridSpec(num...  6.51 us
  transfers between devices with their start and end apart: 5, of which 4 were waited for; matrix products, arithmetic and copies ran while one was open for 2% of the time, Pallas kernels for 9%

profile of v5, /device:TPU:1, one launch (start us, length us, event | category | flops | bytes accessed | tf_op | source)
XLA Modules:
  0.0 133.4 jit_solution(12568744346271082690)
XLA Ops:
  1.3 1.9 %pack.1 = (f32[8,24,128]{2,1,0:T(8,128)}, f32[16,96,128]{2,1,0:T(8,128)}) custom-call(s32[1]{0:T(128)S(6)} %copy.14.count_ref, s32[8]{0:T(128)} %window_ref.1, f32[3,8,128]{2,1,0:T(8,128)} %bitcast.30, s32[8,128]{1,0:T(8,128)} %spc_ref.1, s32[8,16,128]{2,1,0:T(8,128)} %nb_ref.1), custom_call_target="tpu_custom_call" | custom-call | tf_op jit(solution)/shard_map/pack/pallas_call | solution.py:634
  3.2 7.6 %all-to-all-start = ((f32[16,96,128]{2,1,0:T(8,128)}), f32[16,96,128]{2,1,0:T(8,128)S(1)}, u32[]{:S(2)}, u32[]{:S(2)}) async-start(f32[16,96,128]{2,1,0:T(8,128)} %get-tuple-element.31), calls=%async_computation | async-start | bytes 1572864 | tf_op jit(solution)/shard_map/all_to_all | solution.py:782
  10.7 2.0 %pad_bitcast_fusion.th_ref = f32[1280,128]{1,0:T(8,128)} fusion(f32[160272]{0:T(1024)} %param.8), kind=kLoop, calls=%fused_computation.2 | loop fusion | bytes 1296448 | tf_op jit(solution)/shard_map/reshape | solution.py:783
  12.7 11.9 %first_frame.1 = (bf16[2,64,48]{2,1,0:T(8,128)(2,1)}, bf16[2,64,192]{2,1,0:T(8,128)(2,1)}, bf16[2,128,192]{2,1,0:T(8,128)(2,1)}, bf16[2,128,384]{2,1,0:T(8,128)(...) custom-call(f32[1280,128]{1,0:T(8,128)} %pad_bitcast_fusion.th_ref, ...), custom_call_target="tpu_custom_call" | custom-call | flops 1000000000 | bytes 40000000 | tf_op jit(solution)/shard_map/first_frame/pallas_call | solution.py:662
  24.6 1.4 %collective-permute-start = (f32[16,96,128]{2,1,0:T(8,128)S(1)}, f32[16,96,128]{2,1,0:T(8,128)S(1)}, u32[]{:S(2)}, u32[]{:S(2)}) collective-permute-start(f32[16,96,128]{2,1,0:T(8,128)S(1)} %all-to-all-done.here_ref), channel_id=1, source_target_pairs={{0,1},{1,0},{2,3},{3,2},{4,5},{5,4},{6,7},{7,6},{8,9},{9,8},{10,11... | collective-permute-start | bytes 2359304 | tf_op jit(solution)/shard_map/ppermute | solution.py:752
  26.1 1.9 %collective-permute-done.there_ref = f32[16,96,128]{2,1,0:T(8,128)S(1)} collective-permute-done((f32[16,96,128]{2,1,0:T(8,128)S(1)}, f32[16,96,128]{2,1,0:T(8,128)S(1)}, u32[]{:S(2)}, u32[]{:S(2)}) %collective-permute-start) | collective-permute-done | bytes 786464 | tf_op jit(solution)/shard_map/ppermute | solution.py:752
  28.0 0.5 deal.1.plan_ref
  28.4 0.6 copy-done.2
  29.1 24.0 %other_frames.1 = (f32[9,8,128]{2,1,0:T(8,128)}, f32[9,2,1384,128]{3,2,1,0:T(8,128)}, f32[128,128]{1,0:T(8,128)}) custom-call(s32[16,128]{1,0:T(8,128)} %copy-done.2, f32[8,24,128]{2,1,0:T(8,128)} %get-tuple-element.32.own_ref, f32[64,24,128]{2,1,0:T(8,128)} %bitcast.19, f32[64,24,128]{2,1,0:T(8,128)} %bitcast.20, f32[64,24,128]{2,1,0:T(8,128)} %bitcast.21, ...), custom_call_target="tpu_custom_call" | custom-call | tf_op jit(solution)/shard_map/other_frames/pallas_call | solution.py:693
  53.0 25.8 %all_to_all.31 = f32[128,1,128]{2,1,0:T(1,128)S(1)} all-to-all(f32[128,1,128]{2,1,0:T(1,128)} %bitcast.29), channel_id=1, replica_groups=mesh['x'=4,'y'=4,'z'=8,'core'=2] {'x','y','z'}, dimensions={0} | all-to-all | bytes 131072 | tf_op jit(solution)/shard_map/all_to_all | solution.py:756
  78.8 1.9 %collective-permute-start.1 = (f32[128,128]{1,0:T(8,128)S(1)}, f32[128,128]{1,0:T(8,128)S(1)}, u32[]{:S(2)}, u32[]{:S(2)}) collective-permute-start(f32[128,128]{1,0:T(8,128)S(1)} %bitcast.27), channel_id=1, source_target_pairs={{0,1},{1,0},{2,3},{3,2},{4,5},{5,4},{6,7},{7,6},{8,9},{9,8},{10,11... | collective-permute-start | bytes 196616 | tf_op jit(solution)/shard_map/ppermute | solution.py:752
  80.7 0.9 collective-permute-done.1.more_ref
  81.6 0.6 copy-done.7
  82.2 6.5 %combine.1 = (f32[640,128]{1,0:T(8,128)}, f32[640,128]{1,0:T(8,128)}, f32[8,128]{1,0:T(8,128)}) custom-call(s32[16,128]{1,0:T(8,128)} %copy-done.2, s32[1]{0:T(128)} %bitcast.3.core_ref, f32[128,128]{1,0:T(8,128)} %bitcast.28, f32[128,128]{1,0:T(8,128)} %copy-done.7, f32[1,8,128]{2,1,0:T(8,128)} %get-tuple-element.51.deriv0_ref, ...), custom_call_target="tpu_custom_call" | custom-call | tf_op jit(solution)/shard_map/combine/pallas_call | solution.py:720
  88.7 0.8 collective-permute-start.2
  89.5 1.5 %collective-permute-done.2 = f32[640,128]{1,0:T(8,128)S(1)} collective-permute-done((f32[640,128]{1,0:T(8,128)}, f32[640,128]{1,0:T(8,128)S(1)}, u32[]{:S(2)}, u32[]{:S(2)}) %collective-permute-start.2) | collective-permute-done | bytes 327712 | tf_op jit(solution)/shard_map/ppermute | solution.py:752
  91.0 1.0 add.28
  92.0 11.2 %all_to_all.32 = f32[16,40,128]{2,1,0:T(8,128)S(1)} all-to-all(f32[16,40,128]{2,1,0:T(8,128)S(1)} %bitcast.26), channel_id=1, replica_groups=mesh['x'=4,'y'=4,'z'=8,'core'=2] {'x','y'}, dimensions={0} | all-to-all | bytes 655360 | tf_op jit(solution)/shard_map/all_to_all | solution.py:768
  103.3 10.7 %all_to_all.33 = f32[8,40,128]{2,1,0:T(8,128)S(1)} all-to-all(f32[8,40,128]{2,1,0:T(8,128)S(1)} %broadcast_in_dim.20), channel_id=1, replica_groups=mesh['x'=4,'y'=4,'z'=8,'core'=2] {'z'}, dimensions={0} | all-to-all | bytes 327680 | tf_op jit(solution)/shard_map/all_to_all | solution.py:761
  114.0 10.9 %all_to_all.34 = f32[16,40,128]{2,1,0:T(8,128)S(1)} all-to-all(f32[16,40,128]{2,1,0:T(8,128)S(1)} %broadcast_in_dim.21), channel_id=1, replica_groups=mesh['x'=4,'y'=4,'z'=8,'core'=2] {'x','y'}, dimensions={0} | all-to-all | bytes 655360 | tf_op jit(solution)/shard_map/all_to_all | solution.py:761
  125.0 4.0 %collective-permute-start.3 = (f32[640,128]{1,0:T(8,128)S(1)}, f32[640,128]{1,0:T(8,128)S(1)}, u32[]{:S(2)}, u32[]{:S(2)}) collective-permute-start(f32[640,128]{1,0:T(8,128)S(1)} %bitcast.25), channel_id=1, source_target_pairs={{0,1},{1,0},{2,3},{3,2},{4,5},{5,4},{6,7},{7,6},{8,9},{9,8},{10,11... | collective-permute-start | bytes 983048 | tf_op jit(solution)/shard_map/ppermute | solution.py:752
  129.0 1.2 slice_bitcast_fusion
  130.3 0.8 multiply_reduce_fusion
  131.9 1.5 %divide_subtract_fusion = (f32[160272]{0:T(1024)}, f32[160272]{0:T(1024)}, f32[160272]{0:T(1024)}) fusion(f32[160272]{0:T(1024)S(1)} %copy-done.3, f32[]{:T(128)S(6)} %div.14, f32[163840]{0:T(1024)S(1)} %maximum_bitcast_fusion, f32[160272]{0:T(1024)S(1)} %copy-done.4, f32[160272]{0:T(1024)S(1)} %copy-done.5), kind=kLoop, calls=%fused_computation.4 | loop fusion | flops 2083536 | bytes 4487620 | tf_op jit(solution)/shard_map/sub | solution.py:747
  (22 shorter events, 0.3 us)
Async XLA Ops:
  3.2 21.5 %all-to-all-start = ((f32[16,96,128]{2,1,0:T(8,128)}), f32[16,96,128]{2,1,0:T(8,128)S(1)}, u32[]{:S(2)}, u32[]{:S(2)}) async-start(f32[16,96,128]{2,1,0:T(8,128)} %get-tuple-element.31), calls=%async_computation | async-start | bytes 1572864 | tf_op jit(solution)/shard_map/all_to_all | solution.py:782
  24.6 4.4 %copy-start = (f32[16,96,128]{2,1,0:T(8,128)}, f32[16,96,128]{2,1,0:T(8,128)S(1)}, u32[]{:S(2)}) copy-start(f32[16,96,128]{2,1,0:T(8,128)S(1)} %all-to-all-done.here_ref) | copy-start | bytes 2359300
  24.6 3.3 %collective-permute-start = (f32[16,96,128]{2,1,0:T(8,128)S(1)}, f32[16,96,128]{2,1,0:T(8,128)S(1)}, u32[]{:S(2)}, u32[]{:S(2)}) collective-permute-start(f32[16,96,128]{2,1,0:T(8,128)S(1)} %all-to-all-done.here_ref), channel_id=1, source_target_pairs={{0,1},{1,0},{2,3},{3,2},{4,5},{5,4},{6,7},{7,6},{8,9},{9,8},{10,11... | collective-permute-start | bytes 2359304 | tf_op jit(solution)/shard_map/ppermute | solution.py:752
  28.0 1.1 copy-start.1
  28.4 0.6 copy-start.2
  29.0 102.8 %copy-start.3 = (f32[160272]{0:T(1024)S(1)}, f32[160272]{0:T(1024)}, u32[]{:S(2)}) copy-start(f32[160272]{0:T(1024)} %param.8) | copy-start | bytes 1923268
  29.0 102.8 %copy-start.4 = (f32[160272]{0:T(1024)S(1)}, f32[160272]{0:T(1024)}, u32[]{:S(2)}) copy-start(f32[160272]{0:T(1024)} %param.9) | copy-start | bytes 1923268
  29.0 102.8 %copy-start.5 = (f32[160272]{0:T(1024)S(1)}, f32[160272]{0:T(1024)}, u32[]{:S(2)}) copy-start(f32[160272]{0:T(1024)} %param.10) | copy-start | bytes 1923268
  78.8 2.8 %copy-start.6 = (f32[128,1,128]{2,1,0:T(1,128)}, f32[128,1,128]{2,1,0:T(1,128)S(1)}, u32[]{:S(2)}) copy-start(f32[128,1,128]{2,1,0:T(1,128)S(1)} %all_to_all.31) | copy-start | bytes 196612
  78.8 2.8 %collective-permute-start.1 = (f32[128,128]{1,0:T(8,128)S(1)}, f32[128,128]{1,0:T(8,128)S(1)}, u32[]{:S(2)}, u32[]{:S(2)}) collective-permute-start(f32[128,128]{1,0:T(8,128)S(1)} %bitcast.27), channel_id=1, source_target_pairs={{0,1},{1,0},{2,3},{3,2},{4,5},{5,4},{6,7},{7,6},{8,9},{9,8},{10,11... | collective-permute-start | bytes 196616 | tf_op jit(solution)/shard_map/ppermute | solution.py:752
  81.6 0.6 copy-start.7
  88.7 2.3 %collective-permute-start.2 = (f32[640,128]{1,0:T(8,128)}, f32[640,128]{1,0:T(8,128)S(1)}, u32[]{:S(2)}, u32[]{:S(2)}) collective-permute-start(f32[640,128]{1,0:T(8,128)} %get-tuple-element.56), channel_id=1, source_target_pairs={{0,1},{1,0},{2,3},{3,2},{4,5},{5,4},{6,7},{7,6},{8,9},{9,8},{10,11... | collective-permute-start | bytes 983048 | tf_op jit(solution)/shard_map/ppermute | solution.py:752
  125.0 5.3 %collective-permute-start.3 = (f32[640,128]{1,0:T(8,128)S(1)}, f32[640,128]{1,0:T(8,128)S(1)}, u32[]{:S(2)}, u32[]{:S(2)}) collective-permute-start(f32[640,128]{1,0:T(8,128)S(1)} %bitcast.25), channel_id=1, source_target_pairs={{0,1},{1,0},{2,3},{3,2},{4,5},{5,4},{6,7},{7,6},{8,9},{9,8},{10,11... | collective-permute-start | bytes 983048 | tf_op jit(solution)/shard_map/ppermute | solution.py:752

commit v6 on v5

--- a/solution.py
+++ b/solution.py
@@ -618,11 +618,12 @@
         pltpu.VMEM((n, LAYERS, 2, HID, EDGES), BF16),
         pltpu.VMEM((n, C, EDGES), F32),
         pltpu.VMEM((n, 2, C, EDGES), BF16),
-        pltpu.VMEM((n, NB * K, ATOMS), F32),
+        pltpu.VMEM((n, NB * K + K, ATOMS), F32),
     ]
 
 
 LIMIT = pltpu.CompilerParams(vmem_limit_bytes=56 * 2**20)
+COMBINE_LIMIT = pltpu.CompilerParams(vmem_limit_bytes=54 * 2**20)
 SMALL_LIMIT = pltpu.CompilerParams(vmem_limit_bytes=4 * 2**20)
 
 
@@ -664,7 +665,7 @@
         grid=(1,),
         in_specs=[whole_spec((ROWS, 128)), whole_spec((1, FRAME_ROWS, 128))],
         out_specs=[whole_spec(s) for s, _ in shapes],
-        scratch_shapes=[pltpu.VMEM((128, 128), F32)] + frame_scratch(1),
+        scratch_shapes=[pltpu.VMEM((136, 128), F32)] + frame_scratch(1),
         out_shape=[jax.ShapeDtypeStruct(s, t) for s, t in shapes],
         compiler_params=LIMIT,
         cost_estimate=pl.CostEstimate(flops=10**9, bytes_accessed=4 * 10**7, transcendentals=10**6),
@@ -730,11 +731,11 @@
                 pltpu.VMEM((ROWS, 128), F32),
                 pltpu.VMEM((G_ROWS, 128), F32),
                 pltpu.VMEM((2, 8, 128), F32),
-                pltpu.VMEM((128, 128), F32),
+                pltpu.VMEM((136, 128), F32),
             ],
         ),
         out_shape=[jax.ShapeDtypeStruct(half, F32), jax.ShapeDtypeStruct(half, F32), TALLY],
-        compiler_params=LIMIT,
+        compiler_params=COMBINE_LIMIT,
         name="combine",
     )(plan, core, parts, more, deriv0, grad0, deriv, grad)
 

time: 134 us -> 134 us (level)
  no operation moved by 1% of the time
where the time goes in v6:
time: 134 us; the launch traced here: 133 us
  blocking collectives  59.1 us (44%)
  Pallas kernels  44.7 us (33%)
  starting transfers between devices  15.1 us (11%)
  local copies, waits for them, and re-layouts  4.42 us (3%)
  waiting for transfers between devices  4.38 us (3%)
  other arithmetic  3.46 us (3%)
  between operations  2.13 us (2%)
    all_to_all x1, blocking collectives, gather_tallies(): own = lax.all_to_all(v, PLANE + ('z',), 0, 0, tiled=True)  25.9 us
    pallas_call x1, Pallas kernels, run_rest(): pl.pallas_call(rest_kernel, grid_spec=pltpu.PrefetchScalarGridSpec(num_sc...  24 us
    all_to_all x2, blocking collectives, to_all(): lax.all_to_all(jnp.broadcast_to(v[None], (size,) + v.shape), axes, 0, 0,...  22.3 us
    pallas_call x1, Pallas kernels, run_first(): pl.pallas_call(first_kernel, grid=(1,), in_specs=[whole_spec((ROWS, 128))...  11.9 us
    all_to_all x1, blocking collectives, sum_large(): lax.all_to_all(own.reshape(PLANE_CHIPS, piece, 128), PLANE, 0, 0, tiled=T...  11 us
    all_to_all x1, starting transfers between devices, on_device(): here = lax.all_to_all(send, PLANE, 0, 0, tiled=True)  7.58 us
    ppermute x4, starting transfers between devices, swap_cores(): return lax.ppermute(v, 'core', [(0, 1), (1, 0)])  7.54 us
    pallas_call x1, Pallas kernels, run_combine(): pl.pallas_call(combine_kernel, grid_spec=pltpu.PrefetchScalarGridSpec(num...  6.51 us
  transfers between devices with their start and end apart: 5, of which 4 were waited for; matrix products, arithmetic and copies ran while one was open for 2% of the time, Pallas kernels for 9%

profile of v6, /device:TPU:1, one launch (start us, length us, event | category | flops | bytes accessed | tf_op | source)
XLA Modules:
  0.0 133.4 jit_solution(6536827564142779917)
XLA Ops:
  1.3 1.9 %pack.1 = (f32[8,24,128]{2,1,0:T(8,128)}, f32[16,96,128]{2,1,0:T(8,128)}) custom-call(s32[1]{0:T(128)S(6)} %copy.14.count_ref, s32[8]{0:T(128)} %window_ref.1, f32[3,8,128]{2,1,0:T(8,128)} %bitcast.30, s32[8,128]{1,0:T(8,128)} %spc_ref.1, s32[8,16,128]{2,1,0:T(8,128)} %nb_ref.1), custom_call_target="tpu_custom_call" | custom-call | tf_op jit(solution)/shard_map/pack/pallas_call | solution.py:635
  3.2 7.6 %all-to-all-start = ((f32[16,96,128]{2,1,0:T(8,128)}), f32[16,96,128]{2,1,0:T(8,128)S(1)}, u32[]{:S(2)}, u32[]{:S(2)}) async-start(f32[16,96,128]{2,1,0:T(8,128)} %get-tuple-element.31), calls=%async_computation | async-start | bytes 1572864 | tf_op jit(solution)/shard_map/all_to_all | solution.py:783
  10.7 2.0 %pad_bitcast_fusion.th_ref = f32[1280,128]{1,0:T(8,128)} fusion(f32[160272]{0:T(1024)} %param.8), kind=kLoop, calls=%fused_computation.2 | loop fusion | bytes 1296448 | tf_op jit(solution)/shard_map/reshape | solution.py:784
  12.7 11.9 %first_frame.1 = (bf16[2,64,48]{2,1,0:T(8,128)(2,1)}, bf16[2,64,192]{2,1,0:T(8,128)(2,1)}, bf16[2,128,192]{2,1,0:T(8,128)(2,1)}, bf16[2,128,384]{2,1,0:T(8,128)(...) custom-call(f32[1280,128]{1,0:T(8,128)} %pad_bitcast_fusion.th_ref, ...), custom_call_target="tpu_custom_call" | custom-call | flops 1000000000 | bytes 40000000 | tf_op jit(solution)/shard_map/first_frame/pallas_call | solution.py:663
  24.6 1.4 %collective-permute-start = (f32[16,96,128]{2,1,0:T(8,128)S(1)}, f32[16,96,128]{2,1,0:T(8,128)S(1)}, u32[]{:S(2)}, u32[]{:S(2)}) collective-permute-start(f32[16,96,128]{2,1,0:T(8,128)S(1)} %all-to-all-done.here_ref), channel_id=1, source_target_pairs={{0,1},{1,0},{2,3},{3,2},{4,5},{5,4},{6,7},{7,6},{8,9},{9,8},{10,11... | collective-permute-start | bytes 2359304 | tf_op jit(solution)/shard_map/ppermute | solution.py:753
  26.1 1.9 %collective-permute-done.there_ref = f32[16,96,128]{2,1,0:T(8,128)S(1)} collective-permute-done((f32[16,96,128]{2,1,0:T(8,128)S(1)}, f32[16,96,128]{2,1,0:T(8,128)S(1)}, u32[]{:S(2)}, u32[]{:S(2)}) %collective-permute-start) | collective-permute-done | bytes 786464 | tf_op jit(solution)/shard_map/ppermute | solution.py:753
  28.0 0.5 deal.1.plan_ref
  28.4 0.6 copy-done.2
  29.1 24.0 %other_frames.1 = (f32[9,8,128]{2,1,0:T(8,128)}, f32[9,2,1384,128]{3,2,1,0:T(8,128)}, f32[128,128]{1,0:T(8,128)}) custom-call(s32[16,128]{1,0:T(8,128)} %copy-done.2, f32[8,24,128]{2,1,0:T(8,128)} %get-tuple-element.32.own_ref, f32[64,24,128]{2,1,0:T(8,128)} %bitcast.19, f32[64,24,128]{2,1,0:T(8,128)} %bitcast.20, f32[64,24,128]{2,1,0:T(8,128)} %bitcast.21, ...), custom_call_target="tpu_custom_call" | custom-call | tf_op jit(solution)/shard_map/other_frames/pallas_call | solution.py:694
  53.0 25.9 %all_to_all.31 = f32[128,1,128]{2,1,0:T(1,128)S(1)} all-to-all(f32[128,1,128]{2,1,0:T(1,128)} %bitcast.29), channel_id=1, replica_groups=mesh['x'=4,'y'=4,'z'=8,'core'=2] {'x','y','z'}, dimensions={0} | all-to-all | bytes 131072 | tf_op jit(solution)/shard_map/all_to_all | solution.py:757
  78.9 1.8 %collective-permute-start.1 = (f32[128,128]{1,0:T(8,128)S(1)}, f32[128,128]{1,0:T(8,128)S(1)}, u32[]{:S(2)}, u32[]{:S(2)}) collective-permute-start(f32[128,128]{1,0:T(8,128)S(1)} %bitcast.27), channel_id=1, source_target_pairs={{0,1},{1,0},{2,3},{3,2},{4,5},{5,4},{6,7},{7,6},{8,9},{9,8},{10,11... | collective-permute-start | bytes 196616 | tf_op jit(solution)/shard_map/ppermute | solution.py:753
  80.6 0.9 collective-permute-done.1.more_ref
  81.6 0.6 copy-done.7
  82.2 6.5 %combine.1 = (f32[640,128]{1,0:T(8,128)}, f32[640,128]{1,0:T(8,128)}, f32[8,128]{1,0:T(8,128)}) custom-call(s32[16,128]{1,0:T(8,128)} %copy-done.2, s32[1]{0:T(128)} %bitcast.3.core_ref, f32[128,128]{1,0:T(8,128)} %bitcast.28, f32[128,128]{1,0:T(8,128)} %copy-done.7, f32[1,8,128]{2,1,0:T(8,128)} %get-tuple-element.51.deriv0_ref, ...), custom_call_target="tpu_custom_call" | custom-call | tf_op jit(solution)/shard_map/combine/pallas_call | solution.py:721
  88.7 0.3 collective-permute-start.2
  89.0 1.5 %collective-permute-done.2 = f32[640,128]{1,0:T(8,128)S(1)} collective-permute-done((f32[640,128]{1,0:T(8,128)}, f32[640,128]{1,0:T(8,128)S(1)}, u32[]{:S(2)}, u32[]{:S(2)}) %collective-permute-start.2) | collective-permute-done | bytes 327712 | tf_op jit(solution)/shard_map/ppermute | solution.py:753
  90.5 1.0 add.28
  91.6 11.0 %all_to_all.32 = f32[16,40,128]{2,1,0:T(8,128)S(1)} all-to-all(f32[16,40,128]{2,1,0:T(8,128)S(1)} %bitcast.26), channel_id=1, replica_groups=mesh['x'=4,'y'=4,'z'=8,'core'=2] {'x','y'}, dimensions={0} | all-to-all | bytes 655360 | tf_op jit(solution)/shard_map/all_to_all | solution.py:769
  102.6 10.8 %all_to_all.33 = f32[8,40,128]{2,1,0:T(8,128)S(1)} all-to-all(f32[8,40,128]{2,1,0:T(8,128)S(1)} %broadcast_in_dim.20), channel_id=1, replica_groups=mesh['x'=4,'y'=4,'z'=8,'core'=2] {'z'}, dimensions={0} | all-to-all | bytes 327680 | tf_op jit(solution)/shard_map/all_to_all | solution.py:762
  113.4 11.5 %all_to_all.34 = f32[16,40,128]{2,1,0:T(8,128)S(1)} all-to-all(f32[16,40,128]{2,1,0:T(8,128)S(1)} %broadcast_in_dim.21), channel_id=1, replica_groups=mesh['x'=4,'y'=4,'z'=8,'core'=2] {'x','y'}, dimensions={0} | all-to-all | bytes 655360 | tf_op jit(solution)/shard_map/all_to_all | solution.py:762
  124.9 4.0 %collective-permute-start.3 = (f32[640,128]{1,0:T(8,128)S(1)}, f32[640,128]{1,0:T(8,128)S(1)}, u32[]{:S(2)}, u32[]{:S(2)}) collective-permute-start(f32[640,128]{1,0:T(8,128)S(1)} %bitcast.25), channel_id=1, source_target_pairs={{0,1},{1,0},{2,3},{3,2},{4,5},{5,4},{6,7},{7,6},{8,9},{9,8},{10,11... | collective-permute-start | bytes 983048 | tf_op jit(solution)/shard_map/ppermute | solution.py:753
  128.9 1.2 slice_bitcast_fusion
  130.3 0.8 multiply_reduce_fusion
  131.8 1.5 %divide_subtract_fusion = (f32[160272]{0:T(1024)}, f32[160272]{0:T(1024)}, f32[160272]{0:T(1024)}) fusion(f32[160272]{0:T(1024)S(1)} %copy-done.3, f32[]{:T(128)S(6)} %div.14, f32[163840]{0:T(1024)S(1)} %maximum_bitcast_fusion, f32[160272]{0:T(1024)S(1)} %copy-done.4, f32[160272]{0:T(1024)S(1)} %copy-done.5), kind=kLoop, calls=%fused_computation.4 | loop fusion | flops 2083536 | bytes 4487620 | tf_op jit(solution)/shard_map/sub | solution.py:748
  (22 shorter events, 0.3 us)
Async XLA Ops:
  3.2 21.5 %all-to-all-start = ((f32[16,96,128]{2,1,0:T(8,128)}), f32[16,96,128]{2,1,0:T(8,128)S(1)}, u32[]{:S(2)}, u32[]{:S(2)}) async-start(f32[16,96,128]{2,1,0:T(8,128)} %get-tuple-element.31), calls=%async_computation | async-start | bytes 1572864 | tf_op jit(solution)/shard_map/all_to_all | solution.py:783
  24.6 4.4 %copy-start = (f32[16,96,128]{2,1,0:T(8,128)}, f32[16,96,128]{2,1,0:T(8,128)S(1)}, u32[]{:S(2)}) copy-start(f32[16,96,128]{2,1,0:T(8,128)S(1)} %all-to-all-done.here_ref) | copy-start | bytes 2359300
  24.6 3.4 %collective-permute-start = (f32[16,96,128]{2,1,0:T(8,128)S(1)}, f32[16,96,128]{2,1,0:T(8,128)S(1)}, u32[]{:S(2)}, u32[]{:S(2)}) collective-permute-start(f32[16,96,128]{2,1,0:T(8,128)S(1)} %all-to-all-done.here_ref), channel_id=1, source_target_pairs={{0,1},{1,0},{2,3},{3,2},{4,5},{5,4},{6,7},{7,6},{8,9},{9,8},{10,11... | collective-permute-start | bytes 2359304 | tf_op jit(solution)/shard_map/ppermute | solution.py:753
  28.0 1.1 copy-start.1
  28.4 0.6 copy-start.2
  29.0 102.8 %copy-start.3 = (f32[160272]{0:T(1024)S(1)}, f32[160272]{0:T(1024)}, u32[]{:S(2)}) copy-start(f32[160272]{0:T(1024)} %param.8) | copy-start | bytes 1923268
  29.0 102.8 %copy-start.4 = (f32[160272]{0:T(1024)S(1)}, f32[160272]{0:T(1024)}, u32[]{:S(2)}) copy-start(f32[160272]{0:T(1024)} %param.9) | copy-start | bytes 1923268
  29.0 102.8 %copy-start.5 = (f32[160272]{0:T(1024)S(1)}, f32[160272]{0:T(1024)}, u32[]{:S(2)}) copy-start(f32[160272]{0:T(1024)} %param.10) | copy-start | bytes 1923268
  78.9 2.7 %copy-start.6 = (f32[128,1,128]{2,1,0:T(1,128)}, f32[128,1,128]{2,1,0:T(1,128)S(1)}, u32[]{:S(2)}) copy-start(f32[128,1,128]{2,1,0:T(1,128)S(1)} %all_to_all.31) | copy-start | bytes 196612
  78.9 2.7 %collective-permute-start.1 = (f32[128,128]{1,0:T(8,128)S(1)}, f32[128,128]{1,0:T(8,128)S(1)}, u32[]{:S(2)}, u32[]{:S(2)}) collective-permute-start(f32[128,128]{1,0:T(8,128)S(1)} %bitcast.27), channel_id=1, source_target_pairs={{0,1},{1,0},{2,3},{3,2},{4,5},{5,4},{6,7},{7,6},{8,9},{9,8},{10,11... | collective-permute-start | bytes 196616 | tf_op jit(solution)/shard_map/ppermute | solution.py:753
  81.6 0.6 copy-start.7
  88.7 1.8 %collective-permute-start.2 = (f32[640,128]{1,0:T(8,128)}, f32[640,128]{1,0:T(8,128)S(1)}, u32[]{:S(2)}, u32[]{:S(2)}) collective-permute-start(f32[640,128]{1,0:T(8,128)} %get-tuple-element.56), channel_id=1, source_target_pairs={{0,1},{1,0},{2,3},{3,2},{4,5},{5,4},{6,7},{7,6},{8,9},{9,8},{10,11... | collective-permute-start | bytes 983048 | tf_op jit(solution)/shard_map/ppermute | solution.py:753
  124.9 5.2 %collective-permute-start.3 = (f32[640,128]{1,0:T(8,128)S(1)}, f32[640,128]{1,0:T(8,128)S(1)}, u32[]{:S(2)}, u32[]{:S(2)}) collective-permute-start(f32[640,128]{1,0:T(8,128)S(1)} %bitcast.25), channel_id=1, source_target_pairs={{0,1},{1,0},{2,3},{3,2},{4,5},{5,4},{6,7},{7,6},{8,9},{9,8},{10,11... | collective-permute-start | bytes 983048 | tf_op jit(solution)/shard_map/ppermute | solution.py:753
